TPU v7x, 512 devices: a whole 4x8x8 slice. The times are simulated.
512 devices in a mesh: rollout: 64 (over z, y_hi, core), tensor: 8 (over y_lo, x).
Axes of the slice: x: 4, y: 8 (y_hi: 4, y_lo: 2; y = y_hi * 2 + y_lo), z: 8, core: 2. Of those that a mesh axis runs over, the one named last changes fastest.
Arguments:
- tokens: bfloat16 [16384, 8192], P('rollout', 'tensor'), may hold values from -6 to 6
- base_key_value_weight: bfloat16 [8192, 2, 1024], P(None, None, 'tensor'), may hold values from -0.0625 to 0.0625
- key_value_bias: bfloat16 [2, 1024], P(None, 'tensor'), may hold values from -3 to 3
- adapter_down_blocks: bfloat16 [8192, 2, 128], P('rollout'), may hold values from -0.0625 to 0.0625
- adapter_up_blocks: bfloat16 [2, 128, 1024], P(None, 'rollout', 'tensor'), may hold values from -0.29882812 to 0.29882812
- owner_shard_lookup: int32 [64], replicated, may hold values from 0 to 63, each once
- lengths: int32 [64, 8], P('rollout'), may hold values from 1 to 128, 256 in all within a row
- routes: int32 [16384], P('rollout'), may hold values from 0 to 63, as said below
Outputs:
- kv_cache: bfloat16 [32768, 2, 1024], P('rollout', None, 'tensor')
Inputs may be any that keep to these rules, and one draw needn't show every extreme that they name: `owner_shard_lookup`: a permutation of the rollout indices. `routes`: the rows of one group name each destination at most 8 times; one destination, drawn from the seed, is named exactly 8 times by every group.
All inputs are finite; a program needn't handle non-finite values.
Results may differ from a plain program's by a relative error of at most 0.0048.
Values may be sent and summed in bfloat16 or wider, within the bound.
No kernel may reach another device: no remote copies, remote signals or barrier semaphores. Data moves between devices by JAX's collectives and lax.ppermute only.
A program may use at most 128 MiB of HBM per device.

v0:
```python
import jax
import jax.numpy as jnp
from jax import lax
from jax.sharding import PartitionSpec as P

HEAD = 128


adapter_scale = 2.0
rope_base = 1000000.0


def positions_of(lengths_row, row_count):
    ends = jnp.cumsum(lengths_row)
    starts = ends - lengths_row
    index = jnp.arange(row_count, dtype=jnp.int32)
    begins = jnp.max(jnp.where(starts[None, :] <= index[:, None], starts[None, :], 0), axis=1)
    return index - begins


def rotate(keys, places):
    half_width = HEAD // 2
    frequency = rope_base ** (-(jnp.arange(half_width, dtype=jnp.float32) * 2.0) / HEAD)
    angles = places.astype(jnp.float32)[:, None] * frequency[None, :]
    cosine = jnp.cos(angles)[:, None, :]
    sine = jnp.sin(angles)[:, None, :]
    shaped = keys.reshape(keys.shape[0], -1, HEAD)
    first = shaped[..., :half_width]
    second = shaped[..., half_width:]
    turned = jnp.concatenate(
        [first * cosine - second * sine, second * cosine + first * sine], axis=-1
    )
    return turned.reshape(keys.shape)


def finish_rows(summed, places, key_value_bias):
    width = key_value_bias.shape[1]
    shaped = summed.reshape(summed.shape[0], 2, width) + key_value_bias.astype(jnp.float32)[None]
    keys = rotate(shaped[:, 0], places)
    return jnp.stack([keys, shaped[:, 1]], axis=1)


def slot_index(target, group_count, capacity):
    matches = (target[:, None] == jnp.arange(group_count, dtype=jnp.int32)[None, :]).astype(
        jnp.int32
    )
    order_in = jnp.sum((jnp.cumsum(matches, axis=0) - matches) * matches, axis=1)
    return target * capacity + order_in


def place_rows(send_slots, slot_count, values):
    selector = (jnp.arange(slot_count, dtype=jnp.int32)[:, None] == send_slots[None, :]).astype(
        jnp.bfloat16
    )
    return jnp.dot(selector, values, preferred_element_type=jnp.float32).astype(jnp.bfloat16)


def body(
    tokens,
    base_key_value_weight,
    key_value_bias,
    adapter_down_blocks,
    adapter_up_blocks,
    owner_shard_lookup,
    lengths,
    routes,
):
    group_count = lax.axis_size("rollout")
    own_index = lax.axis_index("rollout")
    row_count = tokens.shape[0]
    capacity = 2 * row_count // group_count
    width = base_key_value_weight.shape[2]
    model_width = base_key_value_weight.shape[0]
    row_block_size = adapter_down_blocks.shape[0]
    inverse_permutation = (
        jnp.zeros((group_count,), jnp.int32)
        .at[owner_shard_lookup]
        .set(jnp.arange(group_count, dtype=jnp.int32))
    )
    up_persisted = lax.all_gather(adapter_up_blocks, "rollout", axis=1, tiled=True)
    rank_block_rows = adapter_up_blocks.shape[1]
    up_gathered = up_persisted.reshape(2, group_count, rank_block_rows, width)[
        :, inverse_permutation
    ].reshape(2, group_count * rank_block_rows, width)
    down_persisted = lax.all_gather(adapter_down_blocks, "rollout", axis=0, tiled=True)
    down_gathered = down_persisted.reshape(group_count, row_block_size, 2, -1)[
        inverse_permutation
    ].reshape(model_width, 2, -1)
    weight_update = jnp.einsum(
        "ohd,hde->ohe", down_gathered, up_gathered, preferred_element_type=jnp.float32
    )
    merged_weight = (
        base_key_value_weight.astype(jnp.float32) + adapter_scale * weight_update
    ).astype(jnp.bfloat16)
    merged_flat = merged_weight.reshape(model_width, 2 * width)
    slot_count = group_count * capacity
    send_slots = slot_index(routes, group_count, capacity)
    all_routes, all_lengths = (
        lax.all_gather(routes, "rollout", axis=0, tiled=True),
        lax.all_gather(lengths, "rollout", axis=0, tiled=True),
    )
    places = jax.vmap(lambda row: positions_of(row, row_count))(all_lengths)
    target = all_routes.reshape(group_count, row_count)
    matches = (target == own_index).astype(jnp.int32)
    order_in = jnp.cumsum(matches, axis=1) - matches
    picked = (matches[:, :, None] == 1) & (
        order_in[:, :, None] == jnp.arange(capacity, dtype=jnp.int32)[None, None, :]
    )
    picked_int = picked.astype(jnp.int32)
    slot_places = jnp.sum(picked_int * places[:, :, None], axis=1).reshape(slot_count)
    live = jnp.sum(picked_int, axis=1).astype(jnp.float32).reshape(slot_count)
    outgoing = place_rows(send_slots, slot_count, tokens)
    outgoing = outgoing.reshape(group_count, capacity, tokens.shape[1])
    arrived = lax.all_to_all(outgoing, "rollout", split_axis=0, concat_axis=0, tiled=True).reshape(
        slot_count, tokens.shape[1]
    )
    summed = jnp.dot(
        lax.all_gather(arrived, "tensor", axis=1, tiled=True),
        merged_flat,
        preferred_element_type=jnp.float32,
    )
    finished = finish_rows(summed, slot_places, key_value_bias) * live[:, None, None]
    return finished.astype(jnp.bfloat16)


def solution(mesh):
    in_specs = (
        P("rollout", "tensor"),
        P(None, None, "tensor"),
        P(None, "tensor"),
        P("rollout", None, None),
        P(None, "rollout", "tensor"),
        P(),
        P("rollout", None),
        P("rollout"),
    )
    out_specs = P("rollout", None, "tensor")
    return jax.shard_map(body, mesh=mesh, in_specs=in_specs, out_specs=out_specs, check_vma=False)
```

profile of v0, /device:TPU:1, one launch (start us, length us, event | category | flops | bytes accessed | tf_op | source)
XLA Modules:
  0.0 350.9 jit_solution(6564866927084419163)
XLA Ops:
  6.5 0.0 copy-start
  6.5 0.0 copy-start.4
  6.5 0.0 copy-start.2
  6.5 0.0 copy-start.5
  6.5 0.0 all-gather.7.cloned.1.call-start
  6.6 0.7 all-gather.7.cloned.1.call-update
  7.3 0.0 all-gather.5.cloned.1.call-start
  7.3 0.7 fusion.22
  8.0 0.6 reduce-window.14
  8.6 0.2 slice_reduce_fusion.1
  8.8 0.8 fusion.21
  9.6 0.7 multiply_add_fusion
  10.3 0.0 copy-done
  10.3 0.4 fusion.6
  10.8 52.3 %all_to_all.5 = bf16[64,8,1024]{2,1,0:T(8,128)(2,1)} all-to-all(bf16[64,8,1024]{2,1,0:T(8,128)(2,1)S(1)} %fusion.6), channel_id=1, replica_groups=mesh['rollout'=64,'tensor'=8] {'rollout'}, dimensions={0} | all-to-all | bytes 2097152 | tf_op jit(solution)/shard_map/all_to_all | solution.py:114
  63.0 0.0 all-gather.5.cloned.1.call-update
  63.1 0.0 copy-done.4
  63.1 0.0 copy-done.2
  63.1 79.9 %all_gather.16 = bf16[2,128,128]{2,0,1:T(2,128)(2,1)S(1)} all-gather(bf16[2,2,128]{2,0,1:T(2,128)(2,1)S(1)} %copy.41), channel_id=1, replica_groups=mesh['rollout'=64,'tensor'=8] {'rollout'}, dimensions={1}, use_global_device_ids=true | all-gather | bytes 66560 | tf_op jit(solution)/shard_map/all_gather | solution.py:80
  143.0 0.0 copy-done.5
  143.0 0.8 scatter_custom_fusion
  143.8 0.7 gather_fusion
  144.6 0.0 copy-start.1
  144.6 0.0 copy-start.3
  144.7 11.2 %copy.40 = bf16[8192,2,128]{0,2,1:T(8,128)(2,1)} copy(bf16[8192,2,128]{2,1,0:T(2,128)(2,1)} %param.9) | data formatting | bytes 8388608 | tf_op args[1]
  155.9 0.0 copy-done.1
  155.9 76.5 %all-gather = s32[64,1,256]{2,1,0:T(1,128)S(1)} all-gather(s32[1,1,256]{2,1,0:T(1,128)S(1)} %bitcast.89), channel_id=1, replica_groups=mesh['rollout'=64,'tensor'=8] {'rollout'}, dimensions={0}, use_global_device_ids=true | all-gather | bytes 66560 | tf_op jit(solution)/shard_map/all_gather | solution.py:99
  232.5 0.6 reduce-window.16
  233.1 0.2 slice_reduce_fusion
  233.3 0.0 copy-done.3
  233.3 78.5 %all-gather.1 = s32[64,1,8]{2,1,0:T(1,128)S(1)} all-gather(s32[1,1,8]{2,1,0:T(1,128)S(1)} %bitcast.90), channel_id=1, replica_groups=mesh['rollout'=64,'tensor'=8] {'rollout'}, dimensions={0}, use_global_device_ids=true | all-gather | bytes 2080 | tf_op jit(solution)/shard_map/all_gather | solution.py:100
  311.8 0.2 reduce_window_sum.49
  312.0 0.3 select_reduce_fusion.1
  312.3 0.1 bitcast_subtract_fusion
  312.4 2.2 convert_reduce_fusion
  314.7 0.1 convert_element_type.76
  314.8 0.1 convert_element_type.79
  314.9 0.0 all-gather.7.cloned.1.call-done
  314.9 12.9 %gather_fusion.1 = bf16[64,128,2,128]{3,2,1,0:T(2,128)(2,1)} fusion(bf16[64,128,2,128]{3,2,1,0:T(2,128)(2,1)} %bitcast.80, s32[1024]{0:T(1024)S(1)} %pad_clamp_fusion), kind=kCustom, calls=%fused_computation.1 | custom fusion | bytes 8388864 | tf_op jit(solution)/shard_map/gather | solution.py:86
  327.8 5.3 %copy.44 = bf16[64,128,2,128]{3,1,0,2:T(8,128)(2,1)} copy(bf16[64,128,2,128]{3,2,1,0:T(2,128)(2,1)} %gather_fusion.1) | data formatting | bytes 8388608 | tf_op jit(solution)/shard_map/gather | solution.py:86
  333.1 0.0 all-gather.5.cloned.1.call-done
  333.1 9.5 %fusion.7 = f32[512,2,128]{0,2,1:T(8,128)S(1)} fusion(bf16[512,8192]{1,0:T(8,128)(2,1)} %all-gather.5.cloned.1.call-done, f32[2,128]{1,0:T(2,128)S(1)} %convert_element_type.70, bf16[2,128,128]{2,1,0:T(8,128)(2,1)S(1)} %bitcast.87, bf16[8192,2,128]{2,0,1:T(8,128)(2,1)} %bitcast.81, bf16[8192,2,128]{0,2,1:T(8,128)(2,1)} %copy.40), kind=kOutput, calls=%fused_computation.12 | convolution fusion | flops 2692874240 | bytes 17368064 | tf_op jit(solution)/shard_map/dot_general | solution.py:117
  342.6 0.6 fusion.17
  343.2 0.9 copy.49
  (22 shorter events, 0.3 us)
Async XLA Ops:
  6.5 3.8 %copy-start = (bf16[256,1024]{1,0:T(8,128)(2,1)S(1)}, bf16[256,1024]{1,0:T(8,128)(2,1)}, u32[]{:S(2)}) copy-start(bf16[256,1024]{1,0:T(8,128)(2,1)} %param.8) | copy-start | bytes 1572868
  6.5 56.5 %copy-start.4 = (bf16[2,128]{1,0:T(2,128)(2,1)S(1)}, bf16[2,128]{1,0:T(2,128)(2,1)}, u32[]{:S(2)}) copy-start(bf16[2,128]{1,0:T(2,128)(2,1)} %param.10) | copy-start | bytes 1540
  6.5 56.6 %copy-start.2 = (bf16[2,2,128]{2,1,0:T(2,128)(2,1)S(1)}, bf16[2,2,128]{2,1,0:T(2,128)(2,1)}, u32[]{:S(2)}) copy-start(bf16[2,2,128]{2,1,0:T(2,128)(2,1)} %param.12) | copy-start | bytes 3076
  6.5 136.5 %copy-start.5 = (s32[64]{0:T(128)S(1)}, s32[64]{0:T(128)}, u32[]{:S(2)}) copy-start(s32[64]{0:T(128)} %param.13) | copy-start | bytes 772
  6.5 308.4 %all-gather.7.cloned.1.call-start = ((), (), s32[]{:S(2)}) async-start(), calls=%async_computation.2 | async-start | bytes 4259840 | tf_op jit(solution)/shard_map/all_gather | solution.py:85
  7.3 325.8 %all-gather.5.cloned.1.call-start = ((), (), s32[]{:S(2)}) async-start(), calls=%async_computation.1 | async-start | bytes 9437184 | tf_op jit(solution)/shard_map/all_gather | solution.py:118
  144.6 11.3 %copy-start.1 = (s32[256]{0:T(256)S(1)}, s32[256]{0:T(256)}, u32[]{:S(2)}) copy-start(s32[256]{0:T(256)} %param.15) | copy-start | bytes 3076
  144.6 88.7 %copy-start.3 = (s32[1,8]{1,0:T(1,128)S(1)}, s32[1,8]{1,0:T(1,128)}, u32[]{:S(2)}) copy-start(s32[1,8]{1,0:T(1,128)} %param.14) | copy-start | bytes 100
Sparse Core Ops, SparseCore 0:
  10.7 104.5 all-gather.6
  117.4 93.7 all-gather.4
where the time goes:
time: 351 us
  blocking collectives  287 us (82%)
  local copies, waits for them, and re-layouts  32.5 us (9%)
  between operations  13.7 us (4%)
  matrix products  9.92 us (3%)
  other arithmetic  6.91 us (2%)
    all_gather x1, blocking collectives, body(): lax.all_gather(adapter_up_blocks, 'rollout', axis=1, tiled=True)  79.9 us
    all_gather x1, blocking collectives, body(): lax.all_gather(lengths, 'rollout', axis=0, tiled=True)  78.5 us
    all_gather x1, blocking collectives, body(): lax.all_gather(routes, 'rollout', axis=0, tiled=True)  76.5 us
    all_to_all x1, blocking collectives, body(): lax.all_to_all(outgoing, 'rollout', split_axis=0, concat_axis=0, tiled=True)  52.3 us
    gather x2, local copies, waits for them, and re-layouts, body(): down_persisted.reshape(group_count, row_block_size, 2, -1)  18.2 us
    unnamed x14, local copies, waits for them, and re-layouts  11.3 us
    dot_general x1, matrix products, body(): jnp.dot(lax.all_gather(arrived, 'tensor', axis=1, tiled=True), merged_fla...  9.47 us
  transfers between devices with their start and end apart: 2, of which 0 were waited for; matrix products, arithmetic and copies ran while one was open for 11% of the time, Pallas kernels for 0%

commit v1 on v0

v1 whole, which is shorter than its diff:
```python
import jax
import jax.numpy as jnp
from jax import lax
from jax.experimental import pallas as pl
from jax.experimental.pallas import tpu as pltpu
from jax.sharding import PartitionSpec as P

HEAD = 128
GROUPS = 64
RANK = 128
MODEL = 8192
ROWS = 256
CAP = 8
X = 4
Y_HI = 4
Z = 8

adapter_scale = 2.0
rope_base = 1000000.0

HALF = MODEL // 2
QUARTER = MODEL // 4
WIDE = 2 * HEAD
SLICE = 2 * RANK // X
PART = SLICE // 2
SENT = PART + 8

X_GROUPS = [[0, 1, 2, 3], [4, 5, 6, 7]]
SIBLING = [(a, a ^ 1) for a in range(GROUPS)]
Y_PARTNER = [(a, (a + X) % (2 * X)) for a in range(2 * X)]


def flat_index(z, y, core, x):
    return ((z * Y_HI + y // 2) * 2 + core) * (2 * X) + (y % 2) * X + x


WEIGHT_HOP = [
    (
        flat_index(z, y, core, x),
        flat_index(z, (y + (1 if core == 0 else -1)) % (2 * Y_HI), core, x),
    )
    for z in range(Z)
    for y in range(2 * Y_HI)
    for core in range(2)
    for x in range(X)
]

VMEM_LIMIT = 40 * 1024 * 1024


def vmem(count):
    return [pl.BlockSpec(memory_space=pltpu.VMEM)] * count


def smem(count):
    return [pl.BlockSpec(memory_space=pltpu.SMEM)] * count


def factors_kernel(lookup_ref, own_ref, near_ref, far_ref, down_ref, up_ref, inverse, up_rows):
    y, core = own_ref[0], own_ref[1]

    @pl.loop(0, GROUPS)
    def _(owner):
        inverse[lookup_ref[owner]] = owner

    for local in range(GROUPS // 2):
        owner = inverse[(GROUPS // 2) * y + local]
        mine = near_ref[owner, 0:PART, :]
        other = far_ref[owner, 0:PART, :]
        columns = slice(local * 128, (local + 1) * 128)
        down_ref[0:PART, columns] = jnp.where(core == 0, mine, other)
        down_ref[PART:SLICE, columns] = jnp.where(core == 0, other, mine)
    for shard in range(GROUPS):
        rows = near_ref[inverse[shard], PART:SENT, :].astype(jnp.float32)
        up_rows[2 * shard : 2 * shard + 2, :] = rows[0:2]
        up_rows[RANK + 2 * shard : RANK + 2 * shard + 2, :] = rows[2:4]
    up_ref[...] = up_rows[...].astype(jnp.bfloat16)


def factors(lookup, own, near, far):
    return pl.pallas_call(
        factors_kernel,
        out_shape=(
            jax.ShapeDtypeStruct((SLICE, HALF), jnp.bfloat16),
            jax.ShapeDtypeStruct((2 * RANK, HEAD), jnp.bfloat16),
        ),
        in_specs=smem(2) + vmem(2),
        out_specs=tuple(vmem(2)),
        scratch_shapes=[
            pltpu.SMEM((GROUPS,), jnp.int32),
            pltpu.VMEM((2 * RANK, HEAD), jnp.float32),
        ],
        compiler_params=pltpu.CompilerParams(vmem_limit_bytes=VMEM_LIMIT),
        name="factors",
    )(lookup, own, near, far)


def low_rank_kernel(tokens_ref, down_ref, out_ref):
    total = None
    for step in range(X):
        part = lax.dot_general(
            down_ref[:, step * 1024 : (step + 1) * 1024],
            tokens_ref[step],
            (((1,), (1,)), ((), ())),
            preferred_element_type=jnp.float32,
        )
        total = part if total is None else total + part
    out_ref[...] = total.astype(jnp.bfloat16)


def low_rank(tokens, down):
    return pl.pallas_call(
        low_rank_kernel,
        out_shape=jax.ShapeDtypeStruct((SLICE, ROWS), jnp.bfloat16),
        in_specs=vmem(2),
        out_specs=vmem(1)[0],
        compiler_params=pltpu.CompilerParams(vmem_limit_bytes=VMEM_LIMIT),
        name="low_rank",
    )(tokens, down)


def project_kernel(tokens_ref, weight_ref, out_ref):
    total = None
    for step in range(X):
        part = jnp.dot(
            tokens_ref[step],
            weight_ref[step * 1024 : (step + 1) * 1024, :],
            preferred_element_type=jnp.float32,
        )
        total = part if total is None else total + part
    out_ref[...] = total.astype(out_ref.dtype)


def project(tokens, weight, dtype):
    return pl.pallas_call(
        project_kernel,
        out_shape=jax.ShapeDtypeStruct((ROWS, WIDE), dtype),
        in_specs=vmem(2),
        out_specs=vmem(1)[0],
        compiler_params=pltpu.CompilerParams(vmem_limit_bytes=VMEM_LIMIT),
        name="project",
    )(tokens, weight)


def finish_kernel(own_ref, met_ref, low_ref, up_ref, bias_ref, cos_ref, sin_ref, slot_ref, out_ref):
    base = own_ref[...] + met_ref[...].astype(jnp.float32)
    made = []
    for side in range(2):
        update = None
        for y in range(2):
            for part in range(2):
                first = side * RANK + part * SLICE
                term = lax.dot_general(
                    low_ref[y * X + 2 * side + part],
                    up_ref[first : first + SLICE, :],
                    (((0,), (0,)), ((), ())),
                    preferred_element_type=jnp.float32,
                )
                update = term if update is None else update + term
        made.append(
            base[:, side * HEAD : (side + 1) * HEAD]
            + adapter_scale * update
            + bias_ref[side : side + 1, :].astype(jnp.float32)
        )
    keys = made[0]
    keys = keys * cos_ref[...] + pltpu.roll(keys, HEAD // 2, 1) * sin_ref[...]
    rows = jnp.concatenate([keys, made[1]], axis=1).astype(jnp.bfloat16)
    slots = lax.broadcasted_iota(jnp.int32, (GROUPS * CAP, ROWS), 0)
    chosen = jnp.where(slots == slot_ref[...], 1.0, 0.0).astype(jnp.bfloat16)
    placed = jnp.dot(chosen, rows, preferred_element_type=jnp.float32).astype(jnp.bfloat16)
    out_ref[...] = placed.reshape(GROUPS, CAP, WIDE)


def finish(own, met, low, up, bias, cosine, sine, slots):
    return pl.pallas_call(
        finish_kernel,
        out_shape=jax.ShapeDtypeStruct((GROUPS, CAP, WIDE), jnp.bfloat16),
        in_specs=vmem(8),
        out_specs=vmem(1)[0],
        compiler_params=pltpu.CompilerParams(vmem_limit_bytes=VMEM_LIMIT),
        name="finish",
    )(own, met, low, up, bias, cosine, sine, slots)


def positions_of(lengths_row):
    ends = jnp.cumsum(lengths_row)
    starts = ends - lengths_row
    index = jnp.arange(ROWS, dtype=jnp.int32)
    begins = jnp.max(jnp.where(starts[None, :] <= index[:, None], starts[None, :], 0), axis=1)
    return index - begins


def turn_tables(places):
    half_width = HEAD // 2
    frequency = rope_base ** (-(jnp.arange(half_width, dtype=jnp.float32) * 2.0) / HEAD)
    angles = places.astype(jnp.float32)[:, None] * frequency[None, :]
    cosine, sine = jnp.cos(angles), jnp.sin(angles)
    return jnp.concatenate([cosine, cosine], 1), jnp.concatenate([-sine, sine], 1)


def slot_index(target):
    index = jnp.arange(ROWS, dtype=jnp.int32)
    earlier = (target[:, None] == target[None, :]) & (index[:, None] < index[None, :])
    return target * CAP + jnp.sum(earlier.astype(jnp.int32), axis=0)


def body(tokens, weight, bias, down_blocks, up_blocks, lookup, lengths, routes):
    lane = lax.axis_index("tensor")
    y, x = lane // X, lane % X
    core = lax.axis_index("rollout") % 2

    down_turned = down_blocks.transpose(1, 2, 0).reshape(X, 2, PART, 128)
    down_sent = lax.dynamic_index_in_dim(down_turned, x, 0, keepdims=False)
    up_sent = jnp.broadcast_to(up_blocks.reshape(1, 4, HEAD), (2, 4, HEAD))
    sent = jnp.concatenate([down_sent, up_sent, jnp.zeros((2, 4, HEAD), jnp.bfloat16)], 1)
    sent = jnp.broadcast_to(sent[None], (GROUPS // 2, 2, SENT, HEAD)).reshape(GROUPS, SENT, HEAD)
    near = lax.all_to_all(sent, "rollout", 0, 0, tiled=True)

    gathered = lax.all_gather(tokens, "tensor", axis=0, axis_index_groups=X_GROUPS)

    weight_sent = lax.dynamic_slice_in_dim(weight, (1 - y) * HALF + core * QUARTER, QUARTER, 0)
    weight_near = lax.ppermute(
        weight_sent.reshape(QUARTER, WIDE), ("rollout", "tensor"), WEIGHT_HOP
    )
    weight_far = lax.ppermute(weight_near, "rollout", SIBLING)
    weight_met = jnp.where(
        core == 0,
        jnp.concatenate([weight_near, weight_far], 0),
        jnp.concatenate([weight_far, weight_near], 0),
    )
    weight_own = lax.dynamic_slice_in_dim(weight, y * HALF, HALF, 0).reshape(HALF, WIDE)

    far = lax.ppermute(near, "rollout", SIBLING)
    own = jnp.stack([y, core]).astype(jnp.int32)
    down, up = factors(lookup, own, near, far)

    cosine, sine = turn_tables(positions_of(lengths[0]))
    slots = slot_index(routes).reshape(1, ROWS)

    partial_met = project(gathered, weight_met, jnp.bfloat16)
    partial_in = lax.ppermute(partial_met, "tensor", Y_PARTNER)
    low = low_rank(gathered, down)
    low_all = lax.all_to_all(
        jnp.broadcast_to(low[None], (2 * X, SLICE, ROWS)), "tensor", 0, 0, tiled=True
    )
    partial_own = project(gathered, weight_own, jnp.float32)
    outgoing = finish(partial_own, partial_in, low_all, up, bias, cosine, sine, slots)
    arrived = lax.all_to_all(outgoing, "rollout", 0, 0, tiled=True)
    return arrived.reshape(GROUPS * CAP, 2, HEAD)


def solution(mesh):
    in_specs = (
        P("rollout", "tensor"),
        P(None, None, "tensor"),
        P(None, "tensor"),
        P("rollout", None, None),
        P(None, "rollout", "tensor"),
        P(),
        P("rollout", None),
        P("rollout"),
    )
    out_specs = P("rollout", None, "tensor")
    return jax.shard_map(body, mesh=mesh, in_specs=in_specs, out_specs=out_specs, check_vma=False)
```

time: 351 us -> 113 us (0.32)
  blocking collectives: 287 us -> 25.2 us
  starting transfers between devices: 0.07 us -> 34.8 us
  local copies, waits for them, and re-layouts: 32.5 us -> 10.5 us
  waiting for transfers between devices: 0.72 us -> 19.4 us
  matrix products: 9.92 us -> 0 us
  Pallas kernels: 0 us -> 4.11 us
    all_gather x3 -> x0, blocking collectives: 235 us -> none  [the longest x1 79.9 us: body(): lax.all_gather(adapter_up_blocks, 'rollout', axis=1, tiled=True)]
    all_to_all x1, blocking collectives: 52.3 us -> 25.2 us  [body(): arrived = lax.all_to_all(outgoing, 'rollout', 0, 0, tiled=True)]
    gather x4 -> x0, local copies, waits for them, and re-layouts: 18.9 us -> none  [the longest x2 18.2 us: body(): down_persisted.reshape(group_count, row_block_size, 2, -1)]
    all_to_all x0 -> x2, starting transfers between devices: none -> 18.3 us  [the longest x1 14.3 us: body(): near = lax.all_to_all(sent, 'rollout', 0, 0, tiled=True)]
    all_to_all x0 -> x2, waiting for transfers between devices: none -> 17.5 us  [the longest x1 17.5 us: body(): near = lax.all_to_all(sent, 'rollout', 0, 0, tiled=True)]
    ppermute x0 -> x4, starting transfers between devices: none -> 16.5 us  [the longest x1 5.93 us: body(): lax.ppermute(weight_sent.reshape(QUARTER, WIDE), ('rollout', 'tensor'), W...]
    dot_general x2 -> x0, matrix products: 9.92 us -> none  [the longest x1 9.47 us: body(): jnp.dot(lax.all_gather(arrived, 'tensor', axis=1, tiled=True), merged_fla...]
    unnamed x14 -> x23, local copies, waits for them, and re-layouts: 11.3 us -> 2.86 us
  transfers between devices with their start and end apart: 2 -> 7, of which waited for: 0 -> 2; matrix products, arithmetic and copies ran while one was open for 11% -> 11% of each run, Pallas kernels for 0% -> 3%
where the time goes in v1:
time: 113 us; the launch traced here: 112 us
  starting transfers between devices  34.8 us (31%)
  blocking collectives  25.2 us (22%)
  waiting for transfers between devices  19.4 us (17%)
  between operations  13.7 us (12%)
  local copies, waits for them, and re-layouts  10.5 us (9%)
  other arithmetic  4.74 us (4%)
  Pallas kernels  4.11 us (4%)
    all_to_all x1, blocking collectives, body(): arrived = lax.all_to_all(outgoing, 'rollout', 0, 0, tiled=True)  25.2 us
    all_to_all x1, waiting for transfers between devices, body(): near = lax.all_to_all(sent, 'rollout', 0, 0, tiled=True)  17.5 us
    all_to_all x1, starting transfers between devices, body(): near = lax.all_to_all(sent, 'rollout', 0, 0, tiled=True)  14.3 us
    ppermute x1, starting transfers between devices, body(): lax.ppermute(weight_sent.reshape(QUARTER, WIDE), ('rollout', 'tensor'), W...  5.93 us
    ppermute x1, starting transfers between devices, body(): weight_far = lax.ppermute(weight_near, 'rollout', SIBLING)  5.06 us
    all_to_all x1, starting transfers between devices, body(): lax.all_to_all(jnp.broadcast_to(low[None], (2 * X, SLICE, ROWS)), 'tensor...  4.02 us
    ppermute x1, starting transfers between devices, body(): partial_in = lax.ppermute(partial_met, 'tensor', Y_PARTNER)  3.37 us
    dynamic_slice x1, local copies, waits for them, and re-layouts, body(): lax.dynamic_slice_in_dim(weight, y * HALF, HALF, 0).reshape(HALF, WIDE)  3.25 us
  transfers between devices with their start and end apart: 7, of which 2 were waited for; matrix products, arithmetic and copies ran while one was open for 11% of the time, Pallas kernels for 3%

profile of v1, /device:TPU:1, one launch (start us, length us, event | category | flops | bytes accessed | tf_op | source)
XLA Modules:
  0.0 112.4 jit_solution(3763335063010525853)
XLA Ops:
  6.5 0.0 all-gather.3.cloned.1.call-start
  6.5 0.7 all-gather.3.cloned.1.call-update
  7.3 1.8 %constant_dynamic-slice_fusion = bf16[2048,2,128]{2,1,0:T(2,128)(2,1)S(1)} fusion(bf16[8192,2,128]{2,1,0:T(2,128)(2,1)} %param.9, s32[]{:T(128)S(6)} %select_n.41), kind=kLoop, calls=%fused_computation.17 | loop fusion | bytes 2097156 | tf_op jit(solution)/shard_map/dynamic_slice | solution.py:221
  9.1 0.0 copy-start.9
  9.2 0.0 copy-start.7
  9.2 0.1 copy.16
  9.3 5.9 %collective-permute-start = (bf16[2048,256]{1,0:T(8,128)(2,1)S(1)}, bf16[2048,256]{1,0:T(8,128)(2,1)}, u32[]{:S(2)}, u32[]{:S(2)}) collective-permute-start(bf16[2048,256]{1,0:T(8,128)(2,1)S(1)} %bitcast.28), channel_id=1, source_target_pairs={{0,4},{1,5},{2,6},{3,7},{8,60},{9,61},{10,62},{11,63},{4,16},{5,17... | collective-permute-start | bytes 3145736 | tf_op jit(solution)/shard_map/ppermute | solution.py:222
  15.3 0.1 copy.10
  15.4 0.1 pad.6.clone
  15.5 0.1 maximum_maximum_fusion
  15.6 0.9 broadcast_in_dim.23
  16.5 14.3 %all-to-all-start = ((bf16[64,40,128]{2,1,0:T(8,128)(2,1)}), bf16[64,40,128]{2,1,0:T(8,128)(2,1)S(1)}, u32[]{:S(2)}, u32[]{:S(2)}) async-start(bf16[64,40,128]{2,1,0:T(8,128)(2,1)} %bitcast.7), calls=%async_computation | async-start | bytes 1310720 | tf_op jit(solution)/shard_map/all_to_all | solution.py:217
  30.8 0.0 copy-done.9
  30.8 0.2 reduce-window_clone.1
  31.0 0.0 collective-permute-done
  31.0 5.1 %collective-permute-start.1 = (bf16[2048,256]{1,0:T(8,128)(2,1)}, bf16[2048,256]{1,0:T(8,128)(2,1)}, u32[]{:S(2)}, u32[]{:S(2)}) collective-permute-start(bf16[2048,256]{1,0:T(8,128)(2,1)} %collective-permute-done), channel_id=1, source_target_pairs={{0,8},{8,0},{16,24},{24,16},{32,40},{40,32},{48,56},{56,48},{64,72... | collective-permute-start | bytes 3145736 | tf_op jit(solution)/shard_map/ppermute | solution.py:225
  36.1 0.1 pad_add_fusion.own_ref
  36.2 0.1 select_reduce_fusion
  36.3 17.5 %all-to-all-done.near_ref = bf16[64,40,128]{2,1,0:T(8,128)(2,1)S(1)} async-done(((bf16[64,40,128]{2,1,0:T(8,128)(2,1)}), bf16[64,40,128]{2,1,0:T(8,128)(2,1)S(1)}, u32[]{:S(2)}, u32[]{:S(2)}) %all-to-all-start) | async-done | bytes 655392 | tf_op jit(solution)/shard_map/all_to_all | solution.py:217
  53.7 2.2 %collective-permute-start.3 = (bf16[64,40,128]{2,1,0:T(8,128)(2,1)S(1)}, bf16[64,40,128]{2,1,0:T(8,128)(2,1)S(1)}, u32[]{:S(2)}, u32[]{:S(2)}) collective-permute-start(bf16[64,40,128]{2,1,0:T(8,128)(2,1)S(1)} %all-to-all-done.near_ref), channel_id=1, source_target_pairs={{0,8},{8,0},{16,24},{24,16},{32,40},{40,32},{48,56},{56,48},{64,72... | collective-permute-start | bytes 1966088 | tf_op jit(solution)/shard_map/ppermute | solution.py:233
  55.9 0.0 copy-done.7
  55.9 0.1 convert_reduce_fusion
  56.0 1.2 %fusion.1 = (f32[256,64]{1,0:T(8,128)S(1)}, f32[256,64]{1,0:T(8,128)}, f32[256,64]{1,0:T(8,128)}) fusion(f32[64]{0:T(128)S(1)} %multiply_power_fusion, f32[256]{0:T(256)S(1)} %subtract_convert_fusion), kind=kLoop, calls=%fused_computation.10 | loop fusion | flops 32768 | bytes 197888 | tf_op jit(solution)/shard_map/neg | solution.py:198
  57.3 3.3 %constant_dynamic-slice_fusion.1 = bf16[4096,2,128]{2,1,0:T(2,128)(2,1)S(1)} fusion(bf16[8192,2,128]{2,1,0:T(2,128)(2,1)} %param.9, s32[]{:T(128)S(6)} %select_n.38), kind=kLoop, calls=%fused_computation.18 | loop fusion | bytes 4194308 | tf_op jit(solution)/shard_map/dynamic_slice | solution.py:231
  60.5 0.0 collective-permute-done.3.far_ref
  60.5 1.3 %factors.1 = (bf16[64,4096]{1,0:T(8,128)(2,1)S(1)}, bf16[256,128]{1,0:T(8,128)(2,1)S(1)}) custom-call(s32[64]{0:T(128)S(1)} %copy-done.2, s32[2]{0:T(128)S(1)} %pad_add_fusion.own_ref, bf16[64,40,128]{2,1,0:T(8,128)(2,1)S(1)} %all-to-all-done.near_ref, bf16[64,40,128]{2,1,0:T(8,128)(2,1)S(1)} %collective-permute-done.3.far_ref), custom_call_target="tpu_custom_call" | custom-call | tf_op jit(solution)/shard_map/factors/pallas_call | solution.py:81
  61.9 0.0 all-gather.3.cloned.1.call-done
  61.9 0.0 copy-start
  61.9 1.6 %copy-done = bf16[1024,1024]{1,0:T(8,128)(2,1)S(1)} copy-done((bf16[1024,1024]{1,0:T(8,128)(2,1)S(1)}, bf16[1024,1024]{1,0:T(8,128)(2,1)}, u32[]{:S(2)}) %copy-start) | copy-done | bytes 2097176
  63.5 0.8 low_rank.1
  64.3 0.7 broadcast_in_dim.24
  65.0 4.0 %all-to-all-start.1 = ((bf16[8,64,256]{2,1,0:T(8,128)(2,1)}), bf16[8,64,256]{2,1,0:T(8,128)(2,1)S(1)}, u32[]{:S(2)}, u32[]{:S(2)}) async-start(bf16[8,64,256]{2,1,0:T(8,128)(2,1)} %broadcast_in_dim.24), calls=%async_computation.1 | async-start | bytes 524288 | tf_op jit(solution)/shard_map/all_to_all | solution.py:243
  69.0 0.0 collective-permute-done.1
  69.0 2.8 %maximum_select_fusion.weight_ref = bf16[4096,256]{1,0:T(8,128)(2,1)S(1)} fusion(bf16[2048,256]{1,0:T(8,128)(2,1)} %collective-permute-done.1, bf16[2048,256]{1,0:T(8,128)(2,1)} %collective-permute-done, pred[]{:T(512)S(6)} %eq.19), kind=kLoop, calls=%fused_computation.1 | loop fusion | flops 9437184 | bytes 4194305 | tf_op jit(solution)/shard_map/jit(_where)/select_n | solution.py:226
  71.8 0.0 copy-done.1
  71.9 0.7 project.3
  72.6 3.4 %collective-permute-start.2 = (bf16[256,256]{1,0:T(8,128)(2,1)S(1)}, bf16[256,256]{1,0:T(8,128)(2,1)S(1)}, u32[]{:S(2)}, u32[]{:S(2)}) collective-permute-start(bf16[256,256]{1,0:T(8,128)(2,1)S(1)} %project.3), channel_id=1, source_target_pairs={{0,4},{1,5},{2,6},{3,7},{4,0},{5,1},{6,2},{7,3},{8,12},{9,13},{10,... | collective-permute-start | bytes 393224 | tf_op jit(solution)/shard_map/ppermute | solution.py:241
  76.0 0.3 copy.15
  76.3 0.6 copy-done.4
  76.9 0.1 copy-done.5
  77.0 0.1 pad_maximum_fusion
  77.1 0.0 copy-start.3
  77.1 0.7 project.2.own_ref
  77.8 1.2 %collective-permute-done.2.met_ref = bf16[256,256]{1,0:T(8,128)(2,1)S(1)} collective-permute-done((bf16[256,256]{1,0:T(8,128)(2,1)S(1)}, bf16[256,256]{1,0:T(8,128)(2,1)S(1)}, u32[]{:S(2)}, u32[]{:S(2)}) %collective-permute-start.2) | collective-permute-done | bytes 131104 | tf_op jit(solution)/shard_map/ppermute | solution.py:241
  79.0 0.0 all-to-all-done.1.low_ref
  79.0 0.6 finish.1
  79.6 25.2 %all_to_all.15 = bf16[64,8,256]{2,1,0:T(8,128)(2,1)S(1)} all-to-all(bf16[64,8,256]{2,1,0:T(8,128)(2,1)S(1)} %finish.1), channel_id=1, replica_groups=mesh['rollout'=64,'tensor'=8] {'rollout'}, dimensions={0} | all-to-all | bytes 524288 | tf_op jit(solution)/shard_map/all_to_all | solution.py:248
  104.8 0.8 reshape.49
  (17 shorter events, 0.1 us)
Async XLA Ops:
  6.5 55.4 %all-gather.3.cloned.1.call-start = ((), (), s32[]{:S(2)}) async-start(), calls=%async_computation.3 | async-start | bytes 2621440 | tf_op jit(solution)/shard_map/all_gather | solution.py:219
  7.3 8.0 %copy-start.6 = (bf16[128,2,128]{2,1,0:T(2,128)(2,1)S(1)}, bf16[128,2,128]{2,1,0:T(2,128)(2,1)}, u32[]{:S(2)}) copy-start(bf16[128,2,128]{2,1,0:T(2,128)(2,1)} %param.11) | copy-start | bytes 196612
  7.3 8.2 %copy-start.8 = (bf16[2,2,128]{2,1,0:T(2,128)(2,1)S(1)}, bf16[2,2,128]{2,1,0:T(2,128)(2,1)}, u32[]{:S(2)}) copy-start(bf16[2,2,128]{2,1,0:T(2,128)(2,1)} %param.12) | copy-start | bytes 3076
  9.1 21.7 %copy-start.9 = (s32[1,8]{1,0:T(1,128)S(1)}, s32[1,8]{1,0:T(1,128)}, u32[]{:S(2)}) copy-start(s32[1,8]{1,0:T(1,128)} %param.14) | copy-start | bytes 100
  9.2 46.7 %copy-start.7 = (s32[256]{0:T(256)S(1)}, s32[256]{0:T(256)}, u32[]{:S(2)}) copy-start(s32[256]{0:T(256)} %param.15) | copy-start | bytes 3076
  9.3 21.7 %collective-permute-start = (bf16[2048,256]{1,0:T(8,128)(2,1)S(1)}, bf16[2048,256]{1,0:T(8,128)(2,1)}, u32[]{:S(2)}, u32[]{:S(2)}) collective-permute-start(bf16[2048,256]{1,0:T(8,128)(2,1)S(1)} %bitcast.28), channel_id=1, source_target_pairs={{0,4},{1,5},{2,6},{3,7},{8,60},{9,61},{10,62},{11,63},{4,16},{5,17... | collective-permute-start | bytes 3145736 | tf_op jit(solution)/shard_map/ppermute | solution.py:222
  16.5 37.2 %all-to-all-start = ((bf16[64,40,128]{2,1,0:T(8,128)(2,1)}), bf16[64,40,128]{2,1,0:T(8,128)(2,1)S(1)}, u32[]{:S(2)}, u32[]{:S(2)}) async-start(bf16[64,40,128]{2,1,0:T(8,128)(2,1)} %bitcast.7), calls=%async_computation | async-start | bytes 1310720 | tf_op jit(solution)/shard_map/all_to_all | solution.py:217
  31.0 38.0 %collective-permute-start.1 = (bf16[2048,256]{1,0:T(8,128)(2,1)}, bf16[2048,256]{1,0:T(8,128)(2,1)}, u32[]{:S(2)}, u32[]{:S(2)}) collective-permute-start(bf16[2048,256]{1,0:T(8,128)(2,1)} %collective-permute-done), channel_id=1, source_target_pairs={{0,8},{8,0},{16,24},{24,16},{32,40},{40,32},{48,56},{56,48},{64,72... | collective-permute-start | bytes 3145736 | tf_op jit(solution)/shard_map/ppermute | solution.py:225
  53.7 6.8 %collective-permute-start.3 = (bf16[64,40,128]{2,1,0:T(8,128)(2,1)S(1)}, bf16[64,40,128]{2,1,0:T(8,128)(2,1)S(1)}, u32[]{:S(2)}, u32[]{:S(2)}) collective-permute-start(bf16[64,40,128]{2,1,0:T(8,128)(2,1)S(1)} %all-to-all-done.near_ref), channel_id=1, source_target_pairs={{0,8},{8,0},{16,24},{24,16},{32,40},{40,32},{48,56},{56,48},{64,72... | collective-permute-start | bytes 1966088 | tf_op jit(solution)/shard_map/ppermute | solution.py:233
  57.3 3.3 %copy-start.2 = (s32[64]{0:T(128)S(1)}, s32[64]{0:T(128)}, u32[]{:S(2)}) copy-start(s32[64]{0:T(128)} %lookup_ref.1) | copy-start | bytes 772
  61.9 1.6 %copy-start = (bf16[1024,1024]{1,0:T(8,128)(2,1)S(1)}, bf16[1024,1024]{1,0:T(8,128)(2,1)}, u32[]{:S(2)}) copy-start(bf16[1024,1024]{1,0:T(8,128)(2,1)} %all-gather.3.cloned.1.call-done) | copy-start | bytes 6291460
  65.0 14.0 %all-to-all-start.1 = ((bf16[8,64,256]{2,1,0:T(8,128)(2,1)}), bf16[8,64,256]{2,1,0:T(8,128)(2,1)S(1)}, u32[]{:S(2)}, u32[]{:S(2)}) async-start(bf16[8,64,256]{2,1,0:T(8,128)(2,1)} %broadcast_in_dim.24), calls=%async_computation.1 | async-start | bytes 524288 | tf_op jit(solution)/shard_map/all_to_all | solution.py:243
  69.0 2.9 %copy-start.1 = (bf16[1024,1024]{1,0:T(8,128)(2,1)S(1)}, bf16[1024,1024]{1,0:T(8,128)(2,1)}, u32[]{:S(2)}) copy-start(bf16[1024,1024]{1,0:T(8,128)(2,1)} %all-gather.3.cloned.1.call-done) | copy-start | bytes 6291460
  72.6 6.4 %collective-permute-start.2 = (bf16[256,256]{1,0:T(8,128)(2,1)S(1)}, bf16[256,256]{1,0:T(8,128)(2,1)S(1)}, u32[]{:S(2)}, u32[]{:S(2)}) collective-permute-start(bf16[256,256]{1,0:T(8,128)(2,1)S(1)} %project.3), channel_id=1, source_target_pairs={{0,4},{1,5},{2,6},{3,7},{4,0},{5,1},{6,2},{7,3},{8,12},{9,13},{10,... | collective-permute-start | bytes 393224 | tf_op jit(solution)/shard_map/ppermute | solution.py:241
  76.0 0.9 copy-start.4
  76.0 1.0 copy-start.5
  77.1 1.9 %copy-start.3 = (bf16[2,128]{1,0:T(2,128)(2,1)S(1)}, bf16[2,128]{1,0:T(2,128)(2,1)}, u32[]{:S(2)}) copy-start(bf16[2,128]{1,0:T(2,128)(2,1)} %bias_ref.1) | copy-start | bytes 1540
Sparse Core Ops, SparseCore 0:
  9.5 41.6 all-gather.2

commit v2 on v1

--- a/solution.py
+++ b/solution.py
@@ -22,11 +22,12 @@
 QUARTER = MODEL // 4
 WIDE = 2 * HEAD
 SLICE = 2 * RANK // X
-PART = SLICE // 2
-SENT = PART + 8
-
-X_GROUPS = [[0, 1, 2, 3], [4, 5, 6, 7]]
+SENT = SLICE + 8
+BLOCK = MODEL // (2 * X)
+
+SAME_CORE = [list(range(core, GROUPS, 2)) for core in range(2)]
 SIBLING = [(a, a ^ 1) for a in range(GROUPS)]
+X_HOP = [[(a, a // X * X + (a - hop) % X) for a in range(2 * X)] for hop in range(X)]
 Y_PARTNER = [(a, (a + X) % (2 * X)) for a in range(2 * X)]
 
 
@@ -45,7 +46,7 @@
     for x in range(X)
 ]
 
-VMEM_LIMIT = 40 * 1024 * 1024
+VMEM_LIMIT = 16 * 1024 * 1024
 
 
 def vmem(count):
@@ -57,7 +58,7 @@
 
 
 def factors_kernel(lookup_ref, own_ref, near_ref, far_ref, down_ref, up_ref, inverse, up_rows):
-    y, core = own_ref[0], own_ref[1]
+    y, core = own_ref[0], own_ref[2]
 
     @pl.loop(0, GROUPS)
     def _(owner):
@@ -65,13 +66,15 @@
 
     for local in range(GROUPS // 2):
         owner = inverse[(GROUPS // 2) * y + local]
-        mine = near_ref[owner, 0:PART, :]
-        other = far_ref[owner, 0:PART, :]
-        columns = slice(local * 128, (local + 1) * 128)
-        down_ref[0:PART, columns] = jnp.where(core == 0, mine, other)
-        down_ref[PART:SLICE, columns] = jnp.where(core == 0, other, mine)
+        rows = jnp.where(
+            owner % 2 == core, near_ref[owner // 2, 0:SLICE, :], far_ref[owner // 2, 0:SLICE, :]
+        )
+        down_ref[:, local * 128 : (local + 1) * 128] = rows
     for shard in range(GROUPS):
-        rows = near_ref[inverse[shard], PART:SENT, :].astype(jnp.float32)
+        owner = inverse[shard]
+        rows = jnp.where(
+            owner % 2 == core, near_ref[owner // 2, SLICE:SENT, :], far_ref[owner // 2, SLICE:SENT, :]
+        ).astype(jnp.float32)
         up_rows[2 * shard : 2 * shard + 2, :] = rows[0:2]
         up_rows[RANK + 2 * shard : RANK + 2 * shard + 2, :] = rows[2:4]
     up_ref[...] = up_rows[...].astype(jnp.bfloat16)
@@ -95,12 +98,17 @@
     )(lookup, own, near, far)
 
 
-def low_rank_kernel(tokens_ref, down_ref, out_ref):
+def block_start(own_ref, hop):
+    return pl.multiple_of(((own_ref[1] + hop) % X) * BLOCK, BLOCK)
+
+
+def low_rank_kernel(own_ref, *refs):
+    down_ref, out_ref = refs[X:]
     total = None
-    for step in range(X):
+    for hop in range(X):
         part = lax.dot_general(
-            down_ref[:, step * 1024 : (step + 1) * 1024],
-            tokens_ref[step],
+            down_ref[:, pl.ds(block_start(own_ref, hop), BLOCK)],
+            refs[hop][...],
             (((1,), (1,)), ((), ())),
             preferred_element_type=jnp.float32,
         )
@@ -108,38 +116,74 @@
     out_ref[...] = total.astype(jnp.bfloat16)
 
 
-def low_rank(tokens, down):
+def low_rank(own, blocks, down):
     return pl.pallas_call(
         low_rank_kernel,
         out_shape=jax.ShapeDtypeStruct((SLICE, ROWS), jnp.bfloat16),
-        in_specs=vmem(2),
+        in_specs=smem(1) + vmem(X + 1),
         out_specs=vmem(1)[0],
         compiler_params=pltpu.CompilerParams(vmem_limit_bytes=VMEM_LIMIT),
         name="low_rank",
-    )(tokens, down)
-
-
-def project_kernel(tokens_ref, weight_ref, out_ref):
+    )(own, *blocks, down)
+
+
+def project_met_kernel(own_ref, *refs):
+    near_ref, far_ref, out_ref, total = refs[X:]
+    core = own_ref[2]
+    total[...] = jnp.zeros_like(total)
+    for hop in range(X):
+        source = (own_ref[1] + hop) % X
+        rows = pl.ds(pl.multiple_of((source % 2) * BLOCK, BLOCK), BLOCK)
+
+        @pl.when(source // 2 == core)
+        def _():
+            total[...] += jnp.dot(
+                refs[hop][...], near_ref[rows, :], preferred_element_type=jnp.float32
+            )
+
+        @pl.when(source // 2 != core)
+        def _():
+            total[...] += jnp.dot(
+                refs[hop][...], far_ref[rows, :], preferred_element_type=jnp.float32
+            )
+
+    out_ref[...] = total[...].astype(jnp.bfloat16)
+
+
+def project_met(own, blocks, near, far):
+    return pl.pallas_call(
+        project_met_kernel,
+        out_shape=jax.ShapeDtypeStruct((ROWS, WIDE), jnp.bfloat16),
+        in_specs=smem(1) + vmem(X + 2),
+        out_specs=vmem(1)[0],
+        scratch_shapes=[pltpu.VMEM((ROWS, WIDE), jnp.float32)],
+        compiler_params=pltpu.CompilerParams(vmem_limit_bytes=VMEM_LIMIT),
+        name="project_met",
+    )(own, *blocks, near, far)
+
+
+def project_own_kernel(own_ref, *refs):
+    weight_ref, out_ref = refs[X:]
     total = None
-    for step in range(X):
+    for hop in range(X):
         part = jnp.dot(
-            tokens_ref[step],
-            weight_ref[step * 1024 : (step + 1) * 1024, :],
+            refs[hop][...],
+            weight_ref[pl.ds(block_start(own_ref, hop), BLOCK), :],
             preferred_element_type=jnp.float32,
         )
         total = part if total is None else total + part
-    out_ref[...] = total.astype(out_ref.dtype)
-
-
-def project(tokens, weight, dtype):
-    return pl.pallas_call(
-        project_kernel,
-        out_shape=jax.ShapeDtypeStruct((ROWS, WIDE), dtype),
-        in_specs=vmem(2),
+    out_ref[...] = total
+
+
+def project_own(own, blocks, weight):
+    return pl.pallas_call(
+        project_own_kernel,
+        out_shape=jax.ShapeDtypeStruct((ROWS, WIDE), jnp.float32),
+        in_specs=smem(1) + vmem(X + 1),
         out_specs=vmem(1)[0],
         compiler_params=pltpu.CompilerParams(vmem_limit_bytes=VMEM_LIMIT),
-        name="project",
-    )(tokens, weight)
+        name="project_own",
+    )(own, *blocks, weight)
 
 
 def finish_kernel(own_ref, met_ref, low_ref, up_ref, bias_ref, cos_ref, sin_ref, slot_ref, out_ref):
@@ -208,42 +252,40 @@
     lane = lax.axis_index("tensor")
     y, x = lane // X, lane % X
     core = lax.axis_index("rollout") % 2
-
-    down_turned = down_blocks.transpose(1, 2, 0).reshape(X, 2, PART, 128)
+    own = jnp.stack([y, x, core]).astype(jnp.int32)
+
+    weight_sent = lax.dynamic_slice_in_dim(weight, (1 - y) * HALF + core * QUARTER, QUARTER, 0)
+    weight_sent = weight_sent.reshape(QUARTER, WIDE)
+    weight_near = lax.ppermute(weight_sent, ("rollout", "tensor"), WEIGHT_HOP)
+    blocks = [tokens] + [lax.ppermute(tokens, "tensor", X_HOP[hop]) for hop in range(1, X)]
+    weight_far = lax.ppermute(weight_near, "rollout", SIBLING)
+
+    down_blocks, up_blocks, _ = lax.optimization_barrier((down_blocks, up_blocks, weight_sent))
+    down_turned = down_blocks.transpose(1, 2, 0).reshape(X, SLICE, 128)
     down_sent = lax.dynamic_index_in_dim(down_turned, x, 0, keepdims=False)
-    up_sent = jnp.broadcast_to(up_blocks.reshape(1, 4, HEAD), (2, 4, HEAD))
-    sent = jnp.concatenate([down_sent, up_sent, jnp.zeros((2, 4, HEAD), jnp.bfloat16)], 1)
-    sent = jnp.broadcast_to(sent[None], (GROUPS // 2, 2, SENT, HEAD)).reshape(GROUPS, SENT, HEAD)
-    near = lax.all_to_all(sent, "rollout", 0, 0, tiled=True)
-
-    gathered = lax.all_gather(tokens, "tensor", axis=0, axis_index_groups=X_GROUPS)
-
-    weight_sent = lax.dynamic_slice_in_dim(weight, (1 - y) * HALF + core * QUARTER, QUARTER, 0)
-    weight_near = lax.ppermute(
-        weight_sent.reshape(QUARTER, WIDE), ("rollout", "tensor"), WEIGHT_HOP
-    )
-    weight_far = lax.ppermute(weight_near, "rollout", SIBLING)
-    weight_met = jnp.where(
-        core == 0,
-        jnp.concatenate([weight_near, weight_far], 0),
-        jnp.concatenate([weight_far, weight_near], 0),
-    )
+    sent = jnp.concatenate(
+        [down_sent, up_blocks.reshape(4, HEAD), jnp.zeros((4, HEAD), jnp.bfloat16)], 0
+    )
+    sent = jnp.broadcast_to(sent[None], (GROUPS // 2, SENT, HEAD))
+    near = lax.all_to_all(sent, "rollout", 0, 0, tiled=True, axis_index_groups=SAME_CORE)
+
+    partial_met = project_met(own, blocks, weight_near, weight_far)
+    partial_in = lax.ppermute(partial_met, "tensor", Y_PARTNER)
     weight_own = lax.dynamic_slice_in_dim(weight, y * HALF, HALF, 0).reshape(HALF, WIDE)
-
-    far = lax.ppermute(near, "rollout", SIBLING)
-    own = jnp.stack([y, core]).astype(jnp.int32)
-    down, up = factors(lookup, own, near, far)
-
+    partial_own = project_own(own, blocks, weight_own)
     cosine, sine = turn_tables(positions_of(lengths[0]))
     slots = slot_index(routes).reshape(1, ROWS)
 
-    partial_met = project(gathered, weight_met, jnp.bfloat16)
-    partial_in = lax.ppermute(partial_met, "tensor", Y_PARTNER)
-    low = low_rank(gathered, down)
+    near, cosine, sine, slots, partial_own, partial_in = lax.optimization_barrier(
+        (near, cosine, sine, slots, partial_own, partial_in)
+    )
+    far = lax.ppermute(near, "rollout", SIBLING)
+    down, up = factors(lookup, own, near, far)
+
+    low = low_rank(own, blocks, down)
     low_all = lax.all_to_all(
         jnp.broadcast_to(low[None], (2 * X, SLICE, ROWS)), "tensor", 0, 0, tiled=True
     )
-    partial_own = project(gathered, weight_own, jnp.float32)
     outgoing = finish(partial_own, partial_in, low_all, up, bias, cosine, sine, slots)
     arrived = lax.all_to_all(outgoing, "rollout", 0, 0, tiled=True)
     return arrived.reshape(GROUPS * CAP, 2, HEAD)

time: 113 us -> 99.8 us (0.88)
  waiting for transfers between devices: 19.4 us -> 4.96 us
  between operations: 13.7 us -> 0.33 us
  blocking collectives: 25.2 us -> 38.3 us
  Pallas kernels: 4.11 us -> 7.98 us
  other arithmetic: 4.74 us -> 1.24 us
  starting transfers between devices: 34.8 us -> 38 us
  local copies, waits for them, and re-layouts: 10.5 us -> 8.46 us
    all_to_all x2 -> x1, waiting for transfers between devices: 17.5 us -> 0.01 us  [body(): lax.all_to_all(sent, 'rollout', 0, 0, tiled=True, axis_index_groups=SAME_...]
    all_to_all x0 -> x1, blocking collectives: none -> 12.5 us  [body(): lax.all_to_all(jnp.broadcast_to(low[None], (2 * X, SLICE, ROWS)), 'tensor...]
    ppermute x1 -> x4, starting transfers between devices: 5.93 us -> 16.5 us  [the longest x3 10.5 us: body(): lax.ppermute(tokens, 'tensor', X_HOP[hop])]
    all_to_all x2 -> x1, starting transfers between devices: 18.3 us -> 12.7 us  [body(): lax.all_to_all(sent, 'rollout', 0, 0, tiled=True, axis_index_groups=SAME_...]
    select_n x1 -> x0, other arithmetic: 2.8 us -> none  [body(): jnp.where(core == 0, jnp.concatenate([weight_near, weight_far], 0), jnp.c...]
    pallas_call x2, Pallas kernels: 1.41 us -> 4.15 us  [the longest x1 2.86 us: project_met(): pl.pallas_call(project_met_kernel, out_shape=jax.ShapeDtypeStruct((ROWS,...]
    ppermute x1, waiting for transfers between devices: 1.2 us -> 3.34 us  [body(): partial_in = lax.ppermute(partial_met, 'tensor', Y_PARTNER)]
    ppermute x1, waiting for transfers between devices: 0.01 us -> 1.61 us  [body(): far = lax.ppermute(near, 'rollout', SIBLING)]
  transfers between devices with their start and end apart: 7 -> 8, of which waited for: 2 -> 2; matrix products, arithmetic and copies ran while one was open for 11% -> 6% of each run, Pallas kernels for 3% -> 4%
where the time goes in v2:
time: 99.8 us; the launch traced here: 99.3 us
  blocking collectives  38.3 us (38%)
  starting transfers between devices  38 us (38%)
  local copies, waits for them, and re-layouts  8.46 us (8%)
  Pallas kernels  7.98 us (8%)
  waiting for transfers between devices  4.96 us (5%)
  other arithmetic  1.24 us (1%)
    all_to_all x1, blocking collectives, body(): arrived = lax.all_to_all(outgoing, 'rollout', 0, 0, tiled=True)  25.8 us
    all_to_all x1, starting transfers between devices, body(): lax.all_to_all(sent, 'rollout', 0, 0, tiled=True, axis_index_groups=SAME_...  12.7 us
    all_to_all x1, blocking collectives, body(): lax.all_to_all(jnp.broadcast_to(low[None], (2 * X, SLICE, ROWS)), 'tensor...  12.5 us
    ppermute x3, starting transfers between devices, body(): lax.ppermute(tokens, 'tensor', X_HOP[hop])  10.5 us
    ppermute x1, starting transfers between devices, body(): weight_near = lax.ppermute(weight_sent, ('rollout', 'tensor'), WEIGHT_HOP)  5.92 us
    ppermute x1, starting transfers between devices, body(): weight_far = lax.ppermute(weight_near, 'rollout', SIBLING)  4.21 us
    ppermute x1, waiting for transfers between devices, body(): partial_in = lax.ppermute(partial_met, 'tensor', Y_PARTNER)  3.34 us
    dynamic_slice x1, local copies, waits for them, and re-layouts, body(): lax.dynamic_slice_in_dim(weight, y * HALF, HALF, 0).reshape(HALF, WIDE)  3.25 us
  transfers between devices with their start and end apart: 8, of which 2 were waited for; matrix products, arithmetic and copies ran while one was open for 6% of the time, Pallas kernels for 4%

profile of v2, /device:TPU:1, one launch (start us, length us, event | category | flops | bytes accessed | tf_op | source)
XLA Modules:
  0.0 99.3 jit_solution(16840442582283133393)
XLA Ops:
  0.0 0.0 copy-start.6
  0.0 0.0 copy-start.4
  0.1 1.9 %constant_dynamic-slice_fusion.1 = bf16[2048,2,128]{2,1,0:T(2,128)(2,1)S(1)} fusion(bf16[8192,2,128]{2,1,0:T(2,128)(2,1)} %param.9, s32[]{:T(128)S(6)} %select_n.31), kind=kLoop, calls=%fused_computation.17 | loop fusion | bytes 2097156 | tf_op jit(solution)/shard_map/dynamic_slice | solution.py:257
  1.9 1.2 %copy.17 = bf16[256,8,2,128]{3,1,2,0:T(8,128)(2,1)} copy(bf16[256,8,2,128]{3,2,1,0:T(2,128)(2,1)S(1)} %bitcast.23) | data formatting | bytes 2097152
  3.1 5.9 %collective-permute-start.3 = (bf16[2048,256]{1,0:T(8,128)(2,1)}, bf16[2048,256]{1,0:T(8,128)(2,1)}, u32[]{:S(2)}, u32[]{:S(2)}) collective-permute-start(bf16[2048,256]{1,0:T(8,128)(2,1)} %bitcast.19), channel_id=1, source_target_pairs={{0,4},{1,5},{2,6},{3,7},{8,60},{9,61},{10,62},{11,63},{4,16},{5,17... | collective-permute-start | bytes 3145736 | tf_op jit(solution)/shard_map/ppermute | solution.py:259
  9.0 0.0 copy-done
  9.0 3.1 %collective-permute-start.2 = (bf16[256,1024]{1,0:T(8,128)(2,1)S(1)}, bf16[256,1024]{1,0:T(8,128)(2,1)S(1)}, u32[]{:S(2)}, u32[]{:S(2)}) collective-permute-start(bf16[256,1024]{1,0:T(8,128)(2,1)S(1)} %copy-done), channel_id=1, source_target_pairs={{0,1},{1,2},{2,3},{3,0},{4,5},{5,6},{6,7},{7,4},{8,9},{9,10},{10,1... | collective-permute-start | bytes 1572872 | tf_op jit(solution)/shard_map/ppermute | solution.py:260
  12.1 4.4 %collective-permute-start.1 = (bf16[256,1024]{1,0:T(8,128)(2,1)S(1)}, bf16[256,1024]{1,0:T(8,128)(2,1)S(1)}, u32[]{:S(2)}, u32[]{:S(2)}) collective-permute-start(bf16[256,1024]{1,0:T(8,128)(2,1)S(1)} %copy-done), channel_id=1, source_target_pairs={{0,2},{1,3},{2,0},{3,1},{4,6},{5,7},{6,4},{7,5},{8,10},{9,11},{10,... | collective-permute-start | bytes 1572872 | tf_op jit(solution)/shard_map/ppermute | solution.py:260
  16.5 3.1 %collective-permute-start = (bf16[256,1024]{1,0:T(8,128)(2,1)S(1)}, bf16[256,1024]{1,0:T(8,128)(2,1)S(1)}, u32[]{:S(2)}, u32[]{:S(2)}) collective-permute-start(bf16[256,1024]{1,0:T(8,128)(2,1)S(1)} %copy-done), channel_id=1, source_target_pairs={{0,3},{1,0},{2,1},{3,2},{4,7},{5,4},{6,5},{7,6},{8,11},{9,8},{10,9... | collective-permute-start | bytes 1572872 | tf_op jit(solution)/shard_map/ppermute | solution.py:260
  19.6 0.0 copy-done.3
  19.6 0.1 copy.11
  19.7 0.1 pad.9.clone
  19.8 0.0 copy-done.5
  19.8 0.1 maximum_maximum_fusion
  19.9 0.9 broadcast_in_dim.17
  20.8 12.7 %all-to-all-start = ((bf16[32,72,128]{2,1,0:T(8,128)(2,1)}), bf16[32,72,128]{2,1,0:T(8,128)(2,1)S(1)}, u32[]{:S(2)}, u32[]{:S(2)}) async-start(bf16[32,72,128]{2,1,0:T(8,128)(2,1)} %broadcast_in_dim.17), calls=%async_computation | async-start | bytes 1179648 | tf_op jit(solution)/shard_map/all_to_all | solution.py:270
  33.5 0.0 copy-done.6
  33.5 0.2 reduce-window_clone.1
  33.7 0.1 select_reduce_fusion
  33.8 0.0 collective-permute-done.3.refs_4_
  33.8 4.2 %collective-permute-start.4 = (bf16[2048,256]{1,0:T(8,128)(2,1)}, bf16[2048,256]{1,0:T(8,128)(2,1)}, u32[]{:S(2)}, u32[]{:S(2)}) collective-permute-start(bf16[2048,256]{1,0:T(8,128)(2,1)} %collective-permute-done.3.refs_4_), channel_id=1, source_target_pairs={{0,8},{8,0},{16,24},{24,16},{32,40},{40,32},{48,56},{56,48},{64,72... | collective-permute-start | bytes 3145736 | tf_op jit(solution)/shard_map/ppermute | solution.py:261
  38.0 0.0 copy-done.4
  38.0 0.1 convert_reduce_fusion
  38.1 0.1 pad_add_fusion.own_ref
  38.2 0.5 fusion.1
  38.8 3.2 %constant_dynamic-slice_fusion = bf16[4096,2,128]{2,1,0:T(2,128)(2,1)S(1)} fusion(bf16[8192,2,128]{2,1,0:T(2,128)(2,1)} %param.9, s32[]{:T(128)S(6)} %select_n.35), kind=kLoop, calls=%fused_computation.16 | loop fusion | bytes 4194308 | tf_op jit(solution)/shard_map/dynamic_slice | solution.py:274
  42.0 0.0 collective-permute-done.2.refs_3_
  42.0 0.0 collective-permute-done.1.refs_2_
  42.0 0.0 collective-permute-done.refs_1_
  42.1 0.0 collective-permute-done.4.refs_5_
  42.1 2.9 %project_met.1 = bf16[256,256]{1,0:T(8,128)(2,1)S(1)} custom-call(s32[3]{0:T(128)S(1)} %pad_add_fusion.own_ref, bf16[256,1024]{1,0:T(8,128)(2,1)S(1)} %copy-done, bf16[256,1024]{1,0:T(8,128)(2,1)S(1)} %collective-permute-done.refs_1_, bf16[256,1024]{1,0:T(8,128)(2,1)S(1)} %collective-permute-done.1.refs_2_, ...), custom_call_target="tpu_custom_call" | custom-call | tf_op jit(solution)/shard_map/project_met/pallas_call | solution.py:154
  44.9 2.3 %collective-permute-start.5 = (bf16[256,256]{1,0:T(8,128)(2,1)S(1)}, bf16[256,256]{1,0:T(8,128)(2,1)S(1)}, u32[]{:S(2)}, u32[]{:S(2)}) collective-permute-start(bf16[256,256]{1,0:T(8,128)(2,1)S(1)} %project_met.1), channel_id=1, source_target_pairs={{0,4},{1,5},{2,6},{3,7},{4,0},{5,1},{6,2},{7,3},{8,12},{9,13},{10,... | collective-permute-start | bytes 393224 | tf_op jit(solution)/shard_map/ppermute | solution.py:273
  47.3 0.0 copy-start.1
  47.3 0.3 copy.16
  47.5 0.1 pad_maximum_fusion
  47.7 0.0 copy-start.2
  47.7 1.3 %project_own.1.own_ref = f32[256,256]{1,0:T(8,128)S(1)} custom-call(s32[3]{0:T(128)S(1)} %pad_add_fusion.own_ref, bf16[256,1024]{1,0:T(8,128)(2,1)S(1)} %copy-done, bf16[256,1024]{1,0:T(8,128)(2,1)S(1)} %collective-permute-done.refs_1_, bf16[256,1024]{1,0:T(8,128)(2,1)S(1)} %collective-permute-done.1.refs_2_, ...), custom_call_target="tpu_custom_call" | custom-call | tf_op jit(solution)/shard_map/project_own/pallas_call | solution.py:179
  49.0 0.0 all-to-all-done.near_ref
  49.0 3.3 %collective-permute-done.5.met_ref = bf16[256,256]{1,0:T(8,128)(2,1)S(1)} collective-permute-done((bf16[256,256]{1,0:T(8,128)(2,1)S(1)}, bf16[256,256]{1,0:T(8,128)(2,1)S(1)}, u32[]{:S(2)}, u32[]{:S(2)}) %collective-permute-start.5) | collective-permute-done | bytes 131104 | tf_op jit(solution)/shard_map/ppermute | solution.py:273
  52.4 2.4 %collective-permute-start.6 = (bf16[32,72,128]{2,1,0:T(8,128)(2,1)S(1)}, bf16[32,72,128]{2,1,0:T(8,128)(2,1)S(1)}, u32[]{:S(2)}, u32[]{:S(2)}) collective-permute-start(bf16[32,72,128]{2,1,0:T(8,128)(2,1)S(1)} %all-to-all-done.near_ref), channel_id=1, source_target_pairs={{0,8},{8,0},{16,24},{24,16},{32,40},{40,32},{48,56},{56,48},{64,72... | collective-permute-start | bytes 1769480 | tf_op jit(solution)/shard_map/ppermute | solution.py:282
  54.7 1.6 %collective-permute-done.6.far_ref = bf16[32,72,128]{2,1,0:T(8,128)(2,1)S(1)} collective-permute-done((bf16[32,72,128]{2,1,0:T(8,128)(2,1)S(1)}, bf16[32,72,128]{2,1,0:T(8,128)(2,1)S(1)}, u32[]{:S(2)}, u32[]{:S(2)}) %collective-permute-start.6) | collective-permute-done | bytes 589856 | tf_op jit(solution)/shard_map/ppermute | solution.py:282
  56.3 0.0 copy-done.1
  56.3 1.9 %factors.1 = (bf16[64,4096]{1,0:T(8,128)(2,1)S(1)}, bf16[256,128]{1,0:T(8,128)(2,1)S(1)}) custom-call(s32[64]{0:T(128)S(1)} %copy-done.1, s32[3]{0:T(128)S(1)} %pad_add_fusion.own_ref, bf16[32,72,128]{2,1,0:T(8,128)(2,1)S(1)} %all-to-all-done.near_ref, bf16[32,72,128]{2,1,0:T(8,128)(2,1)S(1)} %collective-permute-done.6.far_ref), custom_call_target="tpu_custom_call" | custom-call | tf_op jit(solution)/shard_map/factors/pallas_call | solution.py:84
  58.3 1.3 %low_rank.1 = bf16[64,256]{1,0:T(8,128)(2,1)S(1)} custom-call(s32[3]{0:T(128)S(1)} %pad_add_fusion.own_ref, bf16[256,1024]{1,0:T(8,128)(2,1)S(1)} %copy-done, bf16[256,1024]{1,0:T(8,128)(2,1)S(1)} %collective-permute-done.refs_1_, bf16[256,1024]{1,0:T(8,128)(2,1)S(1)} %collective-permute-done.1.refs_2_, ...), custom_call_target="tpu_custom_call" | custom-call | tf_op jit(solution)/shard_map/low_rank/pallas_call | solution.py:120
  59.6 12.5 %all_to_all.15.low_ref = bf16[8,64,256]{2,1,0:T(8,128)(2,1)S(1)} all-to-all(bf16[8,64,256]{2,1,0:T(8,128)(2,1)S(1)} %broadcast_in_dim.19), channel_id=1, replica_groups=mesh['rollout'=64,'tensor'=8] {'tensor'}, dimensions={0} | all-to-all | bytes 524288 | tf_op jit(solution)/shard_map/all_to_all | solution.py:286
  72.1 0.6 finish.1
  72.7 25.8 %all_to_all.16 = bf16[64,8,256]{2,1,0:T(8,128)(2,1)S(1)} all-to-all(bf16[64,8,256]{2,1,0:T(8,128)(2,1)S(1)} %finish.1), channel_id=1, replica_groups=mesh['rollout'=64,'tensor'=8] {'rollout'}, dimensions={0} | all-to-all | bytes 524288 | tf_op jit(solution)/shard_map/all_to_all | solution.py:290
  98.5 0.8 reshape.47
  (11 shorter events, 0.1 us)
Async XLA Ops:
  0.0 9.0 %copy-start = (bf16[256,1024]{1,0:T(8,128)(2,1)S(1)}, bf16[256,1024]{1,0:T(8,128)(2,1)}, u32[]{:S(2)}) copy-start(bf16[256,1024]{1,0:T(8,128)(2,1)} %refs_0_.5) | copy-start | bytes 1572868
  0.0 19.8 %copy-start.5 = (bf16[2,2,128]{2,1,0:T(2,128)(2,1)S(1)}, bf16[2,2,128]{2,1,0:T(2,128)(2,1)}, u32[]{:S(2)}) copy-start(bf16[2,2,128]{2,1,0:T(2,128)(2,1)} %param.12) | copy-start | bytes 3076
  0.0 19.6 %copy-start.3 = (bf16[128,2,128]{2,1,0:T(2,128)(2,1)S(1)}, bf16[128,2,128]{2,1,0:T(2,128)(2,1)}, u32[]{:S(2)}) copy-start(bf16[128,2,128]{2,1,0:T(2,128)(2,1)} %param.11) | copy-start | bytes 196612
  0.0 33.5 %copy-start.6 = (s32[1,8]{1,0:T(1,128)S(1)}, s32[1,8]{1,0:T(1,128)}, u32[]{:S(2)}) copy-start(s32[1,8]{1,0:T(1,128)} %param.14) | copy-start | bytes 100
  0.0 38.0 %copy-start.4 = (s32[256]{0:T(256)S(1)}, s32[256]{0:T(256)}, u32[]{:S(2)}) copy-start(s32[256]{0:T(256)} %param.15) | copy-start | bytes 3076
  3.1 30.7 %collective-permute-start.3 = (bf16[2048,256]{1,0:T(8,128)(2,1)}, bf16[2048,256]{1,0:T(8,128)(2,1)}, u32[]{:S(2)}, u32[]{:S(2)}) collective-permute-start(bf16[2048,256]{1,0:T(8,128)(2,1)} %bitcast.19), channel_id=1, source_target_pairs={{0,4},{1,5},{2,6},{3,7},{8,60},{9,61},{10,62},{11,63},{4,16},{5,17... | collective-permute-start | bytes 3145736 | tf_op jit(solution)/shard_map/ppermute | solution.py:259
  9.0 33.0 %collective-permute-start.2 = (bf16[256,1024]{1,0:T(8,128)(2,1)S(1)}, bf16[256,1024]{1,0:T(8,128)(2,1)S(1)}, u32[]{:S(2)}, u32[]{:S(2)}) collective-permute-start(bf16[256,1024]{1,0:T(8,128)(2,1)S(1)} %copy-done), channel_id=1, source_target_pairs={{0,1},{1,2},{2,3},{3,0},{4,5},{5,6},{6,7},{7,4},{8,9},{9,10},{10,1... | collective-permute-start | bytes 1572872 | tf_op jit(solution)/shard_map/ppermute | solution.py:260
  12.1 29.9 %collective-permute-start.1 = (bf16[256,1024]{1,0:T(8,128)(2,1)S(1)}, bf16[256,1024]{1,0:T(8,128)(2,1)S(1)}, u32[]{:S(2)}, u32[]{:S(2)}) collective-permute-start(bf16[256,1024]{1,0:T(8,128)(2,1)S(1)} %copy-done), channel_id=1, source_target_pairs={{0,2},{1,3},{2,0},{3,1},{4,6},{5,7},{6,4},{7,5},{8,10},{9,11},{10,... | collective-permute-start | bytes 1572872 | tf_op jit(solution)/shard_map/ppermute | solution.py:260
  16.5 25.5 %collective-permute-start = (bf16[256,1024]{1,0:T(8,128)(2,1)S(1)}, bf16[256,1024]{1,0:T(8,128)(2,1)S(1)}, u32[]{:S(2)}, u32[]{:S(2)}) collective-permute-start(bf16[256,1024]{1,0:T(8,128)(2,1)S(1)} %copy-done), channel_id=1, source_target_pairs={{0,3},{1,0},{2,1},{3,2},{4,7},{5,4},{6,5},{7,6},{8,11},{9,8},{10,9... | collective-permute-start | bytes 1572872 | tf_op jit(solution)/shard_map/ppermute | solution.py:260
  20.8 28.2 %all-to-all-start = ((bf16[32,72,128]{2,1,0:T(8,128)(2,1)}), bf16[32,72,128]{2,1,0:T(8,128)(2,1)S(1)}, u32[]{:S(2)}, u32[]{:S(2)}) async-start(bf16[32,72,128]{2,1,0:T(8,128)(2,1)} %broadcast_in_dim.17), calls=%async_computation | async-start | bytes 1179648 | tf_op jit(solution)/shard_map/all_to_all | solution.py:270
  33.8 8.3 %collective-permute-start.4 = (bf16[2048,256]{1,0:T(8,128)(2,1)}, bf16[2048,256]{1,0:T(8,128)(2,1)}, u32[]{:S(2)}, u32[]{:S(2)}) collective-permute-start(bf16[2048,256]{1,0:T(8,128)(2,1)} %collective-permute-done.3.refs_4_), channel_id=1, source_target_pairs={{0,8},{8,0},{16,24},{24,16},{32,40},{40,32},{48,56},{56,48},{64,72... | collective-permute-start | bytes 3145736 | tf_op jit(solution)/shard_map/ppermute | solution.py:261
  44.9 7.4 %collective-permute-start.5 = (bf16[256,256]{1,0:T(8,128)(2,1)S(1)}, bf16[256,256]{1,0:T(8,128)(2,1)S(1)}, u32[]{:S(2)}, u32[]{:S(2)}) collective-permute-start(bf16[256,256]{1,0:T(8,128)(2,1)S(1)} %project_met.1), channel_id=1, source_target_pairs={{0,4},{1,5},{2,6},{3,7},{4,0},{5,1},{6,2},{7,3},{8,12},{9,13},{10,... | collective-permute-start | bytes 393224 | tf_op jit(solution)/shard_map/ppermute | solution.py:273
  47.3 9.1 %copy-start.1 = (s32[64]{0:T(128)S(1)}, s32[64]{0:T(128)}, u32[]{:S(2)}) copy-start(s32[64]{0:T(128)} %lookup_ref.1) | copy-start | bytes 772
  47.7 24.4 %copy-start.2 = (bf16[2,128]{1,0:T(2,128)(2,1)S(1)}, bf16[2,128]{1,0:T(2,128)(2,1)}, u32[]{:S(2)}) copy-start(bf16[2,128]{1,0:T(2,128)(2,1)} %bias_ref.1) | copy-start | bytes 1540
  52.4 4.0 %collective-permute-start.6 = (bf16[32,72,128]{2,1,0:T(8,128)(2,1)S(1)}, bf16[32,72,128]{2,1,0:T(8,128)(2,1)S(1)}, u32[]{:S(2)}, u32[]{:S(2)}) collective-permute-start(bf16[32,72,128]{2,1,0:T(8,128)(2,1)S(1)} %all-to-all-done.near_ref), channel_id=1, source_target_pairs={{0,8},{8,0},{16,24},{24,16},{32,40},{40,32},{48,56},{56,48},{64,72... | collective-permute-start | bytes 1769480 | tf_op jit(solution)/shard_map/ppermute | solution.py:282

commit v3 on v1

v3 whole, which is shorter than its diff:
```python
import functools

import jax
import jax.numpy as jnp
import numpy as np
from jax import lax
from jax.experimental import pallas as pl
from jax.experimental.pallas import tpu as pltpu
from jax.sharding import PartitionSpec as P

HEAD = 128
GROUPS = 64
RANK = 128
MODEL = 8192
ROWS = 256
CAP = 8
X = 4

adapter_scale = 2.0
rope_base = 1000000.0

SHARE = 2 * X
WIDE = 2 * HEAD
SLICE = 2 * RANK // SHARE
SENT = SLICE + 8
BLOCK = MODEL // SHARE

SAME_CORE = [list(range(core, GROUPS, 2)) for core in range(2)]
SIBLING = [(a, a ^ 1) for a in range(GROUPS)]
X_HOP = [[(a, a // X * X + (a - hop) % X) for a in range(2 * X)] for hop in range(X)]
Y_PARTNER = [(a, (a + X) % (2 * X)) for a in range(2 * X)]


VMEM_LIMIT = 16 * 1024 * 1024
BUFFERS = 4

BESIDE = pl.CostEstimate(flops=8 * 10**9, bytes_accessed=0, transcendentals=0)


def vmem(count):
    return [pl.BlockSpec(memory_space=pltpu.VMEM)] * count


def in_hbm(array):
    return pltpu.with_memory_space_constraint(array, pltpu.HBM)


def hbm(count):
    return [pl.BlockSpec(memory_space=pltpu.HBM)] * count


def smem(count):
    return [pl.BlockSpec(memory_space=pltpu.SMEM)] * count


def share_kernel(
    own_ref,
    lengths_ref,
    rate_ref,
    down_hbm,
    up_hbm,
    out_ref,
    turn_ref,
    down_ref,
    up_ref,
    wide,
    turned,
    done,
):
    down_copy = pltpu.make_async_copy(down_hbm, down_ref, done.at[0])
    up_copy = pltpu.make_async_copy(up_hbm, up_ref, done.at[1])
    down_copy.start()
    up_copy.start()
    row = lax.broadcasted_iota(jnp.int32, (ROWS, HEAD), 0)
    begins = jnp.zeros((ROWS, HEAD), jnp.int32)
    start = jnp.int32(0)
    for piece in range(lengths_ref.shape[1]):
        begins = jnp.where(row >= start, jnp.maximum(begins, start), begins)
        start = start + lengths_ref[0, piece]
    angles = (row - begins).astype(jnp.float32) * rate_ref[...]
    low_half = lax.broadcasted_iota(jnp.int32, (ROWS, HEAD), 1) < HEAD // 2
    turn_ref[...] = jnp.cos(jnp.where(low_half, angles, angles - np.float32(np.pi / 2)))
    down_copy.wait()
    up_copy.wait()
    lane = own_ref[0] * X + own_ref[1]
    wide[...] = down_ref[...].astype(jnp.float32)
    turned[...] = wide[pl.ds(lane // X, 128, stride=2), :].T
    first = pl.multiple_of((lane % X) * SLICE, SLICE)
    down = turned[pl.ds(first, SLICE), :].astype(jnp.bfloat16)
    up = jnp.concatenate([up_ref[...], jnp.zeros((SENT - SLICE - 4, HEAD), jnp.bfloat16)], 0)
    sent = jnp.concatenate([down, up], 0)
    for target in range(GROUPS // 2):
        out_ref[target] = sent


def share(own, lengths, down_rows, up_rows):
    half_rate = rope_base ** (-(np.arange(HEAD // 2, dtype=np.float32) * 2.0) / HEAD)
    rate = jnp.asarray(np.concatenate([half_rate, half_rate])[None], jnp.float32)
    return pl.pallas_call(
        share_kernel,
        out_shape=(
            jax.ShapeDtypeStruct((GROUPS // 2, SENT, HEAD), jnp.bfloat16),
            pltpu.HBM((ROWS, HEAD), jnp.float32),
        ),
        in_specs=smem(2) + vmem(1) + hbm(2),
        out_specs=tuple(vmem(2)),
        scratch_shapes=[
            pltpu.VMEM((2 * 128, RANK), jnp.bfloat16),
            pltpu.VMEM((4, HEAD), jnp.bfloat16),
            pltpu.VMEM((2 * 128, RANK), jnp.float32),
            pltpu.VMEM((RANK, 128), jnp.float32),
            pltpu.SemaphoreType.DMA((2,)),
        ],
        compiler_params=pltpu.CompilerParams(vmem_limit_bytes=VMEM_LIMIT),
        name="share",
    )(own, in_hbm(lengths), in_hbm(rate), in_hbm(down_rows), in_hbm(up_rows))


def source_of(own_ref, place):
    return (own_ref[0] + place // X) % 2 * X + (own_ref[1] + place) % X


def low_part(own_ref, blocks, down_ref, places):
    total = None
    for block, place in zip(blocks, places):
        first = pl.multiple_of(source_of(own_ref, place) * BLOCK, BLOCK)
        part = lax.dot_general(
            block[...],
            down_ref[:, pl.ds(first, BLOCK)],
            (((1,), (1,)), ((), ())),
            preferred_element_type=jnp.float32,
        )
        total = part if total is None else total + part
    return total


def low_begin_kernel(places, lookup_ref, own_ref, near_ref, far_ref, tokens_ref, *refs):
    down_ref, begun_ref, up_ref, inverse, up_rows, held, done = refs[len(places) - 1 :]
    copy = pltpu.make_async_copy(tokens_ref, held, done)
    copy.start()
    core = own_ref[2]
    for owner in range(GROUPS):
        inverse[lookup_ref[owner]] = owner
    for shard in range(GROUPS):
        owner = inverse[shard]
        rows = jnp.where(owner % 2 == core, near_ref[owner // 2], far_ref[owner // 2])
        down_ref[:, shard * 128 : (shard + 1) * 128] = rows[0:SLICE]
        rows = rows[SLICE:SENT].astype(jnp.float32)
        up_rows[2 * shard : 2 * shard + 2, :] = rows[0:2]
        up_rows[RANK + 2 * shard : RANK + 2 * shard + 2, :] = rows[2:4]
    up_ref[...] = up_rows[...].astype(jnp.bfloat16)
    copy.wait()
    begun_ref[...] = low_part(own_ref, [*refs[: len(places) - 1], held], down_ref, places)


def low_begin(lookup, own, near, far, blocks, places):
    return pl.pallas_call(
        functools.partial(low_begin_kernel, places),
        out_shape=(
            jax.ShapeDtypeStruct((SLICE, MODEL), jnp.bfloat16),
            jax.ShapeDtypeStruct((ROWS, SLICE), jnp.float32),
            pltpu.HBM((2 * RANK, HEAD), jnp.bfloat16),
        ),
        in_specs=smem(2) + vmem(2) + hbm(1) + vmem(len(places) - 1),
        out_specs=tuple(vmem(3)),
        scratch_shapes=[
            pltpu.SMEM((GROUPS,), jnp.int32),
            pltpu.VMEM((2 * RANK, HEAD), jnp.float32),
            pltpu.VMEM((ROWS, BLOCK), jnp.bfloat16),
            pltpu.SemaphoreType.DMA,
        ],
        compiler_params=pltpu.CompilerParams(vmem_limit_bytes=VMEM_LIMIT),
        name="low_begin",
    )(
        in_hbm(lookup),
        own,
        near,
        far,
        in_hbm(blocks[0]),
        *[blocks[place] for place in places if place],
    )


def low_end_kernel(places, own_ref, down_ref, begun_ref, *refs):
    total = begun_ref[...] + low_part(own_ref, refs[:-1], down_ref, places)
    low = total.T.astype(jnp.bfloat16)
    for target in range(SHARE):
        refs[-1][target] = low


def low_end(own, down, begun, blocks, places):
    return pl.pallas_call(
        functools.partial(low_end_kernel, places),
        out_shape=pltpu.HBM((SHARE, SLICE, ROWS), jnp.bfloat16),
        in_specs=smem(1) + vmem(2 + len(places)),
        out_specs=vmem(1)[0],
        compiler_params=pltpu.CompilerParams(vmem_limit_bytes=VMEM_LIMIT),
        name="low_end",
    )(own, down, begun, *[blocks[place] for place in places])


def weight_copies(own_ref, weight_ref, weights, done, places):
    copies = []
    for at, place in enumerate(places):
        first = pl.multiple_of(source_of(own_ref, place) * (2 * BLOCK), 2 * BLOCK)
        copies.append(
            pltpu.make_async_copy(
                weight_ref.at[pl.ds(first, 2 * BLOCK)],
                weights.at[at % BUFFERS],
                done.at[at % BUFFERS],
            )
        )
    return copies


def project_blocks(copies, blocks, weights):
    total = None
    for at, (copy, block) in enumerate(zip(copies, blocks)):
        copy.wait()
        part = jnp.dot(
            block[...],
            weights[at % BUFFERS].reshape(BLOCK, WIDE),
            preferred_element_type=jnp.float32,
        )
        total = part if total is None else total + part
        if at + BUFFERS < len(copies):
            copies[at + BUFFERS].start()
    return total


def begin_kernel(places, own_ref, weight_ref, *refs):
    out_ref, weights, done = refs[len(places) :]
    copies = weight_copies(own_ref, weight_ref, weights, done, places)
    for copy in copies[:BUFFERS]:
        copy.start()
    out_ref[...] = project_blocks(copies, refs[: len(places)], weights)


def begin(own, blocks, places, weight_rows):
    return pl.pallas_call(
        functools.partial(begin_kernel, places),
        out_shape=pltpu.HBM((ROWS, WIDE), jnp.float32),
        in_specs=smem(1) + hbm(1) + vmem(len(places)),
        out_specs=vmem(1)[0],
        scratch_shapes=[
            pltpu.VMEM((BUFFERS, 2 * BLOCK, HEAD), jnp.bfloat16),
            pltpu.SemaphoreType.DMA((BUFFERS,)),
        ],
        cost_estimate=BESIDE,
        compiler_params=pltpu.CompilerParams(vmem_limit_bytes=VMEM_LIMIT),
        name="begin",
    )(own, weight_rows, *[blocks[place] for place in places])


def project_kernel(
    places, own_ref, weight_ref, tokens_ref, turn_ref, up_ref, begun_ref, bias_ref, *refs
):
    out_ref, weights, tokens, turn, up, begun, weight_done, done = refs[len(places) - 1 :]
    copies = weight_copies(own_ref, weight_ref, weights, weight_done, places)
    for copy in copies[:BUFFERS]:
        copy.start()
    small = [
        pltpu.make_async_copy(from_ref, to_ref, done.at[at])
        for at, (from_ref, to_ref) in enumerate(
            [(turn_ref, turn), (up_ref, up), (begun_ref, begun), (tokens_ref, tokens)]
        )
    ]
    for copy in small:
        copy.start()
    for copy in small:
        copy.wait()
    table = turn[...]
    swapped = pltpu.roll(table, HEAD // 2, 1)
    low_half = lax.broadcasted_iota(jnp.int32, (ROWS, HEAD), 1) < HEAD // 2
    cosine = jnp.where(low_half, table, swapped)
    sine = jnp.where(low_half, -swapped, table)
    out_ref[:, WIDE : WIDE + HEAD] = cosine
    out_ref[:, WIDE + HEAD : 2 * WIDE] = sine
    out_ref[:, 2 * WIDE :] = up[...].astype(jnp.float32)
    total = begun[...] + project_blocks(copies, [*refs[: len(places) - 1], tokens], weights)
    keys = total[:, :HEAD] + bias_ref[0:1, :].astype(jnp.float32)
    out_ref[:, :HEAD] = keys * cosine + pltpu.roll(keys, HEAD // 2, 1) * sine
    out_ref[:, HEAD:WIDE] = total[:, HEAD:] + bias_ref[1:2, :].astype(jnp.float32)


def project(own, blocks, places, weight_rows, turn, up, begun, bias):
    return pl.pallas_call(
        functools.partial(project_kernel, places),
        out_shape=jax.ShapeDtypeStruct((ROWS, 2 * WIDE + HEAD), jnp.float32),
        in_specs=smem(1) + hbm(5) + vmem(len(places)),
        out_specs=vmem(1)[0],
        scratch_shapes=[
            pltpu.VMEM((BUFFERS, 2 * BLOCK, HEAD), jnp.bfloat16),
            pltpu.VMEM((ROWS, BLOCK), jnp.bfloat16),
            pltpu.VMEM((ROWS, HEAD), jnp.float32),
            pltpu.VMEM((2 * RANK, HEAD), jnp.bfloat16),
            pltpu.VMEM((ROWS, WIDE), jnp.float32),
            pltpu.SemaphoreType.DMA((BUFFERS,)),
            pltpu.SemaphoreType.DMA((4,)),
        ],
        compiler_params=pltpu.CompilerParams(vmem_limit_bytes=VMEM_LIMIT),
        name="project",
    )(
        own,
        weight_rows,
        in_hbm(blocks[0]),
        in_hbm(turn),
        in_hbm(up),
        in_hbm(begun),
        in_hbm(bias),
        *[blocks[place] for place in places if place],
    )


def finish_kernel(made_ref, low_ref, slot_ref, out_ref, placed):
    updates = []
    for side in range(2):
        ranks = slice(side * RANK, (side + 1) * RANK)
        updates.append(
            adapter_scale
            * lax.dot_general(
                low_ref[ranks, :],
                made_ref[ranks, 2 * WIDE :].astype(jnp.bfloat16),
                (((0,), (0,)), ((), ())),
                preferred_element_type=jnp.float32,
            )
        )
    keys = updates[0]
    cosine, sine = made_ref[:, WIDE : WIDE + HEAD], made_ref[:, WIDE + HEAD : 2 * WIDE]
    keys = keys * cosine + pltpu.roll(keys, HEAD // 2, 1) * sine
    rows = made_ref[:, :WIDE] + jnp.concatenate([keys, updates[1]], axis=1)
    rows = rows.astype(jnp.bfloat16)
    slots = lax.broadcasted_iota(jnp.int32, (GROUPS * CAP, ROWS), 0)
    chosen = jnp.where(slots == slot_ref[...], 1.0, 0.0).astype(jnp.bfloat16)
    slot_rows = jnp.dot(chosen, rows, preferred_element_type=jnp.float32)
    for side in range(2):
        placed[pl.ds(side, GROUPS * CAP, stride=2), :] = slot_rows[
            :, side * HEAD : (side + 1) * HEAD
        ]
    out_ref[...] = placed[...].astype(jnp.bfloat16)


def finish(made, low, slots):
    return pl.pallas_call(
        finish_kernel,
        out_shape=jax.ShapeDtypeStruct((2 * GROUPS * CAP, HEAD), jnp.bfloat16),
        in_specs=vmem(3),
        out_specs=vmem(1)[0],
        scratch_shapes=[pltpu.VMEM((2 * GROUPS * CAP, HEAD), jnp.float32)],
        compiler_params=pltpu.CompilerParams(vmem_limit_bytes=VMEM_LIMIT),
        name="finish",
    )(made, low, slots)


def slots_kernel(routes_ref, slot_ref):
    target = routes_ref[...]
    later = jnp.broadcast_to(target.astype(jnp.float32), (ROWS, ROWS))
    below = lax.broadcasted_iota(jnp.int32, (ROWS, ROWS), 0)
    after = lax.broadcasted_iota(jnp.int32, (ROWS, ROWS), 1)
    same = jnp.where((later.T == later) & (below < after), 1, 0)
    slot_ref[...] = target * CAP + jnp.sum(same, axis=0, keepdims=True)


def slots_of(routes):
    return pl.pallas_call(
        slots_kernel,
        out_shape=jax.ShapeDtypeStruct((1, ROWS), jnp.int32),
        in_specs=vmem(1),
        out_specs=vmem(1)[0],
        cost_estimate=BESIDE,
        compiler_params=pltpu.CompilerParams(vmem_limit_bytes=VMEM_LIMIT),
        name="slots",
    )(in_hbm(routes.reshape(1, ROWS)))


def body(tokens, weight, bias, down_blocks, up_blocks, lookup, lengths, routes):
    lane = lax.axis_index("tensor")
    y, x = lane // X, lane % X
    core = lax.axis_index("rollout") % 2
    own = jnp.stack([y, x, core]).astype(jnp.int32)

    weight_rows = in_hbm(weight.reshape(2 * MODEL, HEAD))

    def along_x(block, hop):
        return lax.ppermute(block, "tensor", X_HOP[hop])

    def across_y(block):
        return lax.ppermute(block, "tensor", Y_PARTNER)

    met = across_y(tokens)
    far_x, next_x, last_x = along_x(tokens, 2), along_x(tokens, 1), along_x(tokens, 3)

    sent, turn = share(
        own, lengths, down_blocks.reshape(2 * 128, RANK), up_blocks.reshape(4, HEAD)
    )
    near = lax.all_to_all(sent, "rollout", 0, 0, tiled=True, axis_index_groups=SAME_CORE)
    far = lax.ppermute(near, "rollout", SIBLING)

    met, far_x = lax.optimization_barrier((met, far_x))
    met_far = across_y(far_x)
    met_next, met_last = along_x(met, 1), along_x(met, 3)
    blocks = [tokens, next_x, far_x, last_x, met, met_next, met_far, met_last]
    early, late = (1, 2, 3, 4, 0), (6, 5, 7)
    down, begun, up = low_begin(lookup, own, near, far, blocks, early)
    slots = slots_of(routes)
    started = begin(own, blocks, (1, 2), weight_rows)
    met_far, met_next, met_last, down, begun, up, slots, started = lax.optimization_barrier(
        (met_far, met_next, met_last, down, begun, up, slots, started)
    )
    blocks[5:] = [met_next, met_far, met_last]
    low = low_end(own, down, begun, blocks, late)
    low_all = lax.all_to_all(low, "tensor", 0, 0, tiled=True).reshape(2 * RANK, ROWS)
    made = project(own, blocks, (3, 4, 5, 6, 7, 0), weight_rows, turn, up, started, bias)
    outgoing = finish(made, low_all, slots)
    arrived = lax.all_to_all(outgoing, "rollout", 0, 0, tiled=True)
    return arrived.reshape(GROUPS * CAP, 2, HEAD)


def solution(mesh):
    in_specs = (
        P("rollout", "tensor"),
        P(None, None, "tensor"),
        P(None, "tensor"),
        P("rollout", None, None),
        P(None, "rollout", "tensor"),
        P(),
        P("rollout", None),
        P("rollout"),
    )
    out_specs = P("rollout", None, "tensor")
    return jax.shard_map(body, mesh=mesh, in_specs=in_specs, out_specs=out_specs, check_vma=False)
```

time: 113 us -> 97 us (0.86)
  waiting for transfers between devices: 19.4 us -> 3.24 us
  between operations: 13.7 us -> 0.21 us
  Pallas kernels: 4.11 us -> 17.5 us
  starting transfers between devices: 34.8 us -> 47.7 us
  local copies, waits for them, and re-layouts: 10.5 us -> 0.7 us
  other arithmetic: 4.74 us -> 0.08 us
  blocking collectives: 25.2 us -> 26.8 us
    all_to_all x2, waiting for transfers between devices: 17.5 us -> 3.22 us  [the longest x1 2.68 us: body(): lax.all_to_all(sent, 'rollout', 0, 0, tiled=True, axis_index_groups=SAME_...]
    pallas_call x5 -> x7, Pallas kernels: 4.11 us -> 17.5 us  [the longest x1 4.88 us: project(): pl.pallas_call(functools.partial(project_kernel, places), out_shape=jax.S...]
    ppermute x3 -> x7, starting transfers between devices: 14.4 us -> 22.9 us  [the longest x5 15.8 us: along_x(): return lax.ppermute(block, 'tensor', X_HOP[hop])]
    dynamic_slice x2 -> x0, local copies, waits for them, and re-layouts: 5.09 us -> none  [the longest x1 3.25 us: body(): lax.dynamic_slice_in_dim(weight, y * HALF, HALF, 0).reshape(HALF, WIDE)]
    ppermute x1, starting transfers between devices: 2.15 us -> 5.92 us  [body(): far = lax.ppermute(near, 'rollout', SIBLING)]
    select_n x1 -> x0, other arithmetic: 2.8 us -> none  [body(): jnp.where(core == 0, jnp.concatenate([weight_near, weight_far], 0), jnp.c...]
    unnamed x23 -> x1, local copies, waits for them, and re-layouts: 2.86 us -> 0.7 us
    broadcast_in_dim x4 -> x0, local copies, waits for them, and re-layouts: 1.67 us -> none  [the longest x1 0.94 us: body(): jnp.broadcast_to(sent[None], (GROUPS // 2, 2, SENT, HEAD))]
  transfers between devices with their start and end apart: 7 -> 10, of which waited for: 2 -> 2; matrix products, arithmetic and copies ran while one was open for 11% -> 0% of each run, Pallas kernels for 3% -> 16%
where the time goes in v3:
time: 97 us; the launch traced here: 96.2 us
  starting transfers between devices  47.7 us (49%)
  blocking collectives  26.8 us (28%)
  Pallas kernels  17.5 us (18%)
  waiting for transfers between devices  3.24 us (3%)
    all_to_all x1, blocking collectives, body(): arrived = lax.all_to_all(outgoing, 'rollout', 0, 0, tiled=True)  26.8 us
    ppermute x5, starting transfers between devices, along_x(): return lax.ppermute(block, 'tensor', X_HOP[hop])  15.8 us
    all_to_all x1, starting transfers between devices, body(): lax.all_to_all(sent, 'rollout', 0, 0, tiled=True, axis_index_groups=SAME_...  14.8 us
    ppermute x2, starting transfers between devices, across_y(): return lax.ppermute(block, 'tensor', Y_PARTNER)  7.01 us
    ppermute x1, starting transfers between devices, body(): far = lax.ppermute(near, 'rollout', SIBLING)  5.92 us
    pallas_call x1, Pallas kernels, project(): pl.pallas_call(functools.partial(project_kernel, places), out_shape=jax.S...  4.88 us
    all_to_all x1, starting transfers between devices, body(): lax.all_to_all(low, 'tensor', 0, 0, tiled=True).reshape(2 * RANK, ROWS)  4.13 us
    pallas_call x1, Pallas kernels, begin(): pl.pallas_call(functools.partial(begin_kernel, places), out_shape=pltpu.H...  3.6 us
  transfers between devices with their start and end apart: 10, of which 2 were waited for; matrix products, arithmetic and copies ran while one was open for 0% of the time, Pallas kernels for 16%

profile of v3, /device:TPU:1, one launch (start us, length us, event | category | flops | bytes accessed | tf_op | source)
XLA Modules:
  0.0 96.2 jit_solution(7369865820215406590)
XLA Ops:
  0.0 4.0 %collective-permute-start = (bf16[256,1024]{1,0:T(8,128)(2,1)}, bf16[256,1024]{1,0:T(8,128)(2,1)S(1)}, u32[]{:S(2)}, u32[]{:S(2)}) collective-permute-start(bf16[256,1024]{1,0:T(8,128)(2,1)} %tokens_ref.3), channel_id=1, source_target_pairs={{0,4},{1,5},{2,6},{3,7},{4,0},{5,1},{6,2},{7,3},{8,12},{9,13},{10,... | collective-permute-start | bytes 1572872 | tf_op jit(solution)/shard_map/ppermute | solution.py:388
  4.0 4.7 %collective-permute-start.1 = (bf16[256,1024]{1,0:T(8,128)(2,1)}, bf16[256,1024]{1,0:T(8,128)(2,1)}, u32[]{:S(2)}, u32[]{:S(2)}) collective-permute-start(bf16[256,1024]{1,0:T(8,128)(2,1)} %tokens_ref.3), channel_id=1, source_target_pairs={{0,2},{1,3},{2,0},{3,1},{4,6},{5,7},{6,4},{7,5},{8,10},{9,11},{10,... | collective-permute-start | bytes 1572872 | tf_op jit(solution)/shard_map/ppermute | solution.py:385
  8.7 2.8 %collective-permute-start.6 = (bf16[256,1024]{1,0:T(8,128)(2,1)}, bf16[256,1024]{1,0:T(8,128)(2,1)}, u32[]{:S(2)}, u32[]{:S(2)}) collective-permute-start(bf16[256,1024]{1,0:T(8,128)(2,1)} %tokens_ref.3), channel_id=1, source_target_pairs={{0,3},{1,0},{2,1},{3,2},{4,7},{5,4},{6,5},{7,6},{8,11},{9,8},{10,9... | collective-permute-start | bytes 1572872 | tf_op jit(solution)/shard_map/ppermute | solution.py:385
  11.5 2.5 %collective-permute-start.7 = (bf16[256,1024]{1,0:T(8,128)(2,1)}, bf16[256,1024]{1,0:T(8,128)(2,1)S(1)}, u32[]{:S(2)}, u32[]{:S(2)}) collective-permute-start(bf16[256,1024]{1,0:T(8,128)(2,1)} %tokens_ref.3), channel_id=1, source_target_pairs={{0,1},{1,2},{2,3},{3,0},{4,5},{5,6},{6,7},{7,4},{8,9},{9,10},{10,1... | collective-permute-start | bytes 1572872 | tf_op jit(solution)/shard_map/ppermute | solution.py:385
  14.0 0.1 pad_add_fusion.own_ref
  14.1 2.4 %share.1 = (bf16[32,40,128]{2,1,0:T(8,128)(2,1)}, f32[256,128]{1,0:T(8,128)}) custom-call(s32[3]{0:T(128)S(1)} %pad_add_fusion.own_ref, s32[1,8]{1,0:T(1,128)} %lengths_ref.1, f32[1,128]{1,0:T(1,128)} %constant.45.clone.rate_ref, bf16[256,128]{1,0:T(8,128)(2,1)} %bitcast.15, bf16[4,128]{1,0:T(4,128)(2,1)} %bitcast.16), custom_call_target="tpu_custom_call" | custom-call | tf_op jit(solution)/shard_map/share/pallas_call | solution.py:99
  16.5 14.8 %all-to-all-start = ((bf16[32,40,128]{2,1,0:T(8,128)(2,1)}), bf16[32,40,128]{2,1,0:T(8,128)(2,1)S(1)}, u32[]{:S(2)}, u32[]{:S(2)}) async-start(bf16[32,40,128]{2,1,0:T(8,128)(2,1)} %get-tuple-element.23), calls=%async_computation | async-start | bytes 655360 | tf_op jit(solution)/shard_map/all_to_all | solution.py:396
  31.3 0.8 slots.1.slot_ref
  32.1 0.0 collective-permute-done.refs_3_.refs_1_
  32.1 0.0 collective-permute-done.1.refs_1_
  32.1 4.0 %collective-permute-start.3 = (bf16[256,1024]{1,0:T(8,128)(2,1)S(1)}, bf16[256,1024]{1,0:T(8,128)(2,1)S(1)}, u32[]{:S(2)}, u32[]{:S(2)}) collective-permute-start(bf16[256,1024]{1,0:T(8,128)(2,1)S(1)} %collective-permute-done.refs_3_.refs_1_), channel_id=1, source_target_pairs={{0,3},{1,0},{2,1},{3,2},{4,7},{5,4},{6,5},{7,6},{8,11},{9,8},{10,9... | collective-permute-start | bytes 1572872 | tf_op jit(solution)/shard_map/ppermute | solution.py:385
  36.1 1.9 %collective-permute-start.4 = (bf16[256,1024]{1,0:T(8,128)(2,1)S(1)}, bf16[256,1024]{1,0:T(8,128)(2,1)S(1)}, u32[]{:S(2)}, u32[]{:S(2)}) collective-permute-start(bf16[256,1024]{1,0:T(8,128)(2,1)S(1)} %collective-permute-done.refs_3_.refs_1_), channel_id=1, source_target_pairs={{0,1},{1,2},{2,3},{3,0},{4,5},{5,6},{6,7},{7,4},{8,9},{9,10},{10,1... | collective-permute-start | bytes 1572872 | tf_op jit(solution)/shard_map/ppermute | solution.py:385
  38.1 3.0 %collective-permute-start.2 = (bf16[256,1024]{1,0:T(8,128)(2,1)}, bf16[256,1024]{1,0:T(8,128)(2,1)S(1)}, u32[]{:S(2)}, u32[]{:S(2)}) collective-permute-start(bf16[256,1024]{1,0:T(8,128)(2,1)} %collective-permute-done.1.refs_1_), channel_id=1, source_target_pairs={{0,4},{1,5},{2,6},{3,7},{4,0},{5,1},{6,2},{7,3},{8,12},{9,13},{10,... | collective-permute-start | bytes 1572872 | tf_op jit(solution)/shard_map/ppermute | solution.py:388
  41.1 0.0 collective-permute-done.6.refs_0_
  41.1 2.7 %all-to-all-done.near_ref = bf16[32,40,128]{2,1,0:T(8,128)(2,1)S(1)} async-done(((bf16[32,40,128]{2,1,0:T(8,128)(2,1)}), bf16[32,40,128]{2,1,0:T(8,128)(2,1)S(1)}, u32[]{:S(2)}, u32[]{:S(2)}) %all-to-all-start) | async-done | bytes 327712 | tf_op jit(solution)/shard_map/all_to_all | solution.py:396
  43.8 5.9 %collective-permute-start.5 = (bf16[32,40,128]{2,1,0:T(8,128)(2,1)S(1)}, bf16[32,40,128]{2,1,0:T(8,128)(2,1)S(1)}, u32[]{:S(2)}, u32[]{:S(2)}) collective-permute-start(bf16[32,40,128]{2,1,0:T(8,128)(2,1)S(1)} %all-to-all-done.near_ref), channel_id=1, source_target_pairs={{0,8},{8,0},{16,24},{24,16},{32,40},{40,32},{48,56},{56,48},{64,72... | collective-permute-start | bytes 983048 | tf_op jit(solution)/shard_map/ppermute | solution.py:397
  49.7 3.6 %begin.1.begun_ref = f32[256,256]{1,0:T(8,128)} custom-call(s32[3]{0:T(128)S(1)} %pad_add_fusion.own_ref, bf16[16384,128]{1,0:T(8,128)(2,1)} %bitcast.12, bf16[256,1024]{1,0:T(8,128)(2,1)} %collective-permute-done.6.refs_0_, bf16[256,1024]{1,0:T(8,128)(2,1)} %collective-permute-done.1.refs_1_), custom_call_target="tpu_custom_call" | custom-call | flops 8000000000 | tf_op jit(solution)/shard_map/begin/pallas_call | solution.py:240
  53.3 0.0 collective-permute-done.7.refs_2_.refs_0_
  53.3 0.0 collective-permute-done.5.far_ref
  53.3 3.5 %low_begin.1 = (bf16[32,8192]{1,0:T(8,128)(2,1)S(1)}, f32[256,32]{1,0:T(8,128)S(1)}, bf16[256,128]{1,0:T(8,128)(2,1)}) custom-call(s32[64]{0:T(128)} %lookup_ref.1, s32[3]{0:T(128)S(1)} %pad_add_fusion.own_ref, bf16[32,40,128]{2,1,0:T(8,128)(2,1)S(1)} %all-to-all-done.near_ref, bf16[32,40,128]{2,1,0:T(8,128)(2,1)S(1)} %collective-permute-done.5.far_ref, ...), custom_call_target="tpu_custom_call" | custom-call | tf_op jit(solution)/shard_map/low_begin/pallas_call | solution.py:157
  56.9 0.0 collective-permute-done.3.refs_2_.refs_1_
  56.9 0.0 collective-permute-done.4.refs_4_.refs_2_
  56.9 0.0 collective-permute-done.2.refs_3_.refs_0_
  56.9 1.8 %low_end.1 = bf16[8,32,256]{2,1,0:T(8,128)(2,1)} custom-call(s32[3]{0:T(128)S(1)} %pad_add_fusion.own_ref, bf16[32,8192]{1,0:T(8,128)(2,1)S(1)} %get-tuple-element.32.down_ref, f32[256,32]{1,0:T(8,128)S(1)} %get-tuple-element.33.begun_ref, bf16[256,1024]{1,0:T(8,128)(2,1)S(1)} %collective-permute-done.2.refs_3_.refs_0_, ...), custom_call_target="tpu_custom_call" | custom-call | tf_op jit(solution)/shard_map/low_end/pallas_call | solution.py:192
  58.7 4.1 %all-to-all-start.1 = ((bf16[8,32,256]{2,1,0:T(8,128)(2,1)}), bf16[8,32,256]{2,1,0:T(8,128)(2,1)S(1)}, u32[]{:S(2)}, u32[]{:S(2)}) async-start(bf16[8,32,256]{2,1,0:T(8,128)(2,1)} %low_end.1), calls=%async_computation.1 | async-start | bytes 262144 | tf_op jit(solution)/shard_map/all_to_all | solution.py:412
  62.8 4.9 %project.1.made_ref = f32[256,640]{1,0:T(8,128)S(1)} custom-call(s32[3]{0:T(128)S(1)} %pad_add_fusion.own_ref, bf16[16384,128]{1,0:T(8,128)(2,1)} %bitcast.13, bf16[256,1024]{1,0:T(8,128)(2,1)} %tokens_ref.3, f32[256,128]{1,0:T(8,128)} %get-tuple-element.20.turn_ref, bf16[256,128]{1,0:T(8,128)(2,1)} %get-tuple-element.27.up_ref, f32[256,256]{1,0:T(8,128)} %begin.1.begun_ref, ...), custom_call_target="tpu_custom_call" | custom-call | tf_op jit(solution)/shard_map/project/pallas_call | solution.py:287
  67.7 0.5 all-to-all-done.1
  68.3 0.5 finish.1
  68.8 26.8 %all_to_all.19 = bf16[64,16,128]{2,1,0:T(8,128)(2,1)S(1)} all-to-all(bf16[64,16,128]{2,1,0:T(8,128)(2,1)S(1)} %bitcast.10), channel_id=1, replica_groups=mesh['rollout'=64,'tensor'=8] {'rollout'}, dimensions={0} | all-to-all | bytes 524288 | tf_op jit(solution)/shard_map/all_to_all | solution.py:415
  95.5 0.7 copy.11
Async XLA Ops:
  0.0 32.1 %collective-permute-start = (bf16[256,1024]{1,0:T(8,128)(2,1)}, bf16[256,1024]{1,0:T(8,128)(2,1)S(1)}, u32[]{:S(2)}, u32[]{:S(2)}) collective-permute-start(bf16[256,1024]{1,0:T(8,128)(2,1)} %tokens_ref.3), channel_id=1, source_target_pairs={{0,4},{1,5},{2,6},{3,7},{4,0},{5,1},{6,2},{7,3},{8,12},{9,13},{10,... | collective-permute-start | bytes 1572872 | tf_op jit(solution)/shard_map/ppermute | solution.py:388
  4.0 28.1 %collective-permute-start.1 = (bf16[256,1024]{1,0:T(8,128)(2,1)}, bf16[256,1024]{1,0:T(8,128)(2,1)}, u32[]{:S(2)}, u32[]{:S(2)}) collective-permute-start(bf16[256,1024]{1,0:T(8,128)(2,1)} %tokens_ref.3), channel_id=1, source_target_pairs={{0,2},{1,3},{2,0},{3,1},{4,6},{5,7},{6,4},{7,5},{8,10},{9,11},{10,... | collective-permute-start | bytes 1572872 | tf_op jit(solution)/shard_map/ppermute | solution.py:385
  8.7 32.4 %collective-permute-start.6 = (bf16[256,1024]{1,0:T(8,128)(2,1)}, bf16[256,1024]{1,0:T(8,128)(2,1)}, u32[]{:S(2)}, u32[]{:S(2)}) collective-permute-start(bf16[256,1024]{1,0:T(8,128)(2,1)} %tokens_ref.3), channel_id=1, source_target_pairs={{0,3},{1,0},{2,1},{3,2},{4,7},{5,4},{6,5},{7,6},{8,11},{9,8},{10,9... | collective-permute-start | bytes 1572872 | tf_op jit(solution)/shard_map/ppermute | solution.py:385
  11.5 41.8 %collective-permute-start.7 = (bf16[256,1024]{1,0:T(8,128)(2,1)}, bf16[256,1024]{1,0:T(8,128)(2,1)S(1)}, u32[]{:S(2)}, u32[]{:S(2)}) collective-permute-start(bf16[256,1024]{1,0:T(8,128)(2,1)} %tokens_ref.3), channel_id=1, source_target_pairs={{0,1},{1,2},{2,3},{3,0},{4,5},{5,6},{6,7},{7,4},{8,9},{9,10},{10,1... | collective-permute-start | bytes 1572872 | tf_op jit(solution)/shard_map/ppermute | solution.py:385
  16.5 27.2 %all-to-all-start = ((bf16[32,40,128]{2,1,0:T(8,128)(2,1)}), bf16[32,40,128]{2,1,0:T(8,128)(2,1)S(1)}, u32[]{:S(2)}, u32[]{:S(2)}) async-start(bf16[32,40,128]{2,1,0:T(8,128)(2,1)} %get-tuple-element.23), calls=%async_computation | async-start | bytes 655360 | tf_op jit(solution)/shard_map/all_to_all | solution.py:396
  32.1 24.7 %collective-permute-start.3 = (bf16[256,1024]{1,0:T(8,128)(2,1)S(1)}, bf16[256,1024]{1,0:T(8,128)(2,1)S(1)}, u32[]{:S(2)}, u32[]{:S(2)}) collective-permute-start(bf16[256,1024]{1,0:T(8,128)(2,1)S(1)} %collective-permute-done.refs_3_.refs_1_), channel_id=1, source_target_pairs={{0,3},{1,0},{2,1},{3,2},{4,7},{5,4},{6,5},{7,6},{8,11},{9,8},{10,9... | collective-permute-start | bytes 1572872 | tf_op jit(solution)/shard_map/ppermute | solution.py:385
  36.1 20.7 %collective-permute-start.4 = (bf16[256,1024]{1,0:T(8,128)(2,1)S(1)}, bf16[256,1024]{1,0:T(8,128)(2,1)S(1)}, u32[]{:S(2)}, u32[]{:S(2)}) collective-permute-start(bf16[256,1024]{1,0:T(8,128)(2,1)S(1)} %collective-permute-done.refs_3_.refs_1_), channel_id=1, source_target_pairs={{0,1},{1,2},{2,3},{3,0},{4,5},{5,6},{6,7},{7,4},{8,9},{9,10},{10,1... | collective-permute-start | bytes 1572872 | tf_op jit(solution)/shard_map/ppermute | solution.py:385
  38.1 18.8 %collective-permute-start.2 = (bf16[256,1024]{1,0:T(8,128)(2,1)}, bf16[256,1024]{1,0:T(8,128)(2,1)S(1)}, u32[]{:S(2)}, u32[]{:S(2)}) collective-permute-start(bf16[256,1024]{1,0:T(8,128)(2,1)} %collective-permute-done.1.refs_1_), channel_id=1, source_target_pairs={{0,4},{1,5},{2,6},{3,7},{4,0},{5,1},{6,2},{7,3},{8,12},{9,13},{10,... | collective-permute-start | bytes 1572872 | tf_op jit(solution)/shard_map/ppermute | solution.py:388
  43.8 9.6 %collective-permute-start.5 = (bf16[32,40,128]{2,1,0:T(8,128)(2,1)S(1)}, bf16[32,40,128]{2,1,0:T(8,128)(2,1)S(1)}, u32[]{:S(2)}, u32[]{:S(2)}) collective-permute-start(bf16[32,40,128]{2,1,0:T(8,128)(2,1)S(1)} %all-to-all-done.near_ref), channel_id=1, source_target_pairs={{0,8},{8,0},{16,24},{24,16},{32,40},{40,32},{48,56},{56,48},{64,72... | collective-permute-start | bytes 983048 | tf_op jit(solution)/shard_map/ppermute | solution.py:397
  58.7 9.6 %all-to-all-start.1 = ((bf16[8,32,256]{2,1,0:T(8,128)(2,1)}), bf16[8,32,256]{2,1,0:T(8,128)(2,1)S(1)}, u32[]{:S(2)}, u32[]{:S(2)}) async-start(bf16[8,32,256]{2,1,0:T(8,128)(2,1)} %low_end.1), calls=%async_computation.1 | async-start | bytes 262144 | tf_op jit(solution)/shard_map/all_to_all | solution.py:412

commit v4 on v3

--- a/solution.py
+++ b/solution.py
@@ -33,6 +33,8 @@
 
 VMEM_LIMIT = 16 * 1024 * 1024
 BUFFERS = 4
+FIRST = (1, 2, 0)
+REST = (3, 4, 6, 5, 7)
 
 BESIDE = pl.CostEstimate(flops=8 * 10**9, bytes_accessed=0, transcendentals=0)
 
@@ -120,6 +122,23 @@
     return (own_ref[0] + place // X) % 2 * X + (own_ref[1] + place) % X
 
 
+def inverse_kernel(lookup_ref, inverse_ref):
+    for owner in range(GROUPS):
+        inverse_ref[lookup_ref[owner]] = owner
+
+
+def inverse_of(lookup):
+    return pl.pallas_call(
+        inverse_kernel,
+        out_shape=pltpu.HBM((GROUPS,), jnp.int32),
+        in_specs=smem(1),
+        out_specs=smem(1)[0],
+        cost_estimate=BESIDE,
+        compiler_params=pltpu.CompilerParams(vmem_limit_bytes=VMEM_LIMIT),
+        name="inverse",
+    )(in_hbm(lookup))
+
+
 def low_part(own_ref, blocks, down_ref, places):
     total = None
     for block, place in zip(blocks, places):
@@ -132,71 +151,6 @@
         )
         total = part if total is None else total + part
     return total
-
-
-def low_begin_kernel(places, lookup_ref, own_ref, near_ref, far_ref, tokens_ref, *refs):
-    down_ref, begun_ref, up_ref, inverse, up_rows, held, done = refs[len(places) - 1 :]
-    copy = pltpu.make_async_copy(tokens_ref, held, done)
-    copy.start()
-    core = own_ref[2]
-    for owner in range(GROUPS):
-        inverse[lookup_ref[owner]] = owner
-    for shard in range(GROUPS):
-        owner = inverse[shard]
-        rows = jnp.where(owner % 2 == core, near_ref[owner // 2], far_ref[owner // 2])
-        down_ref[:, shard * 128 : (shard + 1) * 128] = rows[0:SLICE]
-        rows = rows[SLICE:SENT].astype(jnp.float32)
-        up_rows[2 * shard : 2 * shard + 2, :] = rows[0:2]
-        up_rows[RANK + 2 * shard : RANK + 2 * shard + 2, :] = rows[2:4]
-    up_ref[...] = up_rows[...].astype(jnp.bfloat16)
-    copy.wait()
-    begun_ref[...] = low_part(own_ref, [*refs[: len(places) - 1], held], down_ref, places)
-
-
-def low_begin(lookup, own, near, far, blocks, places):
-    return pl.pallas_call(
-        functools.partial(low_begin_kernel, places),
-        out_shape=(
-            jax.ShapeDtypeStruct((SLICE, MODEL), jnp.bfloat16),
-            jax.ShapeDtypeStruct((ROWS, SLICE), jnp.float32),
-            pltpu.HBM((2 * RANK, HEAD), jnp.bfloat16),
-        ),
-        in_specs=smem(2) + vmem(2) + hbm(1) + vmem(len(places) - 1),
-        out_specs=tuple(vmem(3)),
-        scratch_shapes=[
-            pltpu.SMEM((GROUPS,), jnp.int32),
-            pltpu.VMEM((2 * RANK, HEAD), jnp.float32),
-            pltpu.VMEM((ROWS, BLOCK), jnp.bfloat16),
-            pltpu.SemaphoreType.DMA,
-        ],
-        compiler_params=pltpu.CompilerParams(vmem_limit_bytes=VMEM_LIMIT),
-        name="low_begin",
-    )(
-        in_hbm(lookup),
-        own,
-        near,
-        far,
-        in_hbm(blocks[0]),
-        *[blocks[place] for place in places if place],
-    )
-
-
-def low_end_kernel(places, own_ref, down_ref, begun_ref, *refs):
-    total = begun_ref[...] + low_part(own_ref, refs[:-1], down_ref, places)
-    low = total.T.astype(jnp.bfloat16)
-    for target in range(SHARE):
-        refs[-1][target] = low
-
-
-def low_end(own, down, begun, blocks, places):
-    return pl.pallas_call(
-        functools.partial(low_end_kernel, places),
-        out_shape=pltpu.HBM((SHARE, SLICE, ROWS), jnp.bfloat16),
-        in_specs=smem(1) + vmem(2 + len(places)),
-        out_specs=vmem(1)[0],
-        compiler_params=pltpu.CompilerParams(vmem_limit_bytes=VMEM_LIMIT),
-        name="low_end",
-    )(own, down, begun, *[blocks[place] for place in places])
 
 
 def weight_copies(own_ref, weight_ref, weights, done, places):
@@ -228,41 +182,91 @@
     return total
 
 
-def begin_kernel(places, own_ref, weight_ref, *refs):
-    out_ref, weights, done = refs[len(places) :]
-    copies = weight_copies(own_ref, weight_ref, weights, done, places)
-    for copy in copies[:BUFFERS]:
-        copy.start()
-    out_ref[...] = project_blocks(copies, refs[: len(places)], weights)
-
-
-def begin(own, blocks, places, weight_rows):
-    return pl.pallas_call(
-        functools.partial(begin_kernel, places),
-        out_shape=pltpu.HBM((ROWS, WIDE), jnp.float32),
-        in_specs=smem(1) + hbm(1) + vmem(len(places)),
-        out_specs=vmem(1)[0],
+def low_begin_kernel(
+    places, inverse_ref, own_ref, near_ref, far_ref, weight_ref, tokens_ref, *refs
+):
+    down_ref, begun_ref, up_ref, base_ref, up_rows, held, weights, done, weight_done = refs[
+        len(places) - 1 :
+    ]
+    copies = weight_copies(own_ref, weight_ref, weights, weight_done, FIRST)
+    for weight_copy in copies[:BUFFERS]:
+        weight_copy.start()
+    copy = pltpu.make_async_copy(tokens_ref, held, done)
+    copy.start()
+    core = own_ref[2]
+    for shard in range(GROUPS):
+        owner = inverse_ref[shard]
+        rows = jnp.where(owner % 2 == core, near_ref[owner // 2], far_ref[owner // 2])
+        down_ref[:, shard * 128 : (shard + 1) * 128] = rows[0:SLICE]
+        rows = rows[SLICE:SENT].astype(jnp.float32)
+        up_rows[2 * shard : 2 * shard + 2, :] = rows[0:2]
+        up_rows[RANK + 2 * shard : RANK + 2 * shard + 2, :] = rows[2:4]
+    up_ref[...] = up_rows[...].astype(jnp.bfloat16)
+    copy.wait()
+    blocks = [*refs[: len(places) - 1], held]
+    begun_ref[...] = low_part(own_ref, blocks, down_ref, places)
+    firsts = [blocks[places.index(place)] for place in FIRST]
+    base_ref[...] = project_blocks(copies, firsts, weights)
+
+
+def low_begin(inverse, own, near, far, weight_rows, blocks, places):
+    return pl.pallas_call(
+        functools.partial(low_begin_kernel, places),
+        out_shape=(
+            jax.ShapeDtypeStruct((SLICE, MODEL), jnp.bfloat16),
+            jax.ShapeDtypeStruct((ROWS, SLICE), jnp.float32),
+            pltpu.HBM((2 * RANK, HEAD), jnp.bfloat16),
+            pltpu.HBM((ROWS, WIDE), jnp.float32),
+        ),
+        in_specs=smem(2) + vmem(2) + hbm(2) + vmem(len(places) - 1),
+        out_specs=tuple(vmem(4)),
         scratch_shapes=[
+            pltpu.VMEM((2 * RANK, HEAD), jnp.float32),
+            pltpu.VMEM((ROWS, BLOCK), jnp.bfloat16),
             pltpu.VMEM((BUFFERS, 2 * BLOCK, HEAD), jnp.bfloat16),
+            pltpu.SemaphoreType.DMA,
             pltpu.SemaphoreType.DMA((BUFFERS,)),
         ],
-        cost_estimate=BESIDE,
-        compiler_params=pltpu.CompilerParams(vmem_limit_bytes=VMEM_LIMIT),
-        name="begin",
-    )(own, weight_rows, *[blocks[place] for place in places])
-
-
-def project_kernel(
-    places, own_ref, weight_ref, tokens_ref, turn_ref, up_ref, begun_ref, bias_ref, *refs
-):
-    out_ref, weights, tokens, turn, up, begun, weight_done, done = refs[len(places) - 1 :]
+        compiler_params=pltpu.CompilerParams(vmem_limit_bytes=VMEM_LIMIT),
+        name="low_begin",
+    )(
+        in_hbm(inverse),
+        own,
+        near,
+        far,
+        weight_rows,
+        in_hbm(blocks[0]),
+        *[blocks[place] for place in places if place],
+    )
+
+
+def low_end_kernel(places, own_ref, down_ref, begun_ref, *refs):
+    total = begun_ref[...] + low_part(own_ref, refs[:-1], down_ref, places)
+    low = total.T.astype(jnp.bfloat16)
+    for target in range(SHARE):
+        refs[-1][target] = low
+
+
+def low_end(own, down, begun, blocks, places):
+    return pl.pallas_call(
+        functools.partial(low_end_kernel, places),
+        out_shape=pltpu.HBM((SHARE, SLICE, ROWS), jnp.bfloat16),
+        in_specs=smem(1) + vmem(2 + len(places)),
+        out_specs=vmem(1)[0],
+        compiler_params=pltpu.CompilerParams(vmem_limit_bytes=VMEM_LIMIT),
+        name="low_end",
+    )(own, down, begun, *[blocks[place] for place in places])
+
+
+def project_kernel(places, own_ref, weight_ref, turn_ref, up_ref, begun_ref, bias_ref, *refs):
+    out_ref, weights, turn, up, begun, weight_done, done = refs[len(places) :]
     copies = weight_copies(own_ref, weight_ref, weights, weight_done, places)
     for copy in copies[:BUFFERS]:
         copy.start()
     small = [
         pltpu.make_async_copy(from_ref, to_ref, done.at[at])
         for at, (from_ref, to_ref) in enumerate(
-            [(turn_ref, turn), (up_ref, up), (begun_ref, begun), (tokens_ref, tokens)]
+            [(turn_ref, turn), (up_ref, up), (begun_ref, begun)]
         )
     ]
     for copy in small:
@@ -277,7 +281,7 @@
     out_ref[:, WIDE : WIDE + HEAD] = cosine
     out_ref[:, WIDE + HEAD : 2 * WIDE] = sine
     out_ref[:, 2 * WIDE :] = up[...].astype(jnp.float32)
-    total = begun[...] + project_blocks(copies, [*refs[: len(places) - 1], tokens], weights)
+    total = begun[...] + project_blocks(copies, refs[: len(places)], weights)
     keys = total[:, :HEAD] + bias_ref[0:1, :].astype(jnp.float32)
     out_ref[:, :HEAD] = keys * cosine + pltpu.roll(keys, HEAD // 2, 1) * sine
     out_ref[:, HEAD:WIDE] = total[:, HEAD:] + bias_ref[1:2, :].astype(jnp.float32)
@@ -287,28 +291,26 @@
     return pl.pallas_call(
         functools.partial(project_kernel, places),
         out_shape=jax.ShapeDtypeStruct((ROWS, 2 * WIDE + HEAD), jnp.float32),
-        in_specs=smem(1) + hbm(5) + vmem(len(places)),
+        in_specs=smem(1) + hbm(4) + vmem(len(places) + 1),
         out_specs=vmem(1)[0],
         scratch_shapes=[
             pltpu.VMEM((BUFFERS, 2 * BLOCK, HEAD), jnp.bfloat16),
-            pltpu.VMEM((ROWS, BLOCK), jnp.bfloat16),
             pltpu.VMEM((ROWS, HEAD), jnp.float32),
             pltpu.VMEM((2 * RANK, HEAD), jnp.bfloat16),
             pltpu.VMEM((ROWS, WIDE), jnp.float32),
             pltpu.SemaphoreType.DMA((BUFFERS,)),
-            pltpu.SemaphoreType.DMA((4,)),
+            pltpu.SemaphoreType.DMA((3,)),
         ],
         compiler_params=pltpu.CompilerParams(vmem_limit_bytes=VMEM_LIMIT),
         name="project",
     )(
         own,
         weight_rows,
-        in_hbm(blocks[0]),
         in_hbm(turn),
         in_hbm(up),
         in_hbm(begun),
         in_hbm(bias),
-        *[blocks[place] for place in places if place],
+        *[blocks[place] for place in places],
     )
 
 
@@ -396,21 +398,22 @@
     near = lax.all_to_all(sent, "rollout", 0, 0, tiled=True, axis_index_groups=SAME_CORE)
     far = lax.ppermute(near, "rollout", SIBLING)
 
-    met, far_x = lax.optimization_barrier((met, far_x))
+    slots = slots_of(routes)
+    far_x, slots = lax.optimization_barrier((far_x, slots))
     met_far = across_y(far_x)
     met_next, met_last = along_x(met, 1), along_x(met, 3)
     blocks = [tokens, next_x, far_x, last_x, met, met_next, met_far, met_last]
     early, late = (1, 2, 3, 4, 0), (6, 5, 7)
-    down, begun, up = low_begin(lookup, own, near, far, blocks, early)
-    slots = slots_of(routes)
-    started = begin(own, blocks, (1, 2), weight_rows)
-    met_far, met_next, met_last, down, begun, up, slots, started = lax.optimization_barrier(
-        (met_far, met_next, met_last, down, begun, up, slots, started)
+    down, begun, up, started = low_begin(
+        inverse_of(lookup), own, near, far, weight_rows, blocks, early
+    )
+    met_far, met_next, met_last, down, begun, up, started, slots = lax.optimization_barrier(
+        (met_far, met_next, met_last, down, begun, up, started, slots)
     )
     blocks[5:] = [met_next, met_far, met_last]
     low = low_end(own, down, begun, blocks, late)
     low_all = lax.all_to_all(low, "tensor", 0, 0, tiled=True).reshape(2 * RANK, ROWS)
-    made = project(own, blocks, (3, 4, 5, 6, 7, 0), weight_rows, turn, up, started, bias)
+    made = project(own, blocks, REST, weight_rows, turn, up, started, bias)
     outgoing = finish(made, low_all, slots)
     arrived = lax.all_to_all(outgoing, "rollout", 0, 0, tiled=True)
     return arrived.reshape(GROUPS * CAP, 2, HEAD)

time: 97 us -> 96.4 us (level)
  blocking collectives: 26.8 us -> 24.7 us
  starting transfers between devices: 47.7 us -> 48.9 us
  waiting for transfers between devices: 3.24 us -> 4.32 us
    pallas_call x1, Pallas kernels: 3.6 us -> 1.25 us  [inverse_of(): pl.pallas_call(inverse_kernel, out_shape=pltpu.HBM((GROUPS,), jnp.int32),...]
    pallas_call x1, Pallas kernels: 3.54 us -> 5.78 us  [low_begin(): pl.pallas_call(functools.partial(low_begin_kernel, places), out_shape=(ja...]
    all_to_all x1, blocking collectives: 26.8 us -> 24.7 us  [body(): arrived = lax.all_to_all(outgoing, 'rollout', 0, 0, tiled=True)]
    ppermute x1, starting transfers between devices: 5.92 us -> 7.32 us  [body(): far = lax.ppermute(near, 'rollout', SIBLING)]
  transfers between devices with their start and end apart: 10 -> 10, of which waited for: 2 -> 2; matrix products, arithmetic and copies ran while one was open for 0% -> 0% of each run, Pallas kernels for 16% -> 15%
where the time goes in v4:
time: 96.4 us; the launch traced here: 95.8 us
  starting transfers between devices  48.9 us (51%)
  blocking collectives  24.7 us (26%)
  Pallas kernels  16.8 us (17%)
  waiting for transfers between devices  4.32 us (4%)
    all_to_all x1, blocking collectives, body(): arrived = lax.all_to_all(outgoing, 'rollout', 0, 0, tiled=True)  24.7 us
    ppermute x5, starting transfers between devices, along_x(): return lax.ppermute(block, 'tensor', X_HOP[hop])  16.4 us
    all_to_all x1, starting transfers between devices, body(): lax.all_to_all(sent, 'rollout', 0, 0, tiled=True, axis_index_groups=SAME_...  14.8 us
    ppermute x1, starting transfers between devices, body(): far = lax.ppermute(near, 'rollout', SIBLING)  7.32 us
    ppermute x2, starting transfers between devices, across_y(): return lax.ppermute(block, 'tensor', Y_PARTNER)  7.02 us
    pallas_call x1, Pallas kernels, low_begin(): pl.pallas_call(functools.partial(low_begin_kernel, places), out_shape=(ja...  5.78 us
    pallas_call x1, Pallas kernels, project(): pl.pallas_call(functools.partial(project_kernel, places), out_shape=jax.S...  4.25 us
    all_to_all x1, starting transfers between devices, body(): lax.all_to_all(low, 'tensor', 0, 0, tiled=True).reshape(2 * RANK, ROWS)  3.37 us
  transfers between devices with their start and end apart: 10, of which 2 were waited for; matrix products, arithmetic and copies ran while one was open for 0% of the time, Pallas kernels for 15%

profile of v4, /device:TPU:1, one launch (start us, length us, event | category | flops | bytes accessed | tf_op | source)
XLA Modules:
  0.0 95.8 jit_solution(9946133530733729219)
XLA Ops:
  0.0 4.0 %collective-permute-start.2 = (bf16[256,1024]{1,0:T(8,128)(2,1)}, bf16[256,1024]{1,0:T(8,128)(2,1)S(1)}, u32[]{:S(2)}, u32[]{:S(2)}) collective-permute-start(bf16[256,1024]{1,0:T(8,128)(2,1)} %tokens_ref.1), channel_id=1, source_target_pairs={{0,4},{1,5},{2,6},{3,7},{4,0},{5,1},{6,2},{7,3},{8,12},{9,13},{10,... | collective-permute-start | bytes 1572872 | tf_op jit(solution)/shard_map/ppermute | solution.py:390
  4.0 4.7 %collective-permute-start = (bf16[256,1024]{1,0:T(8,128)(2,1)}, bf16[256,1024]{1,0:T(8,128)(2,1)}, u32[]{:S(2)}, u32[]{:S(2)}) collective-permute-start(bf16[256,1024]{1,0:T(8,128)(2,1)} %tokens_ref.1), channel_id=1, source_target_pairs={{0,2},{1,3},{2,0},{3,1},{4,6},{5,7},{6,4},{7,5},{8,10},{9,11},{10,... | collective-permute-start | bytes 1572872 | tf_op jit(solution)/shard_map/ppermute | solution.py:387
  8.7 2.2 %collective-permute-start.7 = (bf16[256,1024]{1,0:T(8,128)(2,1)}, bf16[256,1024]{1,0:T(8,128)(2,1)S(1)}, u32[]{:S(2)}, u32[]{:S(2)}) collective-permute-start(bf16[256,1024]{1,0:T(8,128)(2,1)} %tokens_ref.1), channel_id=1, source_target_pairs={{0,1},{1,2},{2,3},{3,0},{4,5},{5,6},{6,7},{7,4},{8,9},{9,10},{10,1... | collective-permute-start | bytes 1572872 | tf_op jit(solution)/shard_map/ppermute | solution.py:387
  10.9 4.3 %collective-permute-start.6 = (bf16[256,1024]{1,0:T(8,128)(2,1)}, bf16[256,1024]{1,0:T(8,128)(2,1)}, u32[]{:S(2)}, u32[]{:S(2)}) collective-permute-start(bf16[256,1024]{1,0:T(8,128)(2,1)} %tokens_ref.1), channel_id=1, source_target_pairs={{0,3},{1,0},{2,1},{3,2},{4,7},{5,4},{6,5},{7,6},{8,11},{9,8},{10,9... | collective-permute-start | bytes 1572872 | tf_op jit(solution)/shard_map/ppermute | solution.py:387
  15.2 0.1 pad_add_fusion.own_ref
  15.3 2.4 %share.1 = (bf16[32,40,128]{2,1,0:T(8,128)(2,1)}, f32[256,128]{1,0:T(8,128)}) custom-call(s32[3]{0:T(128)S(1)} %pad_add_fusion.own_ref, s32[1,8]{1,0:T(1,128)} %lengths_ref.1, f32[1,128]{1,0:T(1,128)} %constant.45.clone.rate_ref, bf16[256,128]{1,0:T(8,128)(2,1)} %bitcast.15, bf16[4,128]{1,0:T(4,128)(2,1)} %bitcast.16), custom_call_target="tpu_custom_call" | custom-call | tf_op jit(solution)/shard_map/share/pallas_call | solution.py:101
  17.7 14.8 %all-to-all-start = ((bf16[32,40,128]{2,1,0:T(8,128)(2,1)}), bf16[32,40,128]{2,1,0:T(8,128)(2,1)S(1)}, u32[]{:S(2)}, u32[]{:S(2)}) async-start(bf16[32,40,128]{2,1,0:T(8,128)(2,1)} %get-tuple-element.23), calls=%async_computation | async-start | bytes 655360 | tf_op jit(solution)/shard_map/all_to_all | solution.py:398
  32.5 0.8 slots.1.slot_ref
  33.3 0.0 collective-permute-done.refs_1_
  33.4 3.0 %collective-permute-start.1 = (bf16[256,1024]{1,0:T(8,128)(2,1)}, bf16[256,1024]{1,0:T(8,128)(2,1)S(1)}, u32[]{:S(2)}, u32[]{:S(2)}) collective-permute-start(bf16[256,1024]{1,0:T(8,128)(2,1)} %collective-permute-done.refs_1_), channel_id=1, source_target_pairs={{0,4},{1,5},{2,6},{3,7},{4,0},{5,1},{6,2},{7,3},{8,12},{9,13},{10,... | collective-permute-start | bytes 1572872 | tf_op jit(solution)/shard_map/ppermute | solution.py:390
  36.4 0.0 collective-permute-done.2.refs_3_.refs_1_
  36.4 1.9 %collective-permute-start.3 = (bf16[256,1024]{1,0:T(8,128)(2,1)S(1)}, bf16[256,1024]{1,0:T(8,128)(2,1)S(1)}, u32[]{:S(2)}, u32[]{:S(2)}) collective-permute-start(bf16[256,1024]{1,0:T(8,128)(2,1)S(1)} %collective-permute-done.2.refs_3_.refs_1_), channel_id=1, source_target_pairs={{0,3},{1,0},{2,1},{3,2},{4,7},{5,4},{6,5},{7,6},{8,11},{9,8},{10,9... | collective-permute-start | bytes 1572872 | tf_op jit(solution)/shard_map/ppermute | solution.py:387
  38.3 3.4 %collective-permute-start.4 = (bf16[256,1024]{1,0:T(8,128)(2,1)S(1)}, bf16[256,1024]{1,0:T(8,128)(2,1)S(1)}, u32[]{:S(2)}, u32[]{:S(2)}) collective-permute-start(bf16[256,1024]{1,0:T(8,128)(2,1)S(1)} %collective-permute-done.2.refs_3_.refs_1_), channel_id=1, source_target_pairs={{0,1},{1,2},{2,3},{3,0},{4,5},{5,6},{6,7},{7,4},{8,9},{9,10},{10,1... | collective-permute-start | bytes 1572872 | tf_op jit(solution)/shard_map/ppermute | solution.py:387
  41.7 0.0 collective-permute-done.7.refs_2_.refs_0_
  41.7 3.2 %all-to-all-done.near_ref = bf16[32,40,128]{2,1,0:T(8,128)(2,1)S(1)} async-done(((bf16[32,40,128]{2,1,0:T(8,128)(2,1)}), bf16[32,40,128]{2,1,0:T(8,128)(2,1)S(1)}, u32[]{:S(2)}, u32[]{:S(2)}) %all-to-all-start) | async-done | bytes 327712 | tf_op jit(solution)/shard_map/all_to_all | solution.py:398
  44.9 7.3 %collective-permute-start.5 = (bf16[32,40,128]{2,1,0:T(8,128)(2,1)S(1)}, bf16[32,40,128]{2,1,0:T(8,128)(2,1)S(1)}, u32[]{:S(2)}, u32[]{:S(2)}) collective-permute-start(bf16[32,40,128]{2,1,0:T(8,128)(2,1)S(1)} %all-to-all-done.near_ref), channel_id=1, source_target_pairs={{0,8},{8,0},{16,24},{24,16},{32,40},{40,32},{48,56},{56,48},{64,72... | collective-permute-start | bytes 983048 | tf_op jit(solution)/shard_map/ppermute | solution.py:399
  52.2 1.3 %inverse.1.inverse_ref = s32[64]{0:T(128)} custom-call(s32[64]{0:T(128)} %lookup_ref.1), custom_call_target="tpu_custom_call" | custom-call | flops 8000000000 | tf_op jit(solution)/shard_map/inverse/pallas_call | solution.py:131
  53.4 0.0 collective-permute-done.6.refs_0_
  53.5 0.0 collective-permute-done.5.far_ref
  53.5 5.8 %low_begin.1 = (bf16[32,8192]{1,0:T(8,128)(2,1)S(1)}, f32[256,32]{1,0:T(8,128)S(1)}, bf16[256,128]{1,0:T(8,128)(2,1)}, f32[256,256]{1,0:T(8,128)}) custom-call(s32[64]{0:T(128)} %inverse.1.inverse_ref, s32[3]{0:T(128)S(1)} %pad_add_fusion.own_ref, bf16[32,40,128]{2,1,0:T(8,128)(2,1)S(1)} %all-to-all-done.near_ref, ...), custom_call_target="tpu_custom_call" | custom-call | tf_op jit(solution)/shard_map/low_begin/pallas_call | solution.py:213
  59.3 0.0 collective-permute-done.3.refs_3_.refs_1_
  59.3 0.0 collective-permute-done.4.refs_4_.refs_2_
  59.3 0.0 collective-permute-done.1.refs_2_.refs_0_
  59.3 1.8 %low_end.1 = bf16[8,32,256]{2,1,0:T(8,128)(2,1)} custom-call(s32[3]{0:T(128)S(1)} %pad_add_fusion.own_ref, bf16[32,8192]{1,0:T(8,128)(2,1)S(1)} %get-tuple-element.34.down_ref, f32[256,32]{1,0:T(8,128)S(1)} %get-tuple-element.35.begun_ref, bf16[256,1024]{1,0:T(8,128)(2,1)S(1)} %collective-permute-done.1.refs_2_.refs_0_, ...), custom_call_target="tpu_custom_call" | custom-call | tf_op jit(solution)/shard_map/low_end/pallas_call | solution.py:251
  61.1 3.4 %all-to-all-start.1 = ((bf16[8,32,256]{2,1,0:T(8,128)(2,1)}), bf16[8,32,256]{2,1,0:T(8,128)(2,1)S(1)}, u32[]{:S(2)}, u32[]{:S(2)}) async-start(bf16[8,32,256]{2,1,0:T(8,128)(2,1)} %low_end.1), calls=%async_computation.1 | async-start | bytes 262144 | tf_op jit(solution)/shard_map/all_to_all | solution.py:415
  64.5 4.2 %project.1.made_ref = f32[256,640]{1,0:T(8,128)S(1)} custom-call(s32[3]{0:T(128)S(1)} %pad_add_fusion.own_ref, bf16[16384,128]{1,0:T(8,128)(2,1)} %bitcast.13, f32[256,128]{1,0:T(8,128)} %get-tuple-element.21.turn_ref, bf16[256,128]{1,0:T(8,128)(2,1)} %get-tuple-element.29.up_ref, f32[256,256]{1,0:T(8,128)} %get-tuple-element.30.begun_ref, ...), custom_call_target="tpu_custom_call" | custom-call | tf_op jit(solution)/shard_map/project/pallas_call | solution.py:291
  68.7 1.1 %all-to-all-done.1 = bf16[8,32,256]{2,1,0:T(8,128)(2,1)S(1)} async-done(((bf16[8,32,256]{2,1,0:T(8,128)(2,1)}), bf16[8,32,256]{2,1,0:T(8,128)(2,1)S(1)}, u32[]{:S(2)}, u32[]{:S(2)}) %all-to-all-start.1) | async-done | bytes 131104 | tf_op jit(solution)/shard_map/all_to_all | solution.py:415
  69.8 0.5 finish.1
  70.3 24.7 %all_to_all.19 = bf16[64,16,128]{2,1,0:T(8,128)(2,1)S(1)} all-to-all(bf16[64,16,128]{2,1,0:T(8,128)(2,1)S(1)} %bitcast.10), channel_id=1, replica_groups=mesh['rollout'=64,'tensor'=8] {'rollout'}, dimensions={0} | all-to-all | bytes 524288 | tf_op jit(solution)/shard_map/all_to_all | solution.py:418
  95.1 0.7 copy.11
Async XLA Ops:
  0.0 36.4 %collective-permute-start.2 = (bf16[256,1024]{1,0:T(8,128)(2,1)}, bf16[256,1024]{1,0:T(8,128)(2,1)S(1)}, u32[]{:S(2)}, u32[]{:S(2)}) collective-permute-start(bf16[256,1024]{1,0:T(8,128)(2,1)} %tokens_ref.1), channel_id=1, source_target_pairs={{0,4},{1,5},{2,6},{3,7},{4,0},{5,1},{6,2},{7,3},{8,12},{9,13},{10,... | collective-permute-start | bytes 1572872 | tf_op jit(solution)/shard_map/ppermute | solution.py:390
  4.0 29.3 %collective-permute-start = (bf16[256,1024]{1,0:T(8,128)(2,1)}, bf16[256,1024]{1,0:T(8,128)(2,1)}, u32[]{:S(2)}, u32[]{:S(2)}) collective-permute-start(bf16[256,1024]{1,0:T(8,128)(2,1)} %tokens_ref.1), channel_id=1, source_target_pairs={{0,2},{1,3},{2,0},{3,1},{4,6},{5,7},{6,4},{7,5},{8,10},{9,11},{10,... | collective-permute-start | bytes 1572872 | tf_op jit(solution)/shard_map/ppermute | solution.py:387
  8.7 33.0 %collective-permute-start.7 = (bf16[256,1024]{1,0:T(8,128)(2,1)}, bf16[256,1024]{1,0:T(8,128)(2,1)S(1)}, u32[]{:S(2)}, u32[]{:S(2)}) collective-permute-start(bf16[256,1024]{1,0:T(8,128)(2,1)} %tokens_ref.1), channel_id=1, source_target_pairs={{0,1},{1,2},{2,3},{3,0},{4,5},{5,6},{6,7},{7,4},{8,9},{9,10},{10,1... | collective-permute-start | bytes 1572872 | tf_op jit(solution)/shard_map/ppermute | solution.py:387
  10.9 42.5 %collective-permute-start.6 = (bf16[256,1024]{1,0:T(8,128)(2,1)}, bf16[256,1024]{1,0:T(8,128)(2,1)}, u32[]{:S(2)}, u32[]{:S(2)}) collective-permute-start(bf16[256,1024]{1,0:T(8,128)(2,1)} %tokens_ref.1), channel_id=1, source_target_pairs={{0,3},{1,0},{2,1},{3,2},{4,7},{5,4},{6,5},{7,6},{8,11},{9,8},{10,9... | collective-permute-start | bytes 1572872 | tf_op jit(solution)/shard_map/ppermute | solution.py:387
  17.7 27.1 %all-to-all-start = ((bf16[32,40,128]{2,1,0:T(8,128)(2,1)}), bf16[32,40,128]{2,1,0:T(8,128)(2,1)S(1)}, u32[]{:S(2)}, u32[]{:S(2)}) async-start(bf16[32,40,128]{2,1,0:T(8,128)(2,1)} %get-tuple-element.23), calls=%async_computation | async-start | bytes 655360 | tf_op jit(solution)/shard_map/all_to_all | solution.py:398
  33.4 25.9 %collective-permute-start.1 = (bf16[256,1024]{1,0:T(8,128)(2,1)}, bf16[256,1024]{1,0:T(8,128)(2,1)S(1)}, u32[]{:S(2)}, u32[]{:S(2)}) collective-permute-start(bf16[256,1024]{1,0:T(8,128)(2,1)} %collective-permute-done.refs_1_), channel_id=1, source_target_pairs={{0,4},{1,5},{2,6},{3,7},{4,0},{5,1},{6,2},{7,3},{8,12},{9,13},{10,... | collective-permute-start | bytes 1572872 | tf_op jit(solution)/shard_map/ppermute | solution.py:390
  36.4 22.9 %collective-permute-start.3 = (bf16[256,1024]{1,0:T(8,128)(2,1)S(1)}, bf16[256,1024]{1,0:T(8,128)(2,1)S(1)}, u32[]{:S(2)}, u32[]{:S(2)}) collective-permute-start(bf16[256,1024]{1,0:T(8,128)(2,1)S(1)} %collective-permute-done.2.refs_3_.refs_1_), channel_id=1, source_target_pairs={{0,3},{1,0},{2,1},{3,2},{4,7},{5,4},{6,5},{7,6},{8,11},{9,8},{10,9... | collective-permute-start | bytes 1572872 | tf_op jit(solution)/shard_map/ppermute | solution.py:387
  38.3 21.0 %collective-permute-start.4 = (bf16[256,1024]{1,0:T(8,128)(2,1)S(1)}, bf16[256,1024]{1,0:T(8,128)(2,1)S(1)}, u32[]{:S(2)}, u32[]{:S(2)}) collective-permute-start(bf16[256,1024]{1,0:T(8,128)(2,1)S(1)} %collective-permute-done.2.refs_3_.refs_1_), channel_id=1, source_target_pairs={{0,1},{1,2},{2,3},{3,0},{4,5},{5,6},{6,7},{7,4},{8,9},{9,10},{10,1... | collective-permute-start | bytes 1572872 | tf_op jit(solution)/shard_map/ppermute | solution.py:387
  44.9 8.6 %collective-permute-start.5 = (bf16[32,40,128]{2,1,0:T(8,128)(2,1)S(1)}, bf16[32,40,128]{2,1,0:T(8,128)(2,1)S(1)}, u32[]{:S(2)}, u32[]{:S(2)}) collective-permute-start(bf16[32,40,128]{2,1,0:T(8,128)(2,1)S(1)} %all-to-all-done.near_ref), channel_id=1, source_target_pairs={{0,8},{8,0},{16,24},{24,16},{32,40},{40,32},{48,56},{56,48},{64,72... | collective-permute-start | bytes 983048 | tf_op jit(solution)/shard_map/ppermute | solution.py:399
  61.1 8.7 %all-to-all-start.1 = ((bf16[8,32,256]{2,1,0:T(8,128)(2,1)}), bf16[8,32,256]{2,1,0:T(8,128)(2,1)S(1)}, u32[]{:S(2)}, u32[]{:S(2)}) async-start(bf16[8,32,256]{2,1,0:T(8,128)(2,1)} %low_end.1), calls=%async_computation.1 | async-start | bytes 262144 | tf_op jit(solution)/shard_map/all_to_all | solution.py:415

commit v5 on v4

--- a/solution.py
+++ b/solution.py
@@ -55,35 +55,7 @@
     return [pl.BlockSpec(memory_space=pltpu.SMEM)] * count
 
 
-def share_kernel(
-    own_ref,
-    lengths_ref,
-    rate_ref,
-    down_hbm,
-    up_hbm,
-    out_ref,
-    turn_ref,
-    down_ref,
-    up_ref,
-    wide,
-    turned,
-    done,
-):
-    down_copy = pltpu.make_async_copy(down_hbm, down_ref, done.at[0])
-    up_copy = pltpu.make_async_copy(up_hbm, up_ref, done.at[1])
-    down_copy.start()
-    up_copy.start()
-    row = lax.broadcasted_iota(jnp.int32, (ROWS, HEAD), 0)
-    begins = jnp.zeros((ROWS, HEAD), jnp.int32)
-    start = jnp.int32(0)
-    for piece in range(lengths_ref.shape[1]):
-        begins = jnp.where(row >= start, jnp.maximum(begins, start), begins)
-        start = start + lengths_ref[0, piece]
-    angles = (row - begins).astype(jnp.float32) * rate_ref[...]
-    low_half = lax.broadcasted_iota(jnp.int32, (ROWS, HEAD), 1) < HEAD // 2
-    turn_ref[...] = jnp.cos(jnp.where(low_half, angles, angles - np.float32(np.pi / 2)))
-    down_copy.wait()
-    up_copy.wait()
+def share_kernel(own_ref, down_ref, up_ref, out_ref, wide, turned):
     lane = own_ref[0] * X + own_ref[1]
     wide[...] = down_ref[...].astype(jnp.float32)
     turned[...] = wide[pl.ds(lane // X, 128, stride=2), :].T
@@ -95,27 +67,19 @@
         out_ref[target] = sent
 
 
-def share(own, lengths, down_rows, up_rows):
-    half_rate = rope_base ** (-(np.arange(HEAD // 2, dtype=np.float32) * 2.0) / HEAD)
-    rate = jnp.asarray(np.concatenate([half_rate, half_rate])[None], jnp.float32)
+def share(own, down_rows, up_rows):
     return pl.pallas_call(
         share_kernel,
-        out_shape=(
-            jax.ShapeDtypeStruct((GROUPS // 2, SENT, HEAD), jnp.bfloat16),
-            pltpu.HBM((ROWS, HEAD), jnp.float32),
-        ),
-        in_specs=smem(2) + vmem(1) + hbm(2),
-        out_specs=tuple(vmem(2)),
+        out_shape=pltpu.HBM((GROUPS // 2, SENT, HEAD), jnp.bfloat16),
+        in_specs=smem(1) + vmem(2),
+        out_specs=vmem(1)[0],
         scratch_shapes=[
-            pltpu.VMEM((2 * 128, RANK), jnp.bfloat16),
-            pltpu.VMEM((4, HEAD), jnp.bfloat16),
             pltpu.VMEM((2 * 128, RANK), jnp.float32),
             pltpu.VMEM((RANK, 128), jnp.float32),
-            pltpu.SemaphoreType.DMA((2,)),
         ],
         compiler_params=pltpu.CompilerParams(vmem_limit_bytes=VMEM_LIMIT),
         name="share",
-    )(own, in_hbm(lengths), in_hbm(rate), in_hbm(down_rows), in_hbm(up_rows))
+    )(own, in_hbm(down_rows), in_hbm(up_rows))
 
 
 def source_of(own_ref, place):
@@ -258,28 +222,37 @@
     )(own, down, begun, *[blocks[place] for place in places])
 
 
-def project_kernel(places, own_ref, weight_ref, turn_ref, up_ref, begun_ref, bias_ref, *refs):
-    out_ref, weights, turn, up, begun, weight_done, done = refs[len(places) :]
+def project_kernel(
+    places, own_ref, lengths_ref, weight_ref, up_ref, begun_ref, rate_ref, bias_ref, *refs
+):
+    out_ref, weights, up, begun, weight_done, done = refs[len(places) :]
     copies = weight_copies(own_ref, weight_ref, weights, weight_done, places)
     for copy in copies[:BUFFERS]:
         copy.start()
     small = [
         pltpu.make_async_copy(from_ref, to_ref, done.at[at])
         for at, (from_ref, to_ref) in enumerate(
-            [(turn_ref, turn), (up_ref, up), (begun_ref, begun)]
+            [(up_ref, up), (begun_ref, begun)]
         )
     ]
     for copy in small:
         copy.start()
-    for copy in small:
-        copy.wait()
-    table = turn[...]
+    row = lax.broadcasted_iota(jnp.int32, (ROWS, HEAD), 0)
+    begins = jnp.zeros((ROWS, HEAD), jnp.int32)
+    start = jnp.int32(0)
+    for piece in range(lengths_ref.shape[1]):
+        begins = jnp.where(row >= start, jnp.maximum(begins, start), begins)
+        start = start + lengths_ref[0, piece]
+    angles = (row - begins).astype(jnp.float32) * rate_ref[...]
+    low_half = lax.broadcasted_iota(jnp.int32, (ROWS, HEAD), 1) < HEAD // 2
+    table = jnp.cos(jnp.where(low_half, angles, angles - np.float32(np.pi / 2)))
     swapped = pltpu.roll(table, HEAD // 2, 1)
-    low_half = lax.broadcasted_iota(jnp.int32, (ROWS, HEAD), 1) < HEAD // 2
     cosine = jnp.where(low_half, table, swapped)
     sine = jnp.where(low_half, -swapped, table)
     out_ref[:, WIDE : WIDE + HEAD] = cosine
     out_ref[:, WIDE + HEAD : 2 * WIDE] = sine
+    for copy in small:
+        copy.wait()
     out_ref[:, 2 * WIDE :] = up[...].astype(jnp.float32)
     total = begun[...] + project_blocks(copies, refs[: len(places)], weights)
     keys = total[:, :HEAD] + bias_ref[0:1, :].astype(jnp.float32)
@@ -287,28 +260,30 @@
     out_ref[:, HEAD:WIDE] = total[:, HEAD:] + bias_ref[1:2, :].astype(jnp.float32)
 
 
-def project(own, blocks, places, weight_rows, turn, up, begun, bias):
+def project(own, lengths, blocks, places, weight_rows, up, begun, bias):
+    half_rate = rope_base ** (-(np.arange(HEAD // 2, dtype=np.float32) * 2.0) / HEAD)
+    rate = jnp.asarray(np.concatenate([half_rate, half_rate])[None], jnp.float32)
     return pl.pallas_call(
         functools.partial(project_kernel, places),
         out_shape=jax.ShapeDtypeStruct((ROWS, 2 * WIDE + HEAD), jnp.float32),
-        in_specs=smem(1) + hbm(4) + vmem(len(places) + 1),
+        in_specs=smem(2) + hbm(3) + vmem(len(places) + 2),
         out_specs=vmem(1)[0],
         scratch_shapes=[
             pltpu.VMEM((BUFFERS, 2 * BLOCK, HEAD), jnp.bfloat16),
-            pltpu.VMEM((ROWS, HEAD), jnp.float32),
             pltpu.VMEM((2 * RANK, HEAD), jnp.bfloat16),
             pltpu.VMEM((ROWS, WIDE), jnp.float32),
             pltpu.SemaphoreType.DMA((BUFFERS,)),
-            pltpu.SemaphoreType.DMA((3,)),
+            pltpu.SemaphoreType.DMA((2,)),
         ],
         compiler_params=pltpu.CompilerParams(vmem_limit_bytes=VMEM_LIMIT),
         name="project",
     )(
         own,
+        in_hbm(lengths),
         weight_rows,
-        in_hbm(turn),
         in_hbm(up),
         in_hbm(begun),
+        in_hbm(rate),
         in_hbm(bias),
         *[blocks[place] for place in places],
     )
@@ -392,9 +367,7 @@
     met = across_y(tokens)
     far_x, next_x, last_x = along_x(tokens, 2), along_x(tokens, 1), along_x(tokens, 3)
 
-    sent, turn = share(
-        own, lengths, down_blocks.reshape(2 * 128, RANK), up_blocks.reshape(4, HEAD)
-    )
+    sent = share(own, down_blocks.reshape(2 * 128, RANK), up_blocks.reshape(4, HEAD))
     near = lax.all_to_all(sent, "rollout", 0, 0, tiled=True, axis_index_groups=SAME_CORE)
     far = lax.ppermute(near, "rollout", SIBLING)
 
@@ -413,7 +386,7 @@
     blocks[5:] = [met_next, met_far, met_last]
     low = low_end(own, down, begun, blocks, late)
     low_all = lax.all_to_all(low, "tensor", 0, 0, tiled=True).reshape(2 * RANK, ROWS)
-    made = project(own, blocks, REST, weight_rows, turn, up, started, bias)
+    made = project(own, lengths, blocks, REST, weight_rows, up, started, bias)
     outgoing = finish(made, low_all, slots)
     arrived = lax.all_to_all(outgoing, "rollout", 0, 0, tiled=True)
     return arrived.reshape(GROUPS * CAP, 2, HEAD)

time: 96.4 us -> 95.7 us (level)
  transfers between devices with their start and end apart: 10 -> 10, of which waited for: 2 -> 2; matrix products, arithmetic and copies ran while one was open for 0% -> 0% of each run, Pallas kernels for 15% -> 14%
where the time goes in v5:
time: 95.7 us; the launch traced here: 95.1 us
  starting transfers between devices  48.9 us (51%)
  blocking collectives  24.7 us (26%)
  Pallas kernels  16 us (17%)
  waiting for transfers between devices  4.43 us (5%)
    all_to_all x1, blocking collectives, body(): arrived = lax.all_to_all(outgoing, 'rollout', 0, 0, tiled=True)  24.7 us
    ppermute x5, starting transfers between devices, along_x(): return lax.ppermute(block, 'tensor', X_HOP[hop])  16.4 us
    all_to_all x1, starting transfers between devices, body(): lax.all_to_all(sent, 'rollout', 0, 0, tiled=True, axis_index_groups=SAME_...  14.8 us
    ppermute x1, starting transfers between devices, body(): far = lax.ppermute(near, 'rollout', SIBLING)  7.32 us
    ppermute x2, starting transfers between devices, across_y(): return lax.ppermute(block, 'tensor', Y_PARTNER)  7.02 us
    pallas_call x1, Pallas kernels, low_begin(): pl.pallas_call(functools.partial(low_begin_kernel, places), out_shape=(ja...  5.78 us
    pallas_call x1, Pallas kernels, project(): pl.pallas_call(functools.partial(project_kernel, places), out_shape=jax.S...  4.14 us
    all_to_all x1, starting transfers between devices, body(): lax.all_to_all(low, 'tensor', 0, 0, tiled=True).reshape(2 * RANK, ROWS)  3.37 us
  transfers between devices with their start and end apart: 10, of which 2 were waited for; matrix products, arithmetic and copies ran while one was open for 0% of the time, Pallas kernels for 14%

profile of v5, /device:TPU:1, one launch (start us, length us, event | category | flops | bytes accessed | tf_op | source)
XLA Modules:
  0.0 95.1 jit_solution(15379495474214191934)
XLA Ops:
  0.0 4.0 %collective-permute-start.2 = (bf16[256,1024]{1,0:T(8,128)(2,1)}, bf16[256,1024]{1,0:T(8,128)(2,1)S(1)}, u32[]{:S(2)}, u32[]{:S(2)}) collective-permute-start(bf16[256,1024]{1,0:T(8,128)(2,1)} %tokens_ref.1), channel_id=1, source_target_pairs={{0,4},{1,5},{2,6},{3,7},{4,0},{5,1},{6,2},{7,3},{8,12},{9,13},{10,... | collective-permute-start | bytes 1572872 | tf_op jit(solution)/shard_map/ppermute | solution.py:365
  4.0 4.7 %collective-permute-start = (bf16[256,1024]{1,0:T(8,128)(2,1)}, bf16[256,1024]{1,0:T(8,128)(2,1)}, u32[]{:S(2)}, u32[]{:S(2)}) collective-permute-start(bf16[256,1024]{1,0:T(8,128)(2,1)} %tokens_ref.1), channel_id=1, source_target_pairs={{0,2},{1,3},{2,0},{3,1},{4,6},{5,7},{6,4},{7,5},{8,10},{9,11},{10,... | collective-permute-start | bytes 1572872 | tf_op jit(solution)/shard_map/ppermute | solution.py:362
  8.7 2.2 %collective-permute-start.7 = (bf16[256,1024]{1,0:T(8,128)(2,1)}, bf16[256,1024]{1,0:T(8,128)(2,1)S(1)}, u32[]{:S(2)}, u32[]{:S(2)}) collective-permute-start(bf16[256,1024]{1,0:T(8,128)(2,1)} %tokens_ref.1), channel_id=1, source_target_pairs={{0,1},{1,2},{2,3},{3,0},{4,5},{5,6},{6,7},{7,4},{8,9},{9,10},{10,1... | collective-permute-start | bytes 1572872 | tf_op jit(solution)/shard_map/ppermute | solution.py:362
  10.9 4.3 %collective-permute-start.6 = (bf16[256,1024]{1,0:T(8,128)(2,1)}, bf16[256,1024]{1,0:T(8,128)(2,1)}, u32[]{:S(2)}, u32[]{:S(2)}) collective-permute-start(bf16[256,1024]{1,0:T(8,128)(2,1)} %tokens_ref.1), channel_id=1, source_target_pairs={{0,3},{1,0},{2,1},{3,2},{4,7},{5,4},{6,5},{7,6},{8,11},{9,8},{10,9... | collective-permute-start | bytes 1572872 | tf_op jit(solution)/shard_map/ppermute | solution.py:362
  15.2 0.1 pad_add_fusion.own_ref
  15.3 1.7 %share.1 = bf16[32,40,128]{2,1,0:T(8,128)(2,1)} custom-call(s32[3]{0:T(128)S(1)} %pad_add_fusion.own_ref, bf16[256,128]{1,0:T(8,128)(2,1)} %bitcast.15, bf16[4,128]{1,0:T(4,128)(2,1)} %bitcast.16), custom_call_target="tpu_custom_call" | custom-call | tf_op jit(solution)/shard_map/share/pallas_call | solution.py:71
  17.0 14.8 %all-to-all-start = ((bf16[32,40,128]{2,1,0:T(8,128)(2,1)}), bf16[32,40,128]{2,1,0:T(8,128)(2,1)S(1)}, u32[]{:S(2)}, u32[]{:S(2)}) async-start(bf16[32,40,128]{2,1,0:T(8,128)(2,1)} %share.1), calls=%async_computation | async-start | bytes 655360 | tf_op jit(solution)/shard_map/all_to_all | solution.py:371
  31.8 0.8 slots.1.slot_ref
  32.6 0.0 collective-permute-done.refs_1_
  32.6 3.0 %collective-permute-start.1 = (bf16[256,1024]{1,0:T(8,128)(2,1)}, bf16[256,1024]{1,0:T(8,128)(2,1)S(1)}, u32[]{:S(2)}, u32[]{:S(2)}) collective-permute-start(bf16[256,1024]{1,0:T(8,128)(2,1)} %collective-permute-done.refs_1_), channel_id=1, source_target_pairs={{0,4},{1,5},{2,6},{3,7},{4,0},{5,1},{6,2},{7,3},{8,12},{9,13},{10,... | collective-permute-start | bytes 1572872 | tf_op jit(solution)/shard_map/ppermute | solution.py:365
  35.7 0.0 collective-permute-done.2.refs_3_.refs_1_
  35.7 1.9 %collective-permute-start.3 = (bf16[256,1024]{1,0:T(8,128)(2,1)S(1)}, bf16[256,1024]{1,0:T(8,128)(2,1)S(1)}, u32[]{:S(2)}, u32[]{:S(2)}) collective-permute-start(bf16[256,1024]{1,0:T(8,128)(2,1)S(1)} %collective-permute-done.2.refs_3_.refs_1_), channel_id=1, source_target_pairs={{0,3},{1,0},{2,1},{3,2},{4,7},{5,4},{6,5},{7,6},{8,11},{9,8},{10,9... | collective-permute-start | bytes 1572872 | tf_op jit(solution)/shard_map/ppermute | solution.py:362
  37.6 3.4 %collective-permute-start.4 = (bf16[256,1024]{1,0:T(8,128)(2,1)S(1)}, bf16[256,1024]{1,0:T(8,128)(2,1)S(1)}, u32[]{:S(2)}, u32[]{:S(2)}) collective-permute-start(bf16[256,1024]{1,0:T(8,128)(2,1)S(1)} %collective-permute-done.2.refs_3_.refs_1_), channel_id=1, source_target_pairs={{0,1},{1,2},{2,3},{3,0},{4,5},{5,6},{6,7},{7,4},{8,9},{9,10},{10,1... | collective-permute-start | bytes 1572872 | tf_op jit(solution)/shard_map/ppermute | solution.py:362
  41.0 0.0 collective-permute-done.7.refs_2_.refs_0_
  41.0 3.2 %all-to-all-done.near_ref = bf16[32,40,128]{2,1,0:T(8,128)(2,1)S(1)} async-done(((bf16[32,40,128]{2,1,0:T(8,128)(2,1)}), bf16[32,40,128]{2,1,0:T(8,128)(2,1)S(1)}, u32[]{:S(2)}, u32[]{:S(2)}) %all-to-all-start) | async-done | bytes 327712 | tf_op jit(solution)/shard_map/all_to_all | solution.py:371
  44.2 7.3 %collective-permute-start.5 = (bf16[32,40,128]{2,1,0:T(8,128)(2,1)S(1)}, bf16[32,40,128]{2,1,0:T(8,128)(2,1)S(1)}, u32[]{:S(2)}, u32[]{:S(2)}) collective-permute-start(bf16[32,40,128]{2,1,0:T(8,128)(2,1)S(1)} %all-to-all-done.near_ref), channel_id=1, source_target_pairs={{0,8},{8,0},{16,24},{24,16},{32,40},{40,32},{48,56},{56,48},{64,72... | collective-permute-start | bytes 983048 | tf_op jit(solution)/shard_map/ppermute | solution.py:372
  51.5 1.3 %inverse.1.inverse_ref = s32[64]{0:T(128)} custom-call(s32[64]{0:T(128)} %lookup_ref.1), custom_call_target="tpu_custom_call" | custom-call | flops 8000000000 | tf_op jit(solution)/shard_map/inverse/pallas_call | solution.py:95
  52.7 0.0 collective-permute-done.6.refs_0_
  52.8 0.0 collective-permute-done.5.far_ref
  52.8 5.8 %low_begin.1 = (bf16[32,8192]{1,0:T(8,128)(2,1)S(1)}, f32[256,32]{1,0:T(8,128)S(1)}, bf16[256,128]{1,0:T(8,128)(2,1)}, f32[256,256]{1,0:T(8,128)}) custom-call(s32[64]{0:T(128)} %inverse.1.inverse_ref, s32[3]{0:T(128)S(1)} %pad_add_fusion.own_ref, bf16[32,40,128]{2,1,0:T(8,128)(2,1)S(1)} %all-to-all-done.near_ref, ...), custom_call_target="tpu_custom_call" | custom-call | tf_op jit(solution)/shard_map/low_begin/pallas_call | solution.py:177
  58.6 0.0 collective-permute-done.3.refs_3_.refs_1_
  58.6 0.0 collective-permute-done.4.refs_4_.refs_2_
  58.6 0.0 collective-permute-done.1.refs_2_.refs_0_
  58.6 1.8 %low_end.1 = bf16[8,32,256]{2,1,0:T(8,128)(2,1)} custom-call(s32[3]{0:T(128)S(1)} %pad_add_fusion.own_ref, bf16[32,8192]{1,0:T(8,128)(2,1)S(1)} %get-tuple-element.30.down_ref, f32[256,32]{1,0:T(8,128)S(1)} %get-tuple-element.31.begun_ref, bf16[256,1024]{1,0:T(8,128)(2,1)S(1)} %collective-permute-done.1.refs_2_.refs_0_, ...), custom_call_target="tpu_custom_call" | custom-call | tf_op jit(solution)/shard_map/low_end/pallas_call | solution.py:215
  60.4 3.4 %all-to-all-start.1 = ((bf16[8,32,256]{2,1,0:T(8,128)(2,1)}), bf16[8,32,256]{2,1,0:T(8,128)(2,1)S(1)}, u32[]{:S(2)}, u32[]{:S(2)}) async-start(bf16[8,32,256]{2,1,0:T(8,128)(2,1)} %low_end.1), calls=%async_computation.1 | async-start | bytes 262144 | tf_op jit(solution)/shard_map/all_to_all | solution.py:388
  63.8 4.1 %project.1.made_ref = f32[256,640]{1,0:T(8,128)S(1)} custom-call(s32[3]{0:T(128)S(1)} %pad_add_fusion.own_ref, s32[1,8]{1,0:T(1,128)} %lengths_ref.1, bf16[16384,128]{1,0:T(8,128)(2,1)} %bitcast.13, bf16[256,128]{1,0:T(8,128)(2,1)} %get-tuple-element.25.up_ref, f32[256,256]{1,0:T(8,128)} %get-tuple-element.26.begun_ref, f32[1,128]{1,0:T(1,128)} %constant.45.clone.rate_ref, ...), custom_call_target="tpu_custom_call" | custom-call | tf_op jit(solution)/shard_map/project/pallas_call | solution.py:266
  67.9 1.2 %all-to-all-done.1 = bf16[8,32,256]{2,1,0:T(8,128)(2,1)S(1)} async-done(((bf16[8,32,256]{2,1,0:T(8,128)(2,1)}), bf16[8,32,256]{2,1,0:T(8,128)(2,1)S(1)}, u32[]{:S(2)}, u32[]{:S(2)}) %all-to-all-start.1) | async-done | bytes 131104 | tf_op jit(solution)/shard_map/all_to_all | solution.py:388
  69.1 0.5 finish.1
  69.6 24.7 %all_to_all.19 = bf16[64,16,128]{2,1,0:T(8,128)(2,1)S(1)} all-to-all(bf16[64,16,128]{2,1,0:T(8,128)(2,1)S(1)} %bitcast.10), channel_id=1, replica_groups=mesh['rollout'=64,'tensor'=8] {'rollout'}, dimensions={0} | all-to-all | bytes 524288 | tf_op jit(solution)/shard_map/all_to_all | solution.py:391
  94.4 0.7 copy.11
Async XLA Ops:
  0.0 35.7 %collective-permute-start.2 = (bf16[256,1024]{1,0:T(8,128)(2,1)}, bf16[256,1024]{1,0:T(8,128)(2,1)S(1)}, u32[]{:S(2)}, u32[]{:S(2)}) collective-permute-start(bf16[256,1024]{1,0:T(8,128)(2,1)} %tokens_ref.1), channel_id=1, source_target_pairs={{0,4},{1,5},{2,6},{3,7},{4,0},{5,1},{6,2},{7,3},{8,12},{9,13},{10,... | collective-permute-start | bytes 1572872 | tf_op jit(solution)/shard_map/ppermute | solution.py:365
  4.0 28.6 %collective-permute-start = (bf16[256,1024]{1,0:T(8,128)(2,1)}, bf16[256,1024]{1,0:T(8,128)(2,1)}, u32[]{:S(2)}, u32[]{:S(2)}) collective-permute-start(bf16[256,1024]{1,0:T(8,128)(2,1)} %tokens_ref.1), channel_id=1, source_target_pairs={{0,2},{1,3},{2,0},{3,1},{4,6},{5,7},{6,4},{7,5},{8,10},{9,11},{10,... | collective-permute-start | bytes 1572872 | tf_op jit(solution)/shard_map/ppermute | solution.py:362
  8.7 32.3 %collective-permute-start.7 = (bf16[256,1024]{1,0:T(8,128)(2,1)}, bf16[256,1024]{1,0:T(8,128)(2,1)S(1)}, u32[]{:S(2)}, u32[]{:S(2)}) collective-permute-start(bf16[256,1024]{1,0:T(8,128)(2,1)} %tokens_ref.1), channel_id=1, source_target_pairs={{0,1},{1,2},{2,3},{3,0},{4,5},{5,6},{6,7},{7,4},{8,9},{9,10},{10,1... | collective-permute-start | bytes 1572872 | tf_op jit(solution)/shard_map/ppermute | solution.py:362
  10.9 41.8 %collective-permute-start.6 = (bf16[256,1024]{1,0:T(8,128)(2,1)}, bf16[256,1024]{1,0:T(8,128)(2,1)}, u32[]{:S(2)}, u32[]{:S(2)}) collective-permute-start(bf16[256,1024]{1,0:T(8,128)(2,1)} %tokens_ref.1), channel_id=1, source_target_pairs={{0,3},{1,0},{2,1},{3,2},{4,7},{5,4},{6,5},{7,6},{8,11},{9,8},{10,9... | collective-permute-start | bytes 1572872 | tf_op jit(solution)/shard_map/ppermute | solution.py:362
  17.0 27.1 %all-to-all-start = ((bf16[32,40,128]{2,1,0:T(8,128)(2,1)}), bf16[32,40,128]{2,1,0:T(8,128)(2,1)S(1)}, u32[]{:S(2)}, u32[]{:S(2)}) async-start(bf16[32,40,128]{2,1,0:T(8,128)(2,1)} %share.1), calls=%async_computation | async-start | bytes 655360 | tf_op jit(solution)/shard_map/all_to_all | solution.py:371
  32.6 25.9 %collective-permute-start.1 = (bf16[256,1024]{1,0:T(8,128)(2,1)}, bf16[256,1024]{1,0:T(8,128)(2,1)S(1)}, u32[]{:S(2)}, u32[]{:S(2)}) collective-permute-start(bf16[256,1024]{1,0:T(8,128)(2,1)} %collective-permute-done.refs_1_), channel_id=1, source_target_pairs={{0,4},{1,5},{2,6},{3,7},{4,0},{5,1},{6,2},{7,3},{8,12},{9,13},{10,... | collective-permute-start | bytes 1572872 | tf_op jit(solution)/shard_map/ppermute | solution.py:365
  35.7 22.9 %collective-permute-start.3 = (bf16[256,1024]{1,0:T(8,128)(2,1)S(1)}, bf16[256,1024]{1,0:T(8,128)(2,1)S(1)}, u32[]{:S(2)}, u32[]{:S(2)}) collective-permute-start(bf16[256,1024]{1,0:T(8,128)(2,1)S(1)} %collective-permute-done.2.refs_3_.refs_1_), channel_id=1, source_target_pairs={{0,3},{1,0},{2,1},{3,2},{4,7},{5,4},{6,5},{7,6},{8,11},{9,8},{10,9... | collective-permute-start | bytes 1572872 | tf_op jit(solution)/shard_map/ppermute | solution.py:362
  37.6 21.0 %collective-permute-start.4 = (bf16[256,1024]{1,0:T(8,128)(2,1)S(1)}, bf16[256,1024]{1,0:T(8,128)(2,1)S(1)}, u32[]{:S(2)}, u32[]{:S(2)}) collective-permute-start(bf16[256,1024]{1,0:T(8,128)(2,1)S(1)} %collective-permute-done.2.refs_3_.refs_1_), channel_id=1, source_target_pairs={{0,1},{1,2},{2,3},{3,0},{4,5},{5,6},{6,7},{7,4},{8,9},{9,10},{10,1... | collective-permute-start | bytes 1572872 | tf_op jit(solution)/shard_map/ppermute | solution.py:362
  44.2 8.6 %collective-permute-start.5 = (bf16[32,40,128]{2,1,0:T(8,128)(2,1)S(1)}, bf16[32,40,128]{2,1,0:T(8,128)(2,1)S(1)}, u32[]{:S(2)}, u32[]{:S(2)}) collective-permute-start(bf16[32,40,128]{2,1,0:T(8,128)(2,1)S(1)} %all-to-all-done.near_ref), channel_id=1, source_target_pairs={{0,8},{8,0},{16,24},{24,16},{32,40},{40,32},{48,56},{56,48},{64,72... | collective-permute-start | bytes 983048 | tf_op jit(solution)/shard_map/ppermute | solution.py:372
  60.4 8.7 %all-to-all-start.1 = ((bf16[8,32,256]{2,1,0:T(8,128)(2,1)}), bf16[8,32,256]{2,1,0:T(8,128)(2,1)S(1)}, u32[]{:S(2)}, u32[]{:S(2)}) async-start(bf16[8,32,256]{2,1,0:T(8,128)(2,1)} %low_end.1), calls=%async_computation.1 | async-start | bytes 262144 | tf_op jit(solution)/shard_map/all_to_all | solution.py:388

commit v6 on v5

--- a/solution.py
+++ b/solution.py
@@ -27,7 +27,17 @@
 
 SAME_CORE = [list(range(core, GROUPS, 2)) for core in range(2)]
 SIBLING = [(a, a ^ 1) for a in range(GROUPS)]
-X_HOP = [[(a, a // X * X + (a - hop) % X) for a in range(2 * X)] for hop in range(X)]
+X_HOP = [
+    [
+        (
+            group * SHARE + lane // X * X + (lane + hop * (1 + 2 * (group % 2))) % X,
+            group * SHARE + lane,
+        )
+        for group in range(GROUPS)
+        for lane in range(SHARE)
+    ]
+    for hop in range(X)
+]
 Y_PARTNER = [(a, (a + X) % (2 * X)) for a in range(2 * X)]
 
 
@@ -83,7 +93,8 @@
 
 
 def source_of(own_ref, place):
-    return (own_ref[0] + place // X) % 2 * X + (own_ref[1] + place) % X
+    x = (own_ref[1] + place * (1 + 2 * own_ref[2])) % X
+    return (own_ref[0] + place // X) % 2 * X + x
 
 
 def inverse_kernel(lookup_ref, inverse_ref):
@@ -359,7 +370,7 @@
     weight_rows = in_hbm(weight.reshape(2 * MODEL, HEAD))
 
     def along_x(block, hop):
-        return lax.ppermute(block, "tensor", X_HOP[hop])
+        return lax.ppermute(block, ("rollout", "tensor"), X_HOP[hop])
 
     def across_y(block):
         return lax.ppermute(block, "tensor", Y_PARTNER)

time: 95.7 us -> 94.5 us (0.987)
  waiting for transfers between devices: 4.43 us -> 2.36 us
  starting transfers between devices: 48.9 us -> 50.4 us
  blocking collectives: 24.7 us -> 23.5 us
    all_to_all x1, waiting for transfers between devices: 3.19 us -> 1.67 us  [body(): lax.all_to_all(sent, 'rollout', 0, 0, tiled=True, axis_index_groups=SAME_...]
    ppermute x1, starting transfers between devices: 7.32 us -> 8.81 us  [body(): far = lax.ppermute(near, 'rollout', SIBLING)]
    all_to_all x1, blocking collectives: 24.7 us -> 23.5 us  [body(): arrived = lax.all_to_all(outgoing, 'rollout', 0, 0, tiled=True)]
  transfers between devices with their start and end apart: 10 -> 10, of which waited for: 2 -> 2; matrix products, arithmetic and copies ran while one was open for 0% -> 0% of each run, Pallas kernels for 14% -> 15%
where the time goes in v6:
time: 94.5 us; the launch traced here: 93.8 us
  starting transfers between devices  50.4 us (53%)
  blocking collectives  23.5 us (25%)
  Pallas kernels  16.6 us (18%)
  waiting for transfers between devices  2.36 us (2%)
    all_to_all x1, blocking collectives, body(): arrived = lax.all_to_all(outgoing, 'rollout', 0, 0, tiled=True)  23.5 us
    ppermute x5, starting transfers between devices, along_x(): return lax.ppermute(block, ('rollout', 'tensor'), X_HOP[hop])  16.4 us
    all_to_all x1, starting transfers between devices, body(): lax.all_to_all(sent, 'rollout', 0, 0, tiled=True, axis_index_groups=SAME_...  14.8 us
    ppermute x1, starting transfers between devices, body(): far = lax.ppermute(near, 'rollout', SIBLING)  8.81 us
    ppermute x2, starting transfers between devices, across_y(): return lax.ppermute(block, 'tensor', Y_PARTNER)  7.02 us
    pallas_call x1, Pallas kernels, low_begin(): pl.pallas_call(functools.partial(low_begin_kernel, places), out_shape=(ja...  5.78 us
    pallas_call x1, Pallas kernels, project(): pl.pallas_call(functools.partial(project_kernel, places), out_shape=jax.S...  4.7 us
    all_to_all x1, starting transfers between devices, body(): lax.all_to_all(low, 'tensor', 0, 0, tiled=True).reshape(2 * RANK, ROWS)  3.37 us
  transfers between devices with their start and end apart: 10, of which 2 were waited for; matrix products, arithmetic and copies ran while one was open for 0% of the time, Pallas kernels for 15%

profile of v6, /device:TPU:1, one launch (start us, length us, event | category | flops | bytes accessed | tf_op | source)
XLA Modules:
  0.0 93.8 jit_solution(10733773018370451443)
XLA Ops:
  0.0 4.0 %collective-permute-start.2 = (bf16[256,1024]{1,0:T(8,128)(2,1)}, bf16[256,1024]{1,0:T(8,128)(2,1)S(1)}, u32[]{:S(2)}, u32[]{:S(2)}) collective-permute-start(bf16[256,1024]{1,0:T(8,128)(2,1)} %tokens_ref.1), channel_id=1, source_target_pairs={{0,4},{1,5},{2,6},{3,7},{4,0},{5,1},{6,2},{7,3},{8,12},{9,13},{10,... | collective-permute-start | bytes 1572872 | tf_op jit(solution)/shard_map/ppermute | solution.py:376
  4.0 4.7 %collective-permute-start = (bf16[256,1024]{1,0:T(8,128)(2,1)}, bf16[256,1024]{1,0:T(8,128)(2,1)}, u32[]{:S(2)}, u32[]{:S(2)}) collective-permute-start(bf16[256,1024]{1,0:T(8,128)(2,1)} %tokens_ref.1), channel_id=1, source_target_pairs={{2,0},{3,1},{0,2},{1,3},{6,4},{7,5},{4,6},{5,7},{10,8},{11,9},{8,1... | collective-permute-start | bytes 1572872 | tf_op jit(solution)/shard_map/ppermute | solution.py:373
  8.7 2.8 %collective-permute-start.7 = (bf16[256,1024]{1,0:T(8,128)(2,1)}, bf16[256,1024]{1,0:T(8,128)(2,1)S(1)}, u32[]{:S(2)}, u32[]{:S(2)}) collective-permute-start(bf16[256,1024]{1,0:T(8,128)(2,1)} %tokens_ref.1), channel_id=1, source_target_pairs={{3,0},{0,1},{1,2},{2,3},{7,4},{4,5},{5,6},{6,7},{9,8},{10,9},{11,1... | collective-permute-start | bytes 1572872 | tf_op jit(solution)/shard_map/ppermute | solution.py:373
  11.5 2.5 %collective-permute-start.6 = (bf16[256,1024]{1,0:T(8,128)(2,1)}, bf16[256,1024]{1,0:T(8,128)(2,1)}, u32[]{:S(2)}, u32[]{:S(2)}) collective-permute-start(bf16[256,1024]{1,0:T(8,128)(2,1)} %tokens_ref.1), channel_id=1, source_target_pairs={{1,0},{2,1},{3,2},{0,3},{5,4},{6,5},{7,6},{4,7},{11,8},{8,9},{9,10... | collective-permute-start | bytes 1572872 | tf_op jit(solution)/shard_map/ppermute | solution.py:373
  14.0 0.1 pad_add_fusion.own_ref
  14.1 1.7 %share.1 = bf16[32,40,128]{2,1,0:T(8,128)(2,1)} custom-call(s32[3]{0:T(128)S(1)} %pad_add_fusion.own_ref, bf16[256,128]{1,0:T(8,128)(2,1)} %bitcast.15, bf16[4,128]{1,0:T(4,128)(2,1)} %bitcast.16), custom_call_target="tpu_custom_call" | custom-call | tf_op jit(solution)/shard_map/share/pallas_call | solution.py:81
  15.8 14.8 %all-to-all-start = ((bf16[32,40,128]{2,1,0:T(8,128)(2,1)}), bf16[32,40,128]{2,1,0:T(8,128)(2,1)S(1)}, u32[]{:S(2)}, u32[]{:S(2)}) async-start(bf16[32,40,128]{2,1,0:T(8,128)(2,1)} %share.1), calls=%async_computation | async-start | bytes 655360 | tf_op jit(solution)/shard_map/all_to_all | solution.py:382
  30.6 0.8 slots.1.slot_ref
  31.4 0.0 collective-permute-done.refs_1_
  31.4 3.0 %collective-permute-start.1 = (bf16[256,1024]{1,0:T(8,128)(2,1)}, bf16[256,1024]{1,0:T(8,128)(2,1)S(1)}, u32[]{:S(2)}, u32[]{:S(2)}) collective-permute-start(bf16[256,1024]{1,0:T(8,128)(2,1)} %collective-permute-done.refs_1_), channel_id=1, source_target_pairs={{0,4},{1,5},{2,6},{3,7},{4,0},{5,1},{6,2},{7,3},{8,12},{9,13},{10,... | collective-permute-start | bytes 1572872 | tf_op jit(solution)/shard_map/ppermute | solution.py:376
  34.4 0.0 collective-permute-done.2.refs_3_.refs_1_
  34.5 2.2 %collective-permute-start.3 = (bf16[256,1024]{1,0:T(8,128)(2,1)S(1)}, bf16[256,1024]{1,0:T(8,128)(2,1)S(1)}, u32[]{:S(2)}, u32[]{:S(2)}) collective-permute-start(bf16[256,1024]{1,0:T(8,128)(2,1)S(1)} %collective-permute-done.2.refs_3_.refs_1_), channel_id=1, source_target_pairs={{1,0},{2,1},{3,2},{0,3},{5,4},{6,5},{7,6},{4,7},{11,8},{8,9},{9,10... | collective-permute-start | bytes 1572872 | tf_op jit(solution)/shard_map/ppermute | solution.py:373
  36.7 4.3 %collective-permute-start.4 = (bf16[256,1024]{1,0:T(8,128)(2,1)S(1)}, bf16[256,1024]{1,0:T(8,128)(2,1)S(1)}, u32[]{:S(2)}, u32[]{:S(2)}) collective-permute-start(bf16[256,1024]{1,0:T(8,128)(2,1)S(1)} %collective-permute-done.2.refs_3_.refs_1_), channel_id=1, source_target_pairs={{3,0},{0,1},{1,2},{2,3},{7,4},{4,5},{5,6},{6,7},{9,8},{10,9},{11,1... | collective-permute-start | bytes 1572872 | tf_op jit(solution)/shard_map/ppermute | solution.py:373
  41.0 0.0 collective-permute-done.7.refs_2_.refs_0_
  41.0 1.7 %all-to-all-done.near_ref = bf16[32,40,128]{2,1,0:T(8,128)(2,1)S(1)} async-done(((bf16[32,40,128]{2,1,0:T(8,128)(2,1)}), bf16[32,40,128]{2,1,0:T(8,128)(2,1)S(1)}, u32[]{:S(2)}, u32[]{:S(2)}) %all-to-all-start) | async-done | bytes 327712 | tf_op jit(solution)/shard_map/all_to_all | solution.py:382
  42.6 8.8 %collective-permute-start.5 = (bf16[32,40,128]{2,1,0:T(8,128)(2,1)S(1)}, bf16[32,40,128]{2,1,0:T(8,128)(2,1)S(1)}, u32[]{:S(2)}, u32[]{:S(2)}) collective-permute-start(bf16[32,40,128]{2,1,0:T(8,128)(2,1)S(1)} %all-to-all-done.near_ref), channel_id=1, source_target_pairs={{0,8},{8,0},{16,24},{24,16},{32,40},{40,32},{48,56},{56,48},{64,72... | collective-permute-start | bytes 983048 | tf_op jit(solution)/shard_map/ppermute | solution.py:383
  51.5 1.3 %inverse.1.inverse_ref = s32[64]{0:T(128)} custom-call(s32[64]{0:T(128)} %lookup_ref.1), custom_call_target="tpu_custom_call" | custom-call | flops 8000000000 | tf_op jit(solution)/shard_map/inverse/pallas_call | solution.py:106
  52.7 0.0 collective-permute-done.6.refs_0_
  52.7 0.0 collective-permute-done.5.far_ref
  52.7 5.8 %low_begin.1 = (bf16[32,8192]{1,0:T(8,128)(2,1)S(1)}, f32[256,32]{1,0:T(8,128)S(1)}, bf16[256,128]{1,0:T(8,128)(2,1)}, f32[256,256]{1,0:T(8,128)}) custom-call(s32[64]{0:T(128)} %inverse.1.inverse_ref, s32[3]{0:T(128)S(1)} %pad_add_fusion.own_ref, bf16[32,40,128]{2,1,0:T(8,128)(2,1)S(1)} %all-to-all-done.near_ref, ...), custom_call_target="tpu_custom_call" | custom-call | tf_op jit(solution)/shard_map/low_begin/pallas_call | solution.py:188
  58.5 0.0 collective-permute-done.3.refs_3_.refs_1_
  58.5 0.0 collective-permute-done.4.refs_4_.refs_2_
  58.6 0.0 collective-permute-done.1.refs_2_.refs_0_
  58.6 1.8 %low_end.1 = bf16[8,32,256]{2,1,0:T(8,128)(2,1)} custom-call(s32[3]{0:T(128)S(1)} %pad_add_fusion.own_ref, bf16[32,8192]{1,0:T(8,128)(2,1)S(1)} %get-tuple-element.30.down_ref, f32[256,32]{1,0:T(8,128)S(1)} %get-tuple-element.31.begun_ref, bf16[256,1024]{1,0:T(8,128)(2,1)S(1)} %collective-permute-done.1.refs_2_.refs_0_, ...), custom_call_target="tpu_custom_call" | custom-call | tf_op jit(solution)/shard_map/low_end/pallas_call | solution.py:226
  60.4 3.4 %all-to-all-start.1 = ((bf16[8,32,256]{2,1,0:T(8,128)(2,1)}), bf16[8,32,256]{2,1,0:T(8,128)(2,1)S(1)}, u32[]{:S(2)}, u32[]{:S(2)}) async-start(bf16[8,32,256]{2,1,0:T(8,128)(2,1)} %low_end.1), calls=%async_computation.1 | async-start | bytes 262144 | tf_op jit(solution)/shard_map/all_to_all | solution.py:399
  63.7 4.7 %project.1.made_ref = f32[256,640]{1,0:T(8,128)S(1)} custom-call(s32[3]{0:T(128)S(1)} %pad_add_fusion.own_ref, s32[1,8]{1,0:T(1,128)} %lengths_ref.1, bf16[16384,128]{1,0:T(8,128)(2,1)} %bitcast.13, bf16[256,128]{1,0:T(8,128)(2,1)} %get-tuple-element.25.up_ref, f32[256,256]{1,0:T(8,128)} %get-tuple-element.26.begun_ref, f32[1,128]{1,0:T(1,128)} %constant.45.clone.rate_ref, ...), custom_call_target="tpu_custom_call" | custom-call | tf_op jit(solution)/shard_map/project/pallas_call | solution.py:277
  68.4 0.7 all-to-all-done.1
  69.1 0.5 finish.1
  69.6 23.5 %all_to_all.19 = bf16[64,16,128]{2,1,0:T(8,128)(2,1)S(1)} all-to-all(bf16[64,16,128]{2,1,0:T(8,128)(2,1)S(1)} %bitcast.10), channel_id=1, replica_groups=mesh['rollout'=64,'tensor'=8] {'rollout'}, dimensions={0} | all-to-all | bytes 524288 | tf_op jit(solution)/shard_map/all_to_all | solution.py:402
  93.1 0.7 copy.11
Async XLA Ops:
  0.0 34.4 %collective-permute-start.2 = (bf16[256,1024]{1,0:T(8,128)(2,1)}, bf16[256,1024]{1,0:T(8,128)(2,1)S(1)}, u32[]{:S(2)}, u32[]{:S(2)}) collective-permute-start(bf16[256,1024]{1,0:T(8,128)(2,1)} %tokens_ref.1), channel_id=1, source_target_pairs={{0,4},{1,5},{2,6},{3,7},{4,0},{5,1},{6,2},{7,3},{8,12},{9,13},{10,... | collective-permute-start | bytes 1572872 | tf_op jit(solution)/shard_map/ppermute | solution.py:376
  4.0 27.4 %collective-permute-start = (bf16[256,1024]{1,0:T(8,128)(2,1)}, bf16[256,1024]{1,0:T(8,128)(2,1)}, u32[]{:S(2)}, u32[]{:S(2)}) collective-permute-start(bf16[256,1024]{1,0:T(8,128)(2,1)} %tokens_ref.1), channel_id=1, source_target_pairs={{2,0},{3,1},{0,2},{1,3},{6,4},{7,5},{4,6},{5,7},{10,8},{11,9},{8,1... | collective-permute-start | bytes 1572872 | tf_op jit(solution)/shard_map/ppermute | solution.py:373
  8.7 32.3 %collective-permute-start.7 = (bf16[256,1024]{1,0:T(8,128)(2,1)}, bf16[256,1024]{1,0:T(8,128)(2,1)S(1)}, u32[]{:S(2)}, u32[]{:S(2)}) collective-permute-start(bf16[256,1024]{1,0:T(8,128)(2,1)} %tokens_ref.1), channel_id=1, source_target_pairs={{3,0},{0,1},{1,2},{2,3},{7,4},{4,5},{5,6},{6,7},{9,8},{10,9},{11,1... | collective-permute-start | bytes 1572872 | tf_op jit(solution)/shard_map/ppermute | solution.py:373
  11.5 41.3 %collective-permute-start.6 = (bf16[256,1024]{1,0:T(8,128)(2,1)}, bf16[256,1024]{1,0:T(8,128)(2,1)}, u32[]{:S(2)}, u32[]{:S(2)}) collective-permute-start(bf16[256,1024]{1,0:T(8,128)(2,1)} %tokens_ref.1), channel_id=1, source_target_pairs={{1,0},{2,1},{3,2},{0,3},{5,4},{6,5},{7,6},{4,7},{11,8},{8,9},{9,10... | collective-permute-start | bytes 1572872 | tf_op jit(solution)/shard_map/ppermute | solution.py:373
  15.8 26.8 %all-to-all-start = ((bf16[32,40,128]{2,1,0:T(8,128)(2,1)}), bf16[32,40,128]{2,1,0:T(8,128)(2,1)S(1)}, u32[]{:S(2)}, u32[]{:S(2)}) async-start(bf16[32,40,128]{2,1,0:T(8,128)(2,1)} %share.1), calls=%async_computation | async-start | bytes 655360 | tf_op jit(solution)/shard_map/all_to_all | solution.py:382
  31.4 27.1 %collective-permute-start.1 = (bf16[256,1024]{1,0:T(8,128)(2,1)}, bf16[256,1024]{1,0:T(8,128)(2,1)S(1)}, u32[]{:S(2)}, u32[]{:S(2)}) collective-permute-start(bf16[256,1024]{1,0:T(8,128)(2,1)} %collective-permute-done.refs_1_), channel_id=1, source_target_pairs={{0,4},{1,5},{2,6},{3,7},{4,0},{5,1},{6,2},{7,3},{8,12},{9,13},{10,... | collective-permute-start | bytes 1572872 | tf_op jit(solution)/shard_map/ppermute | solution.py:376
  34.5 24.1 %collective-permute-start.3 = (bf16[256,1024]{1,0:T(8,128)(2,1)S(1)}, bf16[256,1024]{1,0:T(8,128)(2,1)S(1)}, u32[]{:S(2)}, u32[]{:S(2)}) collective-permute-start(bf16[256,1024]{1,0:T(8,128)(2,1)S(1)} %collective-permute-done.2.refs_3_.refs_1_), channel_id=1, source_target_pairs={{1,0},{2,1},{3,2},{0,3},{5,4},{6,5},{7,6},{4,7},{11,8},{8,9},{9,10... | collective-permute-start | bytes 1572872 | tf_op jit(solution)/shard_map/ppermute | solution.py:373
  36.7 21.9 %collective-permute-start.4 = (bf16[256,1024]{1,0:T(8,128)(2,1)S(1)}, bf16[256,1024]{1,0:T(8,128)(2,1)S(1)}, u32[]{:S(2)}, u32[]{:S(2)}) collective-permute-start(bf16[256,1024]{1,0:T(8,128)(2,1)S(1)} %collective-permute-done.2.refs_3_.refs_1_), channel_id=1, source_target_pairs={{3,0},{0,1},{1,2},{2,3},{7,4},{4,5},{5,6},{6,7},{9,8},{10,9},{11,1... | collective-permute-start | bytes 1572872 | tf_op jit(solution)/shard_map/ppermute | solution.py:373
  42.6 10.1 %collective-permute-start.5 = (bf16[32,40,128]{2,1,0:T(8,128)(2,1)S(1)}, bf16[32,40,128]{2,1,0:T(8,128)(2,1)S(1)}, u32[]{:S(2)}, u32[]{:S(2)}) collective-permute-start(bf16[32,40,128]{2,1,0:T(8,128)(2,1)S(1)} %all-to-all-done.near_ref), channel_id=1, source_target_pairs={{0,8},{8,0},{16,24},{24,16},{32,40},{40,32},{48,56},{56,48},{64,72... | collective-permute-start | bytes 983048 | tf_op jit(solution)/shard_map/ppermute | solution.py:383
  60.4 8.7 %all-to-all-start.1 = ((bf16[8,32,256]{2,1,0:T(8,128)(2,1)}), bf16[8,32,256]{2,1,0:T(8,128)(2,1)S(1)}, u32[]{:S(2)}, u32[]{:S(2)}) async-start(bf16[8,32,256]{2,1,0:T(8,128)(2,1)} %low_end.1), calls=%async_computation.1 | async-start | bytes 262144 | tf_op jit(solution)/shard_map/all_to_all | solution.py:399

commit v7 on v6

--- a/solution.py
+++ b/solution.py
@@ -97,21 +97,30 @@
     return (own_ref[0] + place // X) % 2 * X + x
 
 
-def inverse_kernel(lookup_ref, inverse_ref):
+def places_kernel(lookup_ref, routes_ref, inverse_ref, slot_ref):
     for owner in range(GROUPS):
         inverse_ref[lookup_ref[owner]] = owner
-
-
-def inverse_of(lookup):
-    return pl.pallas_call(
-        inverse_kernel,
-        out_shape=pltpu.HBM((GROUPS,), jnp.int32),
-        in_specs=smem(1),
-        out_specs=smem(1)[0],
+    target = routes_ref[...]
+    later = jnp.broadcast_to(target.astype(jnp.float32), (ROWS, ROWS))
+    below = lax.broadcasted_iota(jnp.int32, (ROWS, ROWS), 0)
+    after = lax.broadcasted_iota(jnp.int32, (ROWS, ROWS), 1)
+    same = jnp.where((later.T == later) & (below < after), 1, 0)
+    slot_ref[...] = target * CAP + jnp.sum(same, axis=0, keepdims=True)
+
+
+def places_of(lookup, routes):
+    return pl.pallas_call(
+        places_kernel,
+        out_shape=(
+            pltpu.HBM((GROUPS,), jnp.int32),
+            jax.ShapeDtypeStruct((1, ROWS), jnp.int32),
+        ),
+        in_specs=smem(1) + vmem(1),
+        out_specs=(smem(1)[0], vmem(1)[0]),
         cost_estimate=BESIDE,
         compiler_params=pltpu.CompilerParams(vmem_limit_bytes=VMEM_LIMIT),
-        name="inverse",
-    )(in_hbm(lookup))
+        name="places",
+    )(in_hbm(lookup), in_hbm(routes.reshape(1, ROWS)))
 
 
 def low_part(own_ref, blocks, down_ref, places):
@@ -271,9 +280,7 @@
     out_ref[:, HEAD:WIDE] = total[:, HEAD:] + bias_ref[1:2, :].astype(jnp.float32)
 
 
-def project(own, lengths, blocks, places, weight_rows, up, begun, bias):
-    half_rate = rope_base ** (-(np.arange(HEAD // 2, dtype=np.float32) * 2.0) / HEAD)
-    rate = jnp.asarray(np.concatenate([half_rate, half_rate])[None], jnp.float32)
+def project(own, lengths, rate, blocks, places, weight_rows, up, begun, bias):
     return pl.pallas_call(
         functools.partial(project_kernel, places),
         out_shape=jax.ShapeDtypeStruct((ROWS, 2 * WIDE + HEAD), jnp.float32),
@@ -340,25 +347,21 @@
     )(made, low, slots)
 
 
-def slots_kernel(routes_ref, slot_ref):
-    target = routes_ref[...]
-    later = jnp.broadcast_to(target.astype(jnp.float32), (ROWS, ROWS))
-    below = lax.broadcasted_iota(jnp.int32, (ROWS, ROWS), 0)
-    after = lax.broadcasted_iota(jnp.int32, (ROWS, ROWS), 1)
-    same = jnp.where((later.T == later) & (below < after), 1, 0)
-    slot_ref[...] = target * CAP + jnp.sum(same, axis=0, keepdims=True)
-
-
-def slots_of(routes):
-    return pl.pallas_call(
-        slots_kernel,
-        out_shape=jax.ShapeDtypeStruct((1, ROWS), jnp.int32),
-        in_specs=vmem(1),
+def rate_kernel(rate_ref):
+    lane = lax.broadcasted_iota(jnp.int32, (1, HEAD), 1) % (HEAD // 2)
+    rate_ref[...] = jnp.exp(lane.astype(jnp.float32) * np.float32(-2.0 * np.log(rope_base) / HEAD))
+
+
+def rates():
+    return pl.pallas_call(
+        rate_kernel,
+        out_shape=pltpu.HBM((1, HEAD), jnp.float32),
+        in_specs=[],
         out_specs=vmem(1)[0],
         cost_estimate=BESIDE,
         compiler_params=pltpu.CompilerParams(vmem_limit_bytes=VMEM_LIMIT),
-        name="slots",
-    )(in_hbm(routes.reshape(1, ROWS)))
+        name="rate",
+    )()
 
 
 def body(tokens, weight, bias, down_blocks, up_blocks, lookup, lengths, routes):
@@ -382,14 +385,15 @@
     near = lax.all_to_all(sent, "rollout", 0, 0, tiled=True, axis_index_groups=SAME_CORE)
     far = lax.ppermute(near, "rollout", SIBLING)
 
-    slots = slots_of(routes)
-    far_x, slots = lax.optimization_barrier((far_x, slots))
+    rate = rates()
+    far_x, rate = lax.optimization_barrier((far_x, rate))
+    inverse, slots = places_of(lookup, routes)
     met_far = across_y(far_x)
     met_next, met_last = along_x(met, 1), along_x(met, 3)
     blocks = [tokens, next_x, far_x, last_x, met, met_next, met_far, met_last]
     early, late = (1, 2, 3, 4, 0), (6, 5, 7)
     down, begun, up, started = low_begin(
-        inverse_of(lookup), own, near, far, weight_rows, blocks, early
+        inverse, own, near, far, weight_rows, blocks, early
     )
     met_far, met_next, met_last, down, begun, up, started, slots = lax.optimization_barrier(
         (met_far, met_next, met_last, down, begun, up, started, slots)
@@ -397,7 +401,7 @@
     blocks[5:] = [met_next, met_far, met_last]
     low = low_end(own, down, begun, blocks, late)
     low_all = lax.all_to_all(low, "tensor", 0, 0, tiled=True).reshape(2 * RANK, ROWS)
-    made = project(own, lengths, blocks, REST, weight_rows, up, started, bias)
+    made = project(own, lengths, rate, blocks, REST, weight_rows, up, started, bias)
     outgoing = finish(made, low_all, slots)
     arrived = lax.all_to_all(outgoing, "rollout", 0, 0, tiled=True)
     return arrived.reshape(GROUPS * CAP, 2, HEAD)

time: 94.5 us -> 94.2 us (level)
  no operation moved by 1% of the time
where the time goes in v7:
time: 94.2 us; the launch traced here: 93.5 us
  starting transfers between devices  50.4 us (54%)
  blocking collectives  23.2 us (25%)
  Pallas kernels  16.3 us (17%)
  waiting for transfers between devices  2.64 us (3%)
    all_to_all x1, blocking collectives, body(): arrived = lax.all_to_all(outgoing, 'rollout', 0, 0, tiled=True)  23.2 us
    ppermute x5, starting transfers between devices, along_x(): return lax.ppermute(block, ('rollout', 'tensor'), X_HOP[hop])  16.4 us
    all_to_all x1, starting transfers between devices, body(): lax.all_to_all(sent, 'rollout', 0, 0, tiled=True, axis_index_groups=SAME_...  14.8 us
    ppermute x1, starting transfers between devices, body(): far = lax.ppermute(near, 'rollout', SIBLING)  8.8 us
    ppermute x2, starting transfers between devices, across_y(): return lax.ppermute(block, 'tensor', Y_PARTNER)  7.01 us
    pallas_call x1, Pallas kernels, low_begin(): pl.pallas_call(functools.partial(low_begin_kernel, places), out_shape=(ja...  5.78 us
    pallas_call x1, Pallas kernels, project(): pl.pallas_call(functools.partial(project_kernel, places), out_shape=jax.S...  4.69 us
    all_to_all x1, starting transfers between devices, body(): lax.all_to_all(low, 'tensor', 0, 0, tiled=True).reshape(2 * RANK, ROWS)  3.37 us
  transfers between devices with their start and end apart: 10, of which 2 were waited for; matrix products, arithmetic and copies ran while one was open for 0% of the time, Pallas kernels for 15%

profile of v7, /device:TPU:1, one launch (start us, length us, event | category | flops | bytes accessed | tf_op | source)
XLA Modules:
  0.0 93.5 jit_solution(13385970694549101967)
XLA Ops:
  0.0 4.0 %collective-permute-start.2 = (bf16[256,1024]{1,0:T(8,128)(2,1)}, bf16[256,1024]{1,0:T(8,128)(2,1)S(1)}, u32[]{:S(2)}, u32[]{:S(2)}) collective-permute-start(bf16[256,1024]{1,0:T(8,128)(2,1)} %tokens_ref.1), channel_id=1, source_target_pairs={{0,4},{1,5},{2,6},{3,7},{4,0},{5,1},{6,2},{7,3},{8,12},{9,13},{10,... | collective-permute-start | bytes 1572872 | tf_op jit(solution)/shard_map/ppermute | solution.py:379
  4.0 4.7 %collective-permute-start = (bf16[256,1024]{1,0:T(8,128)(2,1)}, bf16[256,1024]{1,0:T(8,128)(2,1)}, u32[]{:S(2)}, u32[]{:S(2)}) collective-permute-start(bf16[256,1024]{1,0:T(8,128)(2,1)} %tokens_ref.1), channel_id=1, source_target_pairs={{2,0},{3,1},{0,2},{1,3},{6,4},{7,5},{4,6},{5,7},{10,8},{11,9},{8,1... | collective-permute-start | bytes 1572872 | tf_op jit(solution)/shard_map/ppermute | solution.py:376
  8.7 2.8 %collective-permute-start.7 = (bf16[256,1024]{1,0:T(8,128)(2,1)}, bf16[256,1024]{1,0:T(8,128)(2,1)S(1)}, u32[]{:S(2)}, u32[]{:S(2)}) collective-permute-start(bf16[256,1024]{1,0:T(8,128)(2,1)} %tokens_ref.1), channel_id=1, source_target_pairs={{3,0},{0,1},{1,2},{2,3},{7,4},{4,5},{5,6},{6,7},{9,8},{10,9},{11,1... | collective-permute-start | bytes 1572872 | tf_op jit(solution)/shard_map/ppermute | solution.py:376
  11.5 2.5 %collective-permute-start.6 = (bf16[256,1024]{1,0:T(8,128)(2,1)}, bf16[256,1024]{1,0:T(8,128)(2,1)}, u32[]{:S(2)}, u32[]{:S(2)}) collective-permute-start(bf16[256,1024]{1,0:T(8,128)(2,1)} %tokens_ref.1), channel_id=1, source_target_pairs={{1,0},{2,1},{3,2},{0,3},{5,4},{6,5},{7,6},{4,7},{11,8},{8,9},{9,10... | collective-permute-start | bytes 1572872 | tf_op jit(solution)/shard_map/ppermute | solution.py:376
  14.0 0.1 pad_add_fusion.own_ref
  14.1 1.7 %share.1 = bf16[32,40,128]{2,1,0:T(8,128)(2,1)} custom-call(s32[3]{0:T(128)S(1)} %pad_add_fusion.own_ref, bf16[256,128]{1,0:T(8,128)(2,1)} %bitcast.15, bf16[4,128]{1,0:T(4,128)(2,1)} %bitcast.16), custom_call_target="tpu_custom_call" | custom-call | tf_op jit(solution)/shard_map/share/pallas_call | solution.py:81
  15.8 14.8 %all-to-all-start = ((bf16[32,40,128]{2,1,0:T(8,128)(2,1)}), bf16[32,40,128]{2,1,0:T(8,128)(2,1)S(1)}, u32[]{:S(2)}, u32[]{:S(2)}) async-start(bf16[32,40,128]{2,1,0:T(8,128)(2,1)} %share.1), calls=%async_computation | async-start | bytes 655360 | tf_op jit(solution)/shard_map/all_to_all | solution.py:385
  30.6 0.5 rate.1.rate_ref
  31.2 0.0 collective-permute-done.refs_1_
  31.2 3.0 %collective-permute-start.1 = (bf16[256,1024]{1,0:T(8,128)(2,1)}, bf16[256,1024]{1,0:T(8,128)(2,1)S(1)}, u32[]{:S(2)}, u32[]{:S(2)}) collective-permute-start(bf16[256,1024]{1,0:T(8,128)(2,1)} %collective-permute-done.refs_1_), channel_id=1, source_target_pairs={{0,4},{1,5},{2,6},{3,7},{4,0},{5,1},{6,2},{7,3},{8,12},{9,13},{10,... | collective-permute-start | bytes 1572872 | tf_op jit(solution)/shard_map/ppermute | solution.py:379
  34.2 0.0 collective-permute-done.2.refs_3_.refs_1_
  34.2 2.2 %collective-permute-start.3 = (bf16[256,1024]{1,0:T(8,128)(2,1)S(1)}, bf16[256,1024]{1,0:T(8,128)(2,1)S(1)}, u32[]{:S(2)}, u32[]{:S(2)}) collective-permute-start(bf16[256,1024]{1,0:T(8,128)(2,1)S(1)} %collective-permute-done.2.refs_3_.refs_1_), channel_id=1, source_target_pairs={{1,0},{2,1},{3,2},{0,3},{5,4},{6,5},{7,6},{4,7},{11,8},{8,9},{9,10... | collective-permute-start | bytes 1572872 | tf_op jit(solution)/shard_map/ppermute | solution.py:376
  36.4 4.3 %collective-permute-start.4 = (bf16[256,1024]{1,0:T(8,128)(2,1)S(1)}, bf16[256,1024]{1,0:T(8,128)(2,1)S(1)}, u32[]{:S(2)}, u32[]{:S(2)}) collective-permute-start(bf16[256,1024]{1,0:T(8,128)(2,1)S(1)} %collective-permute-done.2.refs_3_.refs_1_), channel_id=1, source_target_pairs={{3,0},{0,1},{1,2},{2,3},{7,4},{4,5},{5,6},{6,7},{9,8},{10,9},{11,1... | collective-permute-start | bytes 1572872 | tf_op jit(solution)/shard_map/ppermute | solution.py:376
  40.7 0.0 collective-permute-done.7.refs_2_.refs_0_
  40.7 1.9 %all-to-all-done.near_ref = bf16[32,40,128]{2,1,0:T(8,128)(2,1)S(1)} async-done(((bf16[32,40,128]{2,1,0:T(8,128)(2,1)}), bf16[32,40,128]{2,1,0:T(8,128)(2,1)S(1)}, u32[]{:S(2)}, u32[]{:S(2)}) %all-to-all-start) | async-done | bytes 327712 | tf_op jit(solution)/shard_map/all_to_all | solution.py:385
  42.6 8.8 %collective-permute-start.5 = (bf16[32,40,128]{2,1,0:T(8,128)(2,1)S(1)}, bf16[32,40,128]{2,1,0:T(8,128)(2,1)S(1)}, u32[]{:S(2)}, u32[]{:S(2)}) collective-permute-start(bf16[32,40,128]{2,1,0:T(8,128)(2,1)S(1)} %all-to-all-done.near_ref), channel_id=1, source_target_pairs={{0,8},{8,0},{16,24},{24,16},{32,40},{40,32},{48,56},{56,48},{64,72... | collective-permute-start | bytes 983048 | tf_op jit(solution)/shard_map/ppermute | solution.py:386
  51.5 1.3 %places.1 = (s32[64]{0:T(128)}, s32[1,256]{1,0:T(1,128)S(1)}) custom-call(s32[64]{0:T(128)} %lookup_ref.1, s32[1,256]{1,0:T(1,128)} %bitcast.17), custom_call_target="tpu_custom_call" | custom-call | flops 8000000000 | tf_op jit(solution)/shard_map/places/pallas_call | solution.py:112
  52.7 0.0 collective-permute-done.6.refs_0_
  52.7 0.0 collective-permute-done.5.far_ref
  52.8 5.8 %low_begin.1 = (bf16[32,8192]{1,0:T(8,128)(2,1)S(1)}, f32[256,32]{1,0:T(8,128)S(1)}, bf16[256,128]{1,0:T(8,128)(2,1)}, f32[256,256]{1,0:T(8,128)}) custom-call(s32[64]{0:T(128)} %get-tuple-element.22.inverse_ref, s32[3]{0:T(128)S(1)} %pad_add_fusion.own_ref, bf16[32,40,128]{2,1,0:T(8,128)(2,1)S(1)} %all-to-all-done.near_ref, ...), custom_call_target="tpu_custom_call" | custom-call | tf_op jit(solution)/shard_map/low_begin/pallas_call | solution.py:197
  58.5 0.0 collective-permute-done.3.refs_3_.refs_1_
  58.6 0.0 collective-permute-done.4.refs_4_.refs_2_
  58.6 0.0 collective-permute-done.1.refs_2_.refs_0_
  58.6 1.8 %low_end.1 = bf16[8,32,256]{2,1,0:T(8,128)(2,1)} custom-call(s32[3]{0:T(128)S(1)} %pad_add_fusion.own_ref, bf16[32,8192]{1,0:T(8,128)(2,1)S(1)} %get-tuple-element.34.down_ref, f32[256,32]{1,0:T(8,128)S(1)} %get-tuple-element.35.begun_ref, bf16[256,1024]{1,0:T(8,128)(2,1)S(1)} %collective-permute-done.1.refs_2_.refs_0_, ...), custom_call_target="tpu_custom_call" | custom-call | tf_op jit(solution)/shard_map/low_end/pallas_call | solution.py:235
  60.4 3.4 %all-to-all-start.1 = ((bf16[8,32,256]{2,1,0:T(8,128)(2,1)}), bf16[8,32,256]{2,1,0:T(8,128)(2,1)S(1)}, u32[]{:S(2)}, u32[]{:S(2)}) async-start(bf16[8,32,256]{2,1,0:T(8,128)(2,1)} %low_end.1), calls=%async_computation.1 | async-start | bytes 262144 | tf_op jit(solution)/shard_map/all_to_all | solution.py:403
  63.8 4.7 %project.1.made_ref = f32[256,640]{1,0:T(8,128)S(1)} custom-call(s32[3]{0:T(128)S(1)} %pad_add_fusion.own_ref, s32[1,8]{1,0:T(1,128)} %lengths_ref.1, bf16[16384,128]{1,0:T(8,128)(2,1)} %bitcast.13, bf16[256,128]{1,0:T(8,128)(2,1)} %get-tuple-element.28.up_ref, f32[256,256]{1,0:T(8,128)} %get-tuple-element.29.begun_ref, f32[1,128]{1,0:T(1,128)} %rate.1.rate_ref, ...), custom_call_target="tpu_custom_call" | custom-call | tf_op jit(solution)/shard_map/project/pallas_call | solution.py:284
  68.5 0.7 all-to-all-done.1
  69.1 0.5 finish.1
  69.6 23.2 %all_to_all.19 = bf16[64,16,128]{2,1,0:T(8,128)(2,1)S(1)} all-to-all(bf16[64,16,128]{2,1,0:T(8,128)(2,1)S(1)} %bitcast.10), channel_id=1, replica_groups=mesh['rollout'=64,'tensor'=8] {'rollout'}, dimensions={0} | all-to-all | bytes 524288 | tf_op jit(solution)/shard_map/all_to_all | solution.py:406
  92.8 0.7 copy.10
Async XLA Ops:
  0.0 34.2 %collective-permute-start.2 = (bf16[256,1024]{1,0:T(8,128)(2,1)}, bf16[256,1024]{1,0:T(8,128)(2,1)S(1)}, u32[]{:S(2)}, u32[]{:S(2)}) collective-permute-start(bf16[256,1024]{1,0:T(8,128)(2,1)} %tokens_ref.1), channel_id=1, source_target_pairs={{0,4},{1,5},{2,6},{3,7},{4,0},{5,1},{6,2},{7,3},{8,12},{9,13},{10,... | collective-permute-start | bytes 1572872 | tf_op jit(solution)/shard_map/ppermute | solution.py:379
  4.0 27.1 %collective-permute-start = (bf16[256,1024]{1,0:T(8,128)(2,1)}, bf16[256,1024]{1,0:T(8,128)(2,1)}, u32[]{:S(2)}, u32[]{:S(2)}) collective-permute-start(bf16[256,1024]{1,0:T(8,128)(2,1)} %tokens_ref.1), channel_id=1, source_target_pairs={{2,0},{3,1},{0,2},{1,3},{6,4},{7,5},{4,6},{5,7},{10,8},{11,9},{8,1... | collective-permute-start | bytes 1572872 | tf_op jit(solution)/shard_map/ppermute | solution.py:376
  8.7 32.0 %collective-permute-start.7 = (bf16[256,1024]{1,0:T(8,128)(2,1)}, bf16[256,1024]{1,0:T(8,128)(2,1)S(1)}, u32[]{:S(2)}, u32[]{:S(2)}) collective-permute-start(bf16[256,1024]{1,0:T(8,128)(2,1)} %tokens_ref.1), channel_id=1, source_target_pairs={{3,0},{0,1},{1,2},{2,3},{7,4},{4,5},{5,6},{6,7},{9,8},{10,9},{11,1... | collective-permute-start | bytes 1572872 | tf_op jit(solution)/shard_map/ppermute | solution.py:376
  11.5 41.3 %collective-permute-start.6 = (bf16[256,1024]{1,0:T(8,128)(2,1)}, bf16[256,1024]{1,0:T(8,128)(2,1)}, u32[]{:S(2)}, u32[]{:S(2)}) collective-permute-start(bf16[256,1024]{1,0:T(8,128)(2,1)} %tokens_ref.1), channel_id=1, source_target_pairs={{1,0},{2,1},{3,2},{0,3},{5,4},{6,5},{7,6},{4,7},{11,8},{8,9},{9,10... | collective-permute-start | bytes 1572872 | tf_op jit(solution)/shard_map/ppermute | solution.py:376
  15.8 26.8 %all-to-all-start = ((bf16[32,40,128]{2,1,0:T(8,128)(2,1)}), bf16[32,40,128]{2,1,0:T(8,128)(2,1)S(1)}, u32[]{:S(2)}, u32[]{:S(2)}) async-start(bf16[32,40,128]{2,1,0:T(8,128)(2,1)} %share.1), calls=%async_computation | async-start | bytes 655360 | tf_op jit(solution)/shard_map/all_to_all | solution.py:385
  31.2 27.4 %collective-permute-start.1 = (bf16[256,1024]{1,0:T(8,128)(2,1)}, bf16[256,1024]{1,0:T(8,128)(2,1)S(1)}, u32[]{:S(2)}, u32[]{:S(2)}) collective-permute-start(bf16[256,1024]{1,0:T(8,128)(2,1)} %collective-permute-done.refs_1_), channel_id=1, source_target_pairs={{0,4},{1,5},{2,6},{3,7},{4,0},{5,1},{6,2},{7,3},{8,12},{9,13},{10,... | collective-permute-start | bytes 1572872 | tf_op jit(solution)/shard_map/ppermute | solution.py:379
  34.2 24.4 %collective-permute-start.3 = (bf16[256,1024]{1,0:T(8,128)(2,1)S(1)}, bf16[256,1024]{1,0:T(8,128)(2,1)S(1)}, u32[]{:S(2)}, u32[]{:S(2)}) collective-permute-start(bf16[256,1024]{1,0:T(8,128)(2,1)S(1)} %collective-permute-done.2.refs_3_.refs_1_), channel_id=1, source_target_pairs={{1,0},{2,1},{3,2},{0,3},{5,4},{6,5},{7,6},{4,7},{11,8},{8,9},{9,10... | collective-permute-start | bytes 1572872 | tf_op jit(solution)/shard_map/ppermute | solution.py:376
  36.4 22.2 %collective-permute-start.4 = (bf16[256,1024]{1,0:T(8,128)(2,1)S(1)}, bf16[256,1024]{1,0:T(8,128)(2,1)S(1)}, u32[]{:S(2)}, u32[]{:S(2)}) collective-permute-start(bf16[256,1024]{1,0:T(8,128)(2,1)S(1)} %collective-permute-done.2.refs_3_.refs_1_), channel_id=1, source_target_pairs={{3,0},{0,1},{1,2},{2,3},{7,4},{4,5},{5,6},{6,7},{9,8},{10,9},{11,1... | collective-permute-start | bytes 1572872 | tf_op jit(solution)/shard_map/ppermute | solution.py:376
  42.6 10.1 %collective-permute-start.5 = (bf16[32,40,128]{2,1,0:T(8,128)(2,1)S(1)}, bf16[32,40,128]{2,1,0:T(8,128)(2,1)S(1)}, u32[]{:S(2)}, u32[]{:S(2)}) collective-permute-start(bf16[32,40,128]{2,1,0:T(8,128)(2,1)S(1)} %all-to-all-done.near_ref), channel_id=1, source_target_pairs={{0,8},{8,0},{16,24},{24,16},{32,40},{40,32},{48,56},{56,48},{64,72... | collective-permute-start | bytes 983048 | tf_op jit(solution)/shard_map/ppermute | solution.py:386
  60.4 8.7 %all-to-all-start.1 = ((bf16[8,32,256]{2,1,0:T(8,128)(2,1)}), bf16[8,32,256]{2,1,0:T(8,128)(2,1)S(1)}, u32[]{:S(2)}, u32[]{:S(2)}) async-start(bf16[8,32,256]{2,1,0:T(8,128)(2,1)} %low_end.1), calls=%async_computation.1 | async-start | bytes 262144 | tf_op jit(solution)/shard_map/all_to_all | solution.py:403

commit v8 on v7

--- a/solution.py
+++ b/solution.py
@@ -42,7 +42,7 @@
 
 
 VMEM_LIMIT = 16 * 1024 * 1024
-BUFFERS = 4
+BUFFERS = 5
 FIRST = (1, 2, 0)
 REST = (3, 4, 6, 5, 7)
 
@@ -207,9 +207,9 @@
         scratch_shapes=[
             pltpu.VMEM((2 * RANK, HEAD), jnp.float32),
             pltpu.VMEM((ROWS, BLOCK), jnp.bfloat16),
-            pltpu.VMEM((BUFFERS, 2 * BLOCK, HEAD), jnp.bfloat16),
+            pltpu.VMEM((len(FIRST), 2 * BLOCK, HEAD), jnp.bfloat16),
             pltpu.SemaphoreType.DMA,
-            pltpu.SemaphoreType.DMA((BUFFERS,)),
+            pltpu.SemaphoreType.DMA((len(FIRST),)),
         ],
         compiler_params=pltpu.CompilerParams(vmem_limit_bytes=VMEM_LIMIT),
         name="low_begin",

time: 94.2 us -> 94.2 us (level)
  no operation moved by 1% of the time
where the time goes in v8:
time: 94.2 us; the launch traced here: 93.5 us
  starting transfers between devices  50.4 us (54%)
  blocking collectives  23.2 us (25%)
  Pallas kernels  15.9 us (17%)
  waiting for transfers between devices  3.04 us (3%)
    all_to_all x1, blocking collectives, body(): arrived = lax.all_to_all(outgoing, 'rollout', 0, 0, tiled=True)  23.2 us
    ppermute x5, starting transfers between devices, along_x(): return lax.ppermute(block, ('rollout', 'tensor'), X_HOP[hop])  16.4 us
    all_to_all x1, starting transfers between devices, body(): lax.all_to_all(sent, 'rollout', 0, 0, tiled=True, axis_index_groups=SAME_...  14.8 us
    ppermute x1, starting transfers between devices, body(): far = lax.ppermute(near, 'rollout', SIBLING)  8.8 us
    ppermute x2, starting transfers between devices, across_y(): return lax.ppermute(block, 'tensor', Y_PARTNER)  7.01 us
    pallas_call x1, Pallas kernels, low_begin(): pl.pallas_call(functools.partial(low_begin_kernel, places), out_shape=(ja...  5.77 us
    pallas_call x1, Pallas kernels, project(): pl.pallas_call(functools.partial(project_kernel, places), out_shape=jax.S...  4.28 us
    all_to_all x1, starting transfers between devices, body(): lax.all_to_all(low, 'tensor', 0, 0, tiled=True).reshape(2 * RANK, ROWS)  3.37 us
  transfers between devices with their start and end apart: 10, of which 2 were waited for; matrix products, arithmetic and copies ran while one was open for 0% of the time, Pallas kernels for 15%

profile of v8, /device:TPU:1, one launch (start us, length us, event | category | flops | bytes accessed | tf_op | source)
XLA Modules:
  0.0 93.5 jit_solution(3433394636487945777)
XLA Ops:
  0.0 4.0 %collective-permute-start.2 = (bf16[256,1024]{1,0:T(8,128)(2,1)}, bf16[256,1024]{1,0:T(8,128)(2,1)S(1)}, u32[]{:S(2)}, u32[]{:S(2)}) collective-permute-start(bf16[256,1024]{1,0:T(8,128)(2,1)} %tokens_ref.1), channel_id=1, source_target_pairs={{0,4},{1,5},{2,6},{3,7},{4,0},{5,1},{6,2},{7,3},{8,12},{9,13},{10,... | collective-permute-start | bytes 1572872 | tf_op jit(solution)/shard_map/ppermute | solution.py:379
  4.0 4.7 %collective-permute-start = (bf16[256,1024]{1,0:T(8,128)(2,1)}, bf16[256,1024]{1,0:T(8,128)(2,1)}, u32[]{:S(2)}, u32[]{:S(2)}) collective-permute-start(bf16[256,1024]{1,0:T(8,128)(2,1)} %tokens_ref.1), channel_id=1, source_target_pairs={{2,0},{3,1},{0,2},{1,3},{6,4},{7,5},{4,6},{5,7},{10,8},{11,9},{8,1... | collective-permute-start | bytes 1572872 | tf_op jit(solution)/shard_map/ppermute | solution.py:376
  8.7 2.8 %collective-permute-start.7 = (bf16[256,1024]{1,0:T(8,128)(2,1)}, bf16[256,1024]{1,0:T(8,128)(2,1)S(1)}, u32[]{:S(2)}, u32[]{:S(2)}) collective-permute-start(bf16[256,1024]{1,0:T(8,128)(2,1)} %tokens_ref.1), channel_id=1, source_target_pairs={{3,0},{0,1},{1,2},{2,3},{7,4},{4,5},{5,6},{6,7},{9,8},{10,9},{11,1... | collective-permute-start | bytes 1572872 | tf_op jit(solution)/shard_map/ppermute | solution.py:376
  11.5 2.5 %collective-permute-start.6 = (bf16[256,1024]{1,0:T(8,128)(2,1)}, bf16[256,1024]{1,0:T(8,128)(2,1)}, u32[]{:S(2)}, u32[]{:S(2)}) collective-permute-start(bf16[256,1024]{1,0:T(8,128)(2,1)} %tokens_ref.1), channel_id=1, source_target_pairs={{1,0},{2,1},{3,2},{0,3},{5,4},{6,5},{7,6},{4,7},{11,8},{8,9},{9,10... | collective-permute-start | bytes 1572872 | tf_op jit(solution)/shard_map/ppermute | solution.py:376
  14.0 0.1 pad_add_fusion.own_ref
  14.1 1.7 %share.1 = bf16[32,40,128]{2,1,0:T(8,128)(2,1)} custom-call(s32[3]{0:T(128)S(1)} %pad_add_fusion.own_ref, bf16[256,128]{1,0:T(8,128)(2,1)} %bitcast.15, bf16[4,128]{1,0:T(4,128)(2,1)} %bitcast.16), custom_call_target="tpu_custom_call" | custom-call | tf_op jit(solution)/shard_map/share/pallas_call | solution.py:81
  15.8 14.8 %all-to-all-start = ((bf16[32,40,128]{2,1,0:T(8,128)(2,1)}), bf16[32,40,128]{2,1,0:T(8,128)(2,1)S(1)}, u32[]{:S(2)}, u32[]{:S(2)}) async-start(bf16[32,40,128]{2,1,0:T(8,128)(2,1)} %share.1), calls=%async_computation | async-start | bytes 655360 | tf_op jit(solution)/shard_map/all_to_all | solution.py:385
  30.6 0.5 rate.1.rate_ref
  31.2 0.0 collective-permute-done.refs_1_
  31.2 3.0 %collective-permute-start.1 = (bf16[256,1024]{1,0:T(8,128)(2,1)}, bf16[256,1024]{1,0:T(8,128)(2,1)S(1)}, u32[]{:S(2)}, u32[]{:S(2)}) collective-permute-start(bf16[256,1024]{1,0:T(8,128)(2,1)} %collective-permute-done.refs_1_), channel_id=1, source_target_pairs={{0,4},{1,5},{2,6},{3,7},{4,0},{5,1},{6,2},{7,3},{8,12},{9,13},{10,... | collective-permute-start | bytes 1572872 | tf_op jit(solution)/shard_map/ppermute | solution.py:379
  34.2 0.0 collective-permute-done.2.refs_3_.refs_1_
  34.2 2.2 %collective-permute-start.3 = (bf16[256,1024]{1,0:T(8,128)(2,1)S(1)}, bf16[256,1024]{1,0:T(8,128)(2,1)S(1)}, u32[]{:S(2)}, u32[]{:S(2)}) collective-permute-start(bf16[256,1024]{1,0:T(8,128)(2,1)S(1)} %collective-permute-done.2.refs_3_.refs_1_), channel_id=1, source_target_pairs={{1,0},{2,1},{3,2},{0,3},{5,4},{6,5},{7,6},{4,7},{11,8},{8,9},{9,10... | collective-permute-start | bytes 1572872 | tf_op jit(solution)/shard_map/ppermute | solution.py:376
  36.4 4.3 %collective-permute-start.4 = (bf16[256,1024]{1,0:T(8,128)(2,1)S(1)}, bf16[256,1024]{1,0:T(8,128)(2,1)S(1)}, u32[]{:S(2)}, u32[]{:S(2)}) collective-permute-start(bf16[256,1024]{1,0:T(8,128)(2,1)S(1)} %collective-permute-done.2.refs_3_.refs_1_), channel_id=1, source_target_pairs={{3,0},{0,1},{1,2},{2,3},{7,4},{4,5},{5,6},{6,7},{9,8},{10,9},{11,1... | collective-permute-start | bytes 1572872 | tf_op jit(solution)/shard_map/ppermute | solution.py:376
  40.7 0.0 collective-permute-done.7.refs_2_.refs_0_
  40.7 1.9 %all-to-all-done.near_ref = bf16[32,40,128]{2,1,0:T(8,128)(2,1)S(1)} async-done(((bf16[32,40,128]{2,1,0:T(8,128)(2,1)}), bf16[32,40,128]{2,1,0:T(8,128)(2,1)S(1)}, u32[]{:S(2)}, u32[]{:S(2)}) %all-to-all-start) | async-done | bytes 327712 | tf_op jit(solution)/shard_map/all_to_all | solution.py:385
  42.6 8.8 %collective-permute-start.5 = (bf16[32,40,128]{2,1,0:T(8,128)(2,1)S(1)}, bf16[32,40,128]{2,1,0:T(8,128)(2,1)S(1)}, u32[]{:S(2)}, u32[]{:S(2)}) collective-permute-start(bf16[32,40,128]{2,1,0:T(8,128)(2,1)S(1)} %all-to-all-done.near_ref), channel_id=1, source_target_pairs={{0,8},{8,0},{16,24},{24,16},{32,40},{40,32},{48,56},{56,48},{64,72... | collective-permute-start | bytes 983048 | tf_op jit(solution)/shard_map/ppermute | solution.py:386
  51.5 1.3 %places.1 = (s32[64]{0:T(128)}, s32[1,256]{1,0:T(1,128)S(1)}) custom-call(s32[64]{0:T(128)} %lookup_ref.1, s32[1,256]{1,0:T(1,128)} %bitcast.17), custom_call_target="tpu_custom_call" | custom-call | flops 8000000000 | tf_op jit(solution)/shard_map/places/pallas_call | solution.py:112
  52.7 0.0 collective-permute-done.6.refs_0_
  52.7 0.0 collective-permute-done.5.far_ref
  52.8 5.8 %low_begin.1 = (bf16[32,8192]{1,0:T(8,128)(2,1)S(1)}, f32[256,32]{1,0:T(8,128)S(1)}, bf16[256,128]{1,0:T(8,128)(2,1)}, f32[256,256]{1,0:T(8,128)}) custom-call(s32[64]{0:T(128)} %get-tuple-element.22.inverse_ref, s32[3]{0:T(128)S(1)} %pad_add_fusion.own_ref, bf16[32,40,128]{2,1,0:T(8,128)(2,1)S(1)} %all-to-all-done.near_ref, ...), custom_call_target="tpu_custom_call" | custom-call | tf_op jit(solution)/shard_map/low_begin/pallas_call | solution.py:197
  58.5 0.0 collective-permute-done.3.refs_3_.refs_1_
  58.5 0.0 collective-permute-done.4.refs_4_.refs_2_
  58.6 0.0 collective-permute-done.1.refs_2_.refs_0_
  58.6 1.8 %low_end.1 = bf16[8,32,256]{2,1,0:T(8,128)(2,1)} custom-call(s32[3]{0:T(128)S(1)} %pad_add_fusion.own_ref, bf16[32,8192]{1,0:T(8,128)(2,1)S(1)} %get-tuple-element.34.down_ref, f32[256,32]{1,0:T(8,128)S(1)} %get-tuple-element.35.begun_ref, bf16[256,1024]{1,0:T(8,128)(2,1)S(1)} %collective-permute-done.1.refs_2_.refs_0_, ...), custom_call_target="tpu_custom_call" | custom-call | tf_op jit(solution)/shard_map/low_end/pallas_call | solution.py:235
  60.4 3.4 %all-to-all-start.1 = ((bf16[8,32,256]{2,1,0:T(8,128)(2,1)}), bf16[8,32,256]{2,1,0:T(8,128)(2,1)S(1)}, u32[]{:S(2)}, u32[]{:S(2)}) async-start(bf16[8,32,256]{2,1,0:T(8,128)(2,1)} %low_end.1), calls=%async_computation.1 | async-start | bytes 262144 | tf_op jit(solution)/shard_map/all_to_all | solution.py:403
  63.7 4.3 %project.1.made_ref = f32[256,640]{1,0:T(8,128)S(1)} custom-call(s32[3]{0:T(128)S(1)} %pad_add_fusion.own_ref, s32[1,8]{1,0:T(1,128)} %lengths_ref.1, bf16[16384,128]{1,0:T(8,128)(2,1)} %bitcast.13, bf16[256,128]{1,0:T(8,128)(2,1)} %get-tuple-element.28.up_ref, f32[256,256]{1,0:T(8,128)} %get-tuple-element.29.begun_ref, f32[1,128]{1,0:T(1,128)} %rate.1.rate_ref, ...), custom_call_target="tpu_custom_call" | custom-call | tf_op jit(solution)/shard_map/project/pallas_call | solution.py:284
  68.0 1.1 %all-to-all-done.1 = bf16[8,32,256]{2,1,0:T(8,128)(2,1)S(1)} async-done(((bf16[8,32,256]{2,1,0:T(8,128)(2,1)}), bf16[8,32,256]{2,1,0:T(8,128)(2,1)S(1)}, u32[]{:S(2)}, u32[]{:S(2)}) %all-to-all-start.1) | async-done | bytes 131104 | tf_op jit(solution)/shard_map/all_to_all | solution.py:403
  69.1 0.5 finish.1
  69.6 23.2 %all_to_all.19 = bf16[64,16,128]{2,1,0:T(8,128)(2,1)S(1)} all-to-all(bf16[64,16,128]{2,1,0:T(8,128)(2,1)S(1)} %bitcast.10), channel_id=1, replica_groups=mesh['rollout'=64,'tensor'=8] {'rollout'}, dimensions={0} | all-to-all | bytes 524288 | tf_op jit(solution)/shard_map/all_to_all | solution.py:406
  92.8 0.7 copy.10
Async XLA Ops:
  0.0 34.2 %collective-permute-start.2 = (bf16[256,1024]{1,0:T(8,128)(2,1)}, bf16[256,1024]{1,0:T(8,128)(2,1)S(1)}, u32[]{:S(2)}, u32[]{:S(2)}) collective-permute-start(bf16[256,1024]{1,0:T(8,128)(2,1)} %tokens_ref.1), channel_id=1, source_target_pairs={{0,4},{1,5},{2,6},{3,7},{4,0},{5,1},{6,2},{7,3},{8,12},{9,13},{10,... | collective-permute-start | bytes 1572872 | tf_op jit(solution)/shard_map/ppermute | solution.py:379
  4.0 27.1 %collective-permute-start = (bf16[256,1024]{1,0:T(8,128)(2,1)}, bf16[256,1024]{1,0:T(8,128)(2,1)}, u32[]{:S(2)}, u32[]{:S(2)}) collective-permute-start(bf16[256,1024]{1,0:T(8,128)(2,1)} %tokens_ref.1), channel_id=1, source_target_pairs={{2,0},{3,1},{0,2},{1,3},{6,4},{7,5},{4,6},{5,7},{10,8},{11,9},{8,1... | collective-permute-start | bytes 1572872 | tf_op jit(solution)/shard_map/ppermute | solution.py:376
  8.7 32.0 %collective-permute-start.7 = (bf16[256,1024]{1,0:T(8,128)(2,1)}, bf16[256,1024]{1,0:T(8,128)(2,1)S(1)}, u32[]{:S(2)}, u32[]{:S(2)}) collective-permute-start(bf16[256,1024]{1,0:T(8,128)(2,1)} %tokens_ref.1), channel_id=1, source_target_pairs={{3,0},{0,1},{1,2},{2,3},{7,4},{4,5},{5,6},{6,7},{9,8},{10,9},{11,1... | collective-permute-start | bytes 1572872 | tf_op jit(solution)/shard_map/ppermute | solution.py:376
  11.5 41.3 %collective-permute-start.6 = (bf16[256,1024]{1,0:T(8,128)(2,1)}, bf16[256,1024]{1,0:T(8,128)(2,1)}, u32[]{:S(2)}, u32[]{:S(2)}) collective-permute-start(bf16[256,1024]{1,0:T(8,128)(2,1)} %tokens_ref.1), channel_id=1, source_target_pairs={{1,0},{2,1},{3,2},{0,3},{5,4},{6,5},{7,6},{4,7},{11,8},{8,9},{9,10... | collective-permute-start | bytes 1572872 | tf_op jit(solution)/shard_map/ppermute | solution.py:376
  15.8 26.8 %all-to-all-start = ((bf16[32,40,128]{2,1,0:T(8,128)(2,1)}), bf16[32,40,128]{2,1,0:T(8,128)(2,1)S(1)}, u32[]{:S(2)}, u32[]{:S(2)}) async-start(bf16[32,40,128]{2,1,0:T(8,128)(2,1)} %share.1), calls=%async_computation | async-start | bytes 655360 | tf_op jit(solution)/shard_map/all_to_all | solution.py:385
  31.2 27.4 %collective-permute-start.1 = (bf16[256,1024]{1,0:T(8,128)(2,1)}, bf16[256,1024]{1,0:T(8,128)(2,1)S(1)}, u32[]{:S(2)}, u32[]{:S(2)}) collective-permute-start(bf16[256,1024]{1,0:T(8,128)(2,1)} %collective-permute-done.refs_1_), channel_id=1, source_target_pairs={{0,4},{1,5},{2,6},{3,7},{4,0},{5,1},{6,2},{7,3},{8,12},{9,13},{10,... | collective-permute-start | bytes 1572872 | tf_op jit(solution)/shard_map/ppermute | solution.py:379
  34.2 24.4 %collective-permute-start.3 = (bf16[256,1024]{1,0:T(8,128)(2,1)S(1)}, bf16[256,1024]{1,0:T(8,128)(2,1)S(1)}, u32[]{:S(2)}, u32[]{:S(2)}) collective-permute-start(bf16[256,1024]{1,0:T(8,128)(2,1)S(1)} %collective-permute-done.2.refs_3_.refs_1_), channel_id=1, source_target_pairs={{1,0},{2,1},{3,2},{0,3},{5,4},{6,5},{7,6},{4,7},{11,8},{8,9},{9,10... | collective-permute-start | bytes 1572872 | tf_op jit(solution)/shard_map/ppermute | solution.py:376
  36.4 22.1 %collective-permute-start.4 = (bf16[256,1024]{1,0:T(8,128)(2,1)S(1)}, bf16[256,1024]{1,0:T(8,128)(2,1)S(1)}, u32[]{:S(2)}, u32[]{:S(2)}) collective-permute-start(bf16[256,1024]{1,0:T(8,128)(2,1)S(1)} %collective-permute-done.2.refs_3_.refs_1_), channel_id=1, source_target_pairs={{3,0},{0,1},{1,2},{2,3},{7,4},{4,5},{5,6},{6,7},{9,8},{10,9},{11,1... | collective-permute-start | bytes 1572872 | tf_op jit(solution)/shard_map/ppermute | solution.py:376
  42.6 10.1 %collective-permute-start.5 = (bf16[32,40,128]{2,1,0:T(8,128)(2,1)S(1)}, bf16[32,40,128]{2,1,0:T(8,128)(2,1)S(1)}, u32[]{:S(2)}, u32[]{:S(2)}) collective-permute-start(bf16[32,40,128]{2,1,0:T(8,128)(2,1)S(1)} %all-to-all-done.near_ref), channel_id=1, source_target_pairs={{0,8},{8,0},{16,24},{24,16},{32,40},{40,32},{48,56},{56,48},{64,72... | collective-permute-start | bytes 983048 | tf_op jit(solution)/shard_map/ppermute | solution.py:386
  60.4 8.7 %all-to-all-start.1 = ((bf16[8,32,256]{2,1,0:T(8,128)(2,1)}), bf16[8,32,256]{2,1,0:T(8,128)(2,1)S(1)}, u32[]{:S(2)}, u32[]{:S(2)}) async-start(bf16[8,32,256]{2,1,0:T(8,128)(2,1)} %low_end.1), calls=%async_computation.1 | async-start | bytes 262144 | tf_op jit(solution)/shard_map/all_to_all | solution.py:403

commit v9 on v8

--- a/solution.py
+++ b/solution.py
@@ -97,9 +97,9 @@
     return (own_ref[0] + place // X) % 2 * X + x
 
 
-def places_kernel(lookup_ref, routes_ref, inverse_ref, slot_ref):
+def places_kernel(lookup_ref, routes_ref, shard_ref, slot_ref):
     for owner in range(GROUPS):
-        inverse_ref[lookup_ref[owner]] = owner
+        shard_ref[owner] = lookup_ref[owner]
     target = routes_ref[...]
     later = jnp.broadcast_to(target.astype(jnp.float32), (ROWS, ROWS))
     below = lax.broadcasted_iota(jnp.int32, (ROWS, ROWS), 0)
@@ -167,7 +167,7 @@
 
 
 def low_begin_kernel(
-    places, inverse_ref, own_ref, near_ref, far_ref, weight_ref, tokens_ref, *refs
+    places, shard_ref, own_ref, near_ref, far_ref, weight_ref, tokens_ref, *refs
 ):
     down_ref, begun_ref, up_ref, base_ref, up_rows, held, weights, done, weight_done = refs[
         len(places) - 1 :
@@ -178,13 +178,14 @@
     copy = pltpu.make_async_copy(tokens_ref, held, done)
     copy.start()
     core = own_ref[2]
-    for shard in range(GROUPS):
-        owner = inverse_ref[shard]
-        rows = jnp.where(owner % 2 == core, near_ref[owner // 2], far_ref[owner // 2])
-        down_ref[:, shard * 128 : (shard + 1) * 128] = rows[0:SLICE]
-        rows = rows[SLICE:SENT].astype(jnp.float32)
-        up_rows[2 * shard : 2 * shard + 2, :] = rows[0:2]
-        up_rows[RANK + 2 * shard : RANK + 2 * shard + 2, :] = rows[2:4]
+    for chip in range(GROUPS // 2):
+        for from_ref, owner in ((near_ref, 2 * chip + core), (far_ref, 2 * chip + 1 - core)):
+            shard = shard_ref[owner]
+            columns = pl.ds(pl.multiple_of(shard * 128, 128), 128)
+            down_ref[:, columns] = from_ref[chip, 0:SLICE, :]
+            rows = from_ref[chip, SLICE:SENT, :].astype(jnp.float32)
+            up_rows[pl.ds(2 * shard, 2), :] = rows[0:2]
+            up_rows[pl.ds(RANK + 2 * shard, 2), :] = rows[2:4]
     up_ref[...] = up_rows[...].astype(jnp.bfloat16)
     copy.wait()
     blocks = [*refs[: len(places) - 1], held]
@@ -193,7 +194,7 @@
     base_ref[...] = project_blocks(copies, firsts, weights)
 
 
-def low_begin(inverse, own, near, far, weight_rows, blocks, places):
+def low_begin(shards, own, near, far, weight_rows, blocks, places):
     return pl.pallas_call(
         functools.partial(low_begin_kernel, places),
         out_shape=(
@@ -214,7 +215,7 @@
         compiler_params=pltpu.CompilerParams(vmem_limit_bytes=VMEM_LIMIT),
         name="low_begin",
     )(
-        in_hbm(inverse),
+        in_hbm(shards),
         own,
         near,
         far,
@@ -387,13 +388,13 @@
 
     rate = rates()
     far_x, rate = lax.optimization_barrier((far_x, rate))
-    inverse, slots = places_of(lookup, routes)
+    shards, slots = places_of(lookup, routes)
     met_far = across_y(far_x)
     met_next, met_last = along_x(met, 1), along_x(met, 3)
     blocks = [tokens, next_x, far_x, last_x, met, met_next, met_far, met_last]
     early, late = (1, 2, 3, 4, 0), (6, 5, 7)
     down, begun, up, started = low_begin(
-        inverse, own, near, far, weight_rows, blocks, early
+        shards, own, near, far, weight_rows, blocks, early
     )
     met_far, met_next, met_last, down, begun, up, started, slots = lax.optimization_barrier(
         (met_far, met_next, met_last, down, begun, up, started, slots)

time: 94.2 us -> 94.2 us (level)
  no operation moved by 1% of the time
where the time goes in v9:
time: 94.2 us; the launch traced here: 93.5 us
  starting transfers between devices  50.4 us (54%)
  blocking collectives  23.3 us (25%)
  Pallas kernels  15.9 us (17%)
  waiting for transfers between devices  3.04 us (3%)
    all_to_all x1, blocking collectives, body(): arrived = lax.all_to_all(outgoing, 'rollout', 0, 0, tiled=True)  23.3 us
    ppermute x5, starting transfers between devices, along_x(): return lax.ppermute(block, ('rollout', 'tensor'), X_HOP[hop])  16.4 us
    all_to_all x1, starting transfers between devices, body(): lax.all_to_all(sent, 'rollout', 0, 0, tiled=True, axis_index_groups=SAME_...  14.8 us
    ppermute x1, starting transfers between devices, body(): far = lax.ppermute(near, 'rollout', SIBLING)  8.8 us
    ppermute x2, starting transfers between devices, across_y(): return lax.ppermute(block, 'tensor', Y_PARTNER)  7.01 us
    pallas_call x1, Pallas kernels, low_begin(): pl.pallas_call(functools.partial(low_begin_kernel, places), out_shape=(ja...  5.77 us
    pallas_call x1, Pallas kernels, project(): pl.pallas_call(functools.partial(project_kernel, places), out_shape=jax.S...  4.28 us
    all_to_all x1, starting transfers between devices, body(): lax.all_to_all(low, 'tensor', 0, 0, tiled=True).reshape(2 * RANK, ROWS)  3.37 us
  transfers between devices with their start and end apart: 10, of which 2 were waited for; matrix products, arithmetic and copies ran while one was open for 0% of the time, Pallas kernels for 15%

profile of v9, /device:TPU:1, one launch (start us, length us, event | category | flops | bytes accessed | tf_op | source)
XLA Modules:
  0.0 93.5 jit_solution(129895520732357155)
XLA Ops:
  0.0 4.0 %collective-permute-start.2 = (bf16[256,1024]{1,0:T(8,128)(2,1)}, bf16[256,1024]{1,0:T(8,128)(2,1)S(1)}, u32[]{:S(2)}, u32[]{:S(2)}) collective-permute-start(bf16[256,1024]{1,0:T(8,128)(2,1)} %tokens_ref.1), channel_id=1, source_target_pairs={{0,4},{1,5},{2,6},{3,7},{4,0},{5,1},{6,2},{7,3},{8,12},{9,13},{10,... | collective-permute-start | bytes 1572872 | tf_op jit(solution)/shard_map/ppermute | solution.py:380
  4.0 4.7 %collective-permute-start = (bf16[256,1024]{1,0:T(8,128)(2,1)}, bf16[256,1024]{1,0:T(8,128)(2,1)}, u32[]{:S(2)}, u32[]{:S(2)}) collective-permute-start(bf16[256,1024]{1,0:T(8,128)(2,1)} %tokens_ref.1), channel_id=1, source_target_pairs={{2,0},{3,1},{0,2},{1,3},{6,4},{7,5},{4,6},{5,7},{10,8},{11,9},{8,1... | collective-permute-start | bytes 1572872 | tf_op jit(solution)/shard_map/ppermute | solution.py:377
  8.7 2.8 %collective-permute-start.7 = (bf16[256,1024]{1,0:T(8,128)(2,1)}, bf16[256,1024]{1,0:T(8,128)(2,1)S(1)}, u32[]{:S(2)}, u32[]{:S(2)}) collective-permute-start(bf16[256,1024]{1,0:T(8,128)(2,1)} %tokens_ref.1), channel_id=1, source_target_pairs={{3,0},{0,1},{1,2},{2,3},{7,4},{4,5},{5,6},{6,7},{9,8},{10,9},{11,1... | collective-permute-start | bytes 1572872 | tf_op jit(solution)/shard_map/ppermute | solution.py:377
  11.5 2.5 %collective-permute-start.6 = (bf16[256,1024]{1,0:T(8,128)(2,1)}, bf16[256,1024]{1,0:T(8,128)(2,1)}, u32[]{:S(2)}, u32[]{:S(2)}) collective-permute-start(bf16[256,1024]{1,0:T(8,128)(2,1)} %tokens_ref.1), channel_id=1, source_target_pairs={{1,0},{2,1},{3,2},{0,3},{5,4},{6,5},{7,6},{4,7},{11,8},{8,9},{9,10... | collective-permute-start | bytes 1572872 | tf_op jit(solution)/shard_map/ppermute | solution.py:377
  14.0 0.1 pad_add_fusion.own_ref
  14.1 1.7 %share.1 = bf16[32,40,128]{2,1,0:T(8,128)(2,1)} custom-call(s32[3]{0:T(128)S(1)} %pad_add_fusion.own_ref, bf16[256,128]{1,0:T(8,128)(2,1)} %bitcast.15, bf16[4,128]{1,0:T(4,128)(2,1)} %bitcast.16), custom_call_target="tpu_custom_call" | custom-call | tf_op jit(solution)/shard_map/share/pallas_call | solution.py:81
  15.8 14.8 %all-to-all-start = ((bf16[32,40,128]{2,1,0:T(8,128)(2,1)}), bf16[32,40,128]{2,1,0:T(8,128)(2,1)S(1)}, u32[]{:S(2)}, u32[]{:S(2)}) async-start(bf16[32,40,128]{2,1,0:T(8,128)(2,1)} %share.1), calls=%async_computation | async-start | bytes 655360 | tf_op jit(solution)/shard_map/all_to_all | solution.py:386
  30.6 0.5 rate.1.rate_ref
  31.2 0.0 collective-permute-done.refs_1_
  31.2 3.0 %collective-permute-start.1 = (bf16[256,1024]{1,0:T(8,128)(2,1)}, bf16[256,1024]{1,0:T(8,128)(2,1)S(1)}, u32[]{:S(2)}, u32[]{:S(2)}) collective-permute-start(bf16[256,1024]{1,0:T(8,128)(2,1)} %collective-permute-done.refs_1_), channel_id=1, source_target_pairs={{0,4},{1,5},{2,6},{3,7},{4,0},{5,1},{6,2},{7,3},{8,12},{9,13},{10,... | collective-permute-start | bytes 1572872 | tf_op jit(solution)/shard_map/ppermute | solution.py:380
  34.2 0.0 collective-permute-done.2.refs_3_.refs_1_
  34.2 2.2 %collective-permute-start.3 = (bf16[256,1024]{1,0:T(8,128)(2,1)S(1)}, bf16[256,1024]{1,0:T(8,128)(2,1)S(1)}, u32[]{:S(2)}, u32[]{:S(2)}) collective-permute-start(bf16[256,1024]{1,0:T(8,128)(2,1)S(1)} %collective-permute-done.2.refs_3_.refs_1_), channel_id=1, source_target_pairs={{1,0},{2,1},{3,2},{0,3},{5,4},{6,5},{7,6},{4,7},{11,8},{8,9},{9,10... | collective-permute-start | bytes 1572872 | tf_op jit(solution)/shard_map/ppermute | solution.py:377
  36.4 4.3 %collective-permute-start.4 = (bf16[256,1024]{1,0:T(8,128)(2,1)S(1)}, bf16[256,1024]{1,0:T(8,128)(2,1)S(1)}, u32[]{:S(2)}, u32[]{:S(2)}) collective-permute-start(bf16[256,1024]{1,0:T(8,128)(2,1)S(1)} %collective-permute-done.2.refs_3_.refs_1_), channel_id=1, source_target_pairs={{3,0},{0,1},{1,2},{2,3},{7,4},{4,5},{5,6},{6,7},{9,8},{10,9},{11,1... | collective-permute-start | bytes 1572872 | tf_op jit(solution)/shard_map/ppermute | solution.py:377
  40.7 0.0 collective-permute-done.7.refs_2_.refs_0_
  40.7 1.9 %all-to-all-done.near_ref = bf16[32,40,128]{2,1,0:T(8,128)(2,1)S(1)} async-done(((bf16[32,40,128]{2,1,0:T(8,128)(2,1)}), bf16[32,40,128]{2,1,0:T(8,128)(2,1)S(1)}, u32[]{:S(2)}, u32[]{:S(2)}) %all-to-all-start) | async-done | bytes 327712 | tf_op jit(solution)/shard_map/all_to_all | solution.py:386
  42.6 8.8 %collective-permute-start.5 = (bf16[32,40,128]{2,1,0:T(8,128)(2,1)S(1)}, bf16[32,40,128]{2,1,0:T(8,128)(2,1)S(1)}, u32[]{:S(2)}, u32[]{:S(2)}) collective-permute-start(bf16[32,40,128]{2,1,0:T(8,128)(2,1)S(1)} %all-to-all-done.near_ref), channel_id=1, source_target_pairs={{0,8},{8,0},{16,24},{24,16},{32,40},{40,32},{48,56},{56,48},{64,72... | collective-permute-start | bytes 983048 | tf_op jit(solution)/shard_map/ppermute | solution.py:387
  51.5 1.2 %places.1 = (s32[64]{0:T(128)}, s32[1,256]{1,0:T(1,128)S(1)}) custom-call(s32[64]{0:T(128)} %lookup_ref.1, s32[1,256]{1,0:T(1,128)} %bitcast.17), custom_call_target="tpu_custom_call" | custom-call | flops 8000000000 | tf_op jit(solution)/shard_map/places/pallas_call | solution.py:112
  52.7 0.0 collective-permute-done.6.refs_0_
  52.7 0.0 collective-permute-done.5.far_ref
  52.7 5.8 %low_begin.1 = (bf16[32,8192]{1,0:T(8,128)(2,1)S(1)}, f32[256,32]{1,0:T(8,128)S(1)}, bf16[256,128]{1,0:T(8,128)(2,1)}, f32[256,256]{1,0:T(8,128)}) custom-call(s32[64]{0:T(128)} %get-tuple-element.22.shard_ref, s32[3]{0:T(128)S(1)} %pad_add_fusion.own_ref, bf16[32,40,128]{2,1,0:T(8,128)(2,1)S(1)} %all-to-all-done.near_ref, ...), custom_call_target="tpu_custom_call" | custom-call | tf_op jit(solution)/shard_map/low_begin/pallas_call | solution.py:198
  58.5 0.0 collective-permute-done.3.refs_3_.refs_1_
  58.5 0.0 collective-permute-done.4.refs_4_.refs_2_
  58.5 0.0 collective-permute-done.1.refs_2_.refs_0_
  58.5 1.8 %low_end.1 = bf16[8,32,256]{2,1,0:T(8,128)(2,1)} custom-call(s32[3]{0:T(128)S(1)} %pad_add_fusion.own_ref, bf16[32,8192]{1,0:T(8,128)(2,1)S(1)} %get-tuple-element.34.down_ref, f32[256,32]{1,0:T(8,128)S(1)} %get-tuple-element.35.begun_ref, bf16[256,1024]{1,0:T(8,128)(2,1)S(1)} %collective-permute-done.1.refs_2_.refs_0_, ...), custom_call_target="tpu_custom_call" | custom-call | tf_op jit(solution)/shard_map/low_end/pallas_call | solution.py:236
  60.3 3.4 %all-to-all-start.1 = ((bf16[8,32,256]{2,1,0:T(8,128)(2,1)}), bf16[8,32,256]{2,1,0:T(8,128)(2,1)S(1)}, u32[]{:S(2)}, u32[]{:S(2)}) async-start(bf16[8,32,256]{2,1,0:T(8,128)(2,1)} %low_end.1), calls=%async_computation.1 | async-start | bytes 262144 | tf_op jit(solution)/shard_map/all_to_all | solution.py:404
  63.7 4.3 %project.1.made_ref = f32[256,640]{1,0:T(8,128)S(1)} custom-call(s32[3]{0:T(128)S(1)} %pad_add_fusion.own_ref, s32[1,8]{1,0:T(1,128)} %lengths_ref.1, bf16[16384,128]{1,0:T(8,128)(2,1)} %bitcast.13, bf16[256,128]{1,0:T(8,128)(2,1)} %get-tuple-element.28.up_ref, f32[256,256]{1,0:T(8,128)} %get-tuple-element.29.begun_ref, f32[1,128]{1,0:T(1,128)} %rate.1.rate_ref, ...), custom_call_target="tpu_custom_call" | custom-call | tf_op jit(solution)/shard_map/project/pallas_call | solution.py:285
  68.0 1.1 %all-to-all-done.1 = bf16[8,32,256]{2,1,0:T(8,128)(2,1)S(1)} async-done(((bf16[8,32,256]{2,1,0:T(8,128)(2,1)}), bf16[8,32,256]{2,1,0:T(8,128)(2,1)S(1)}, u32[]{:S(2)}, u32[]{:S(2)}) %all-to-all-start.1) | async-done | bytes 131104 | tf_op jit(solution)/shard_map/all_to_all | solution.py:404
  69.1 0.5 finish.1
  69.6 23.3 %all_to_all.19 = bf16[64,16,128]{2,1,0:T(8,128)(2,1)S(1)} all-to-all(bf16[64,16,128]{2,1,0:T(8,128)(2,1)S(1)} %bitcast.10), channel_id=1, replica_groups=mesh['rollout'=64,'tensor'=8] {'rollout'}, dimensions={0} | all-to-all | bytes 524288 | tf_op jit(solution)/shard_map/all_to_all | solution.py:407
  92.8 0.7 copy.10
Async XLA Ops:
  0.0 34.2 %collective-permute-start.2 = (bf16[256,1024]{1,0:T(8,128)(2,1)}, bf16[256,1024]{1,0:T(8,128)(2,1)S(1)}, u32[]{:S(2)}, u32[]{:S(2)}) collective-permute-start(bf16[256,1024]{1,0:T(8,128)(2,1)} %tokens_ref.1), channel_id=1, source_target_pairs={{0,4},{1,5},{2,6},{3,7},{4,0},{5,1},{6,2},{7,3},{8,12},{9,13},{10,... | collective-permute-start | bytes 1572872 | tf_op jit(solution)/shard_map/ppermute | solution.py:380
  4.0 27.1 %collective-permute-start = (bf16[256,1024]{1,0:T(8,128)(2,1)}, bf16[256,1024]{1,0:T(8,128)(2,1)}, u32[]{:S(2)}, u32[]{:S(2)}) collective-permute-start(bf16[256,1024]{1,0:T(8,128)(2,1)} %tokens_ref.1), channel_id=1, source_target_pairs={{2,0},{3,1},{0,2},{1,3},{6,4},{7,5},{4,6},{5,7},{10,8},{11,9},{8,1... | collective-permute-start | bytes 1572872 | tf_op jit(solution)/shard_map/ppermute | solution.py:377
  8.7 32.0 %collective-permute-start.7 = (bf16[256,1024]{1,0:T(8,128)(2,1)}, bf16[256,1024]{1,0:T(8,128)(2,1)S(1)}, u32[]{:S(2)}, u32[]{:S(2)}) collective-permute-start(bf16[256,1024]{1,0:T(8,128)(2,1)} %tokens_ref.1), channel_id=1, source_target_pairs={{3,0},{0,1},{1,2},{2,3},{7,4},{4,5},{5,6},{6,7},{9,8},{10,9},{11,1... | collective-permute-start | bytes 1572872 | tf_op jit(solution)/shard_map/ppermute | solution.py:377
  11.5 41.2 %collective-permute-start.6 = (bf16[256,1024]{1,0:T(8,128)(2,1)}, bf16[256,1024]{1,0:T(8,128)(2,1)}, u32[]{:S(2)}, u32[]{:S(2)}) collective-permute-start(bf16[256,1024]{1,0:T(8,128)(2,1)} %tokens_ref.1), channel_id=1, source_target_pairs={{1,0},{2,1},{3,2},{0,3},{5,4},{6,5},{7,6},{4,7},{11,8},{8,9},{9,10... | collective-permute-start | bytes 1572872 | tf_op jit(solution)/shard_map/ppermute | solution.py:377
  15.8 26.8 %all-to-all-start = ((bf16[32,40,128]{2,1,0:T(8,128)(2,1)}), bf16[32,40,128]{2,1,0:T(8,128)(2,1)S(1)}, u32[]{:S(2)}, u32[]{:S(2)}) async-start(bf16[32,40,128]{2,1,0:T(8,128)(2,1)} %share.1), calls=%async_computation | async-start | bytes 655360 | tf_op jit(solution)/shard_map/all_to_all | solution.py:386
  31.2 27.3 %collective-permute-start.1 = (bf16[256,1024]{1,0:T(8,128)(2,1)}, bf16[256,1024]{1,0:T(8,128)(2,1)S(1)}, u32[]{:S(2)}, u32[]{:S(2)}) collective-permute-start(bf16[256,1024]{1,0:T(8,128)(2,1)} %collective-permute-done.refs_1_), channel_id=1, source_target_pairs={{0,4},{1,5},{2,6},{3,7},{4,0},{5,1},{6,2},{7,3},{8,12},{9,13},{10,... | collective-permute-start | bytes 1572872 | tf_op jit(solution)/shard_map/ppermute | solution.py:380
  34.2 24.3 %collective-permute-start.3 = (bf16[256,1024]{1,0:T(8,128)(2,1)S(1)}, bf16[256,1024]{1,0:T(8,128)(2,1)S(1)}, u32[]{:S(2)}, u32[]{:S(2)}) collective-permute-start(bf16[256,1024]{1,0:T(8,128)(2,1)S(1)} %collective-permute-done.2.refs_3_.refs_1_), channel_id=1, source_target_pairs={{1,0},{2,1},{3,2},{0,3},{5,4},{6,5},{7,6},{4,7},{11,8},{8,9},{9,10... | collective-permute-start | bytes 1572872 | tf_op jit(solution)/shard_map/ppermute | solution.py:377
  36.4 22.1 %collective-permute-start.4 = (bf16[256,1024]{1,0:T(8,128)(2,1)S(1)}, bf16[256,1024]{1,0:T(8,128)(2,1)S(1)}, u32[]{:S(2)}, u32[]{:S(2)}) collective-permute-start(bf16[256,1024]{1,0:T(8,128)(2,1)S(1)} %collective-permute-done.2.refs_3_.refs_1_), channel_id=1, source_target_pairs={{3,0},{0,1},{1,2},{2,3},{7,4},{4,5},{5,6},{6,7},{9,8},{10,9},{11,1... | collective-permute-start | bytes 1572872 | tf_op jit(solution)/shard_map/ppermute | solution.py:377
  42.6 10.1 %collective-permute-start.5 = (bf16[32,40,128]{2,1,0:T(8,128)(2,1)S(1)}, bf16[32,40,128]{2,1,0:T(8,128)(2,1)S(1)}, u32[]{:S(2)}, u32[]{:S(2)}) collective-permute-start(bf16[32,40,128]{2,1,0:T(8,128)(2,1)S(1)} %all-to-all-done.near_ref), channel_id=1, source_target_pairs={{0,8},{8,0},{16,24},{24,16},{32,40},{40,32},{48,56},{56,48},{64,72... | collective-permute-start | bytes 983048 | tf_op jit(solution)/shard_map/ppermute | solution.py:387
  60.3 8.7 %all-to-all-start.1 = ((bf16[8,32,256]{2,1,0:T(8,128)(2,1)}), bf16[8,32,256]{2,1,0:T(8,128)(2,1)S(1)}, u32[]{:S(2)}, u32[]{:S(2)}) async-start(bf16[8,32,256]{2,1,0:T(8,128)(2,1)} %low_end.1), calls=%async_computation.1 | async-start | bytes 262144 | tf_op jit(solution)/shard_map/all_to_all | solution.py:404
